TPU v7x, 32 devices: a whole 2x2x4 slice. The times are simulated.
32 devices in a mesh: group: 2 (over x), blk: 8 (over z, y), ulysses: 2 (over core).
Axes of the slice: x: 2, y: 2, z: 4, core: 2. Of those that a mesh axis runs over, the one named last changes fastest.
Arguments:
- query_int: bfloat16 [4096, 8192], P(('group', 'blk', 'ulysses')), parts along dimension 0, may hold values from -127 to 127, as said below
- key_int: bfloat16 [4096, 1024], P(('group', 'blk', 'ulysses')), parts along dimension 0, may hold values from -127 to 127, as said below
- values: bfloat16 [4096, 1024], P(('group', 'blk', 'ulysses')), parts along dimension 0, may hold values from -6 to 6
- query_scale: bfloat16 [32, 64], P(('group', 'blk')), parts along dimension 0, may hold values from 0.001 to 0.02
- key_scale: bfloat16 [32, 8], P('group'), parts along dimension 0, may hold values from 0.002 to 0.04
- verticals: int32 [16, 8], P('group'), parts along dimension 0, may hold values from 0 to 15, as said below
- slashes: int32 [16, 8], P('group'), parts along dimension 0, may hold values from 0 to 8, as said below
Outputs:
- attention: bfloat16 [4096, 8192], P(('group', 'blk', 'ulysses')), parts along dimension 0
There are 2 independent parts, one for each index of `group`. A program takes and returns all parts, laid end to end along the dimension named above; each array names one. Nothing has to cross between parts.
Inputs may be any that keep to these rules, and one draw needn't show every extreme that they name: `query_int`: integer values. `key_int`: integer values. `verticals`: each row holds 8 distinct key blocks, block 0 among them. `slashes`: each row holds 8 distinct offsets, 0 among them.
All inputs are finite; a program needn't handle non-finite values.
Results may differ from a plain program's by a relative error of at most 0.0019.
Values may be sent and summed in bfloat16 or wider, within the bound.
No kernel may reach another device: no remote copies, remote signals or barrier semaphores. Data moves between devices by JAX's collectives and lax.ppermute only.
A program may use at most 128 MiB of HBM per device.

v0:
```python
import jax
import jax.numpy as jnp
from jax import lax
from jax.sharding import PartitionSpec as P

DH = 128
BLOCK = 128


FLOOR_SCORE = -1e30


def block_table(verticals, slashes, first_block, block_count):
    blocks = first_block + jnp.arange(block_count, dtype=jnp.int32)
    slash_keys = blocks[:, None, None] - slashes[None, :, :]
    slash_live = slash_keys >= 0
    vert_keys = jnp.broadcast_to(verticals[None, :, :], (block_count,) + verticals.shape)
    clashes = jnp.any(
        (vert_keys[:, :, :, None] == slash_keys[:, :, None, :]) & slash_live[:, :, None, :], axis=3
    )
    vert_live = (vert_keys <= blocks[:, None, None]) & jnp.logical_not(clashes)
    return (
        jnp.concatenate([vert_keys, slash_keys], axis=2),
        jnp.concatenate([vert_live, slash_live], axis=2),
        blocks,
    )


def gather_blocks(buffer, positions, groups):
    shaped = buffer.reshape(buffer.shape[0] // BLOCK, BLOCK, groups, DH)
    heads_at = jnp.arange(groups, dtype=jnp.int32)[None, :, None]
    return shaped[positions, :, heads_at, :]


def attend_group(pieces):
    query_block, query_scales, key_blocks, value_blocks, key_scales, live_slots, diagonal = pieces
    dots = jnp.einsum("tpd,nsd->ptns", query_block, key_blocks, preferred_element_type=jnp.float32)
    scores = dots * query_scales[:, None, None, None] * key_scales[None, None, :, None]
    width = query_block.shape[0]
    causal = jnp.arange(width)[None, :] <= jnp.arange(width)[:, None]
    allowed = live_slots[None, None, :, None] & (
        jnp.logical_not(diagonal)[None, None, :, None] | causal[None, :, None, :]
    )
    masked = jnp.where(allowed, scores, FLOOR_SCORE)
    largest = jnp.max(masked, axis=(2, 3), keepdims=True)
    weights = jnp.where(allowed, jnp.exp(masked - largest), 0.0)
    totals = jnp.sum(weights, axis=(2, 3))
    numer = jnp.einsum(
        "ptns,nsd->tpd",
        weights.astype(jnp.bfloat16),
        value_blocks,
        preferred_element_type=jnp.float32,
    )
    return (numer / jnp.transpose(totals, (1, 0))[:, :, None]).astype(jnp.bfloat16)


def attend_block(pieces):
    query_block, query_scales, key_blocks, value_blocks, key_scales, live_slots, diagonal = pieces
    by_group = lax.map(
        attend_group,
        (
            jnp.transpose(query_block, (1, 0, 2, 3)),
            query_scales,
            key_blocks,
            value_blocks,
            key_scales,
            live_slots,
            diagonal,
        ),
    )
    return jnp.transpose(by_group, (1, 0, 2, 3))


def local(query_int, key_int, values, query_scale, key_scale, verticals, slashes):
    query_here, key_here, value_here = (
        lax.all_to_all(query_int, "ulysses", split_axis=1, concat_axis=0, tiled=True),
        lax.all_to_all(key_int, "ulysses", split_axis=1, concat_axis=0, tiled=True),
        lax.all_to_all(values, "ulysses", split_axis=1, concat_axis=0, tiled=True),
    )
    half_index = lax.axis_index("ulysses")
    span_index = lax.axis_index("blk")
    span_rows = query_here.shape[0]
    block_count = span_rows // BLOCK
    heads_here = query_here.shape[1] // DH
    groups_here = key_here.shape[1] // DH
    per_group = heads_here // groups_here
    first_block = span_index * block_count
    group_ids = half_index * groups_here + jnp.arange(groups_here, dtype=jnp.int32)
    query_scales = lax.dynamic_slice_in_dim(query_scale, half_index * heads_here, heads_here, 1)
    query_scales = query_scales.astype(jnp.float32).reshape(block_count, groups_here, per_group)
    vert_here = lax.dynamic_slice_in_dim(verticals, half_index * groups_here, groups_here, 0)
    slash_here = lax.dynamic_slice_in_dim(slashes, half_index * groups_here, groups_here, 0)
    block_keys, live_slots, blocks = block_table(vert_here, slash_here, first_block, block_count)
    total_blocks = key_scale.shape[0]
    clipped = jnp.clip(block_keys, 0, total_blocks - 1)
    key_scales = key_scale[clipped, group_ids[None, :, None]].astype(jnp.float32)
    key_all, value_all = (
        lax.all_gather(key_here, "blk", axis=0, tiled=True),
        lax.all_gather(value_here, "blk", axis=0, tiled=True),
    )
    key_blocks = gather_blocks(key_all, clipped, groups_here)
    value_blocks = gather_blocks(value_all, clipped, groups_here)
    diagonal = block_keys == blocks[:, None, None]
    query_blocks = query_here.reshape(block_count, BLOCK, groups_here, per_group, DH)
    outputs = lax.map(
        attend_block,
        (query_blocks, query_scales, key_blocks, value_blocks, key_scales, live_slots, diagonal),
    )
    merged = outputs.reshape(span_rows, heads_here * DH)
    return lax.all_to_all(merged, "ulysses", split_axis=0, concat_axis=1, tiled=True)


def solution(mesh):
    in_specs = (
        P(("group", "blk", "ulysses"), None),
        P(("group", "blk", "ulysses"), None),
        P(("group", "blk", "ulysses"), None),
        P(("group", "blk"), None),
        P("group", None),
        P("group", None),
        P("group", None),
    )
    out_specs = P(("group", "blk", "ulysses"), None)
    return jax.shard_map(local, mesh=mesh, in_specs=in_specs, out_specs=out_specs, check_vma=False)
```

profile of v0, /device:TPU:0, one launch (start us, length us, event | category | flops | bytes accessed | tf_op | source)
XLA Modules:
  0.0 241.9 jit_solution(8448017913891180040)
XLA Ops:
  7.8 3.9 %all_to_all.73 = bf16[128,2,512]{0,2,1:T(8,128)(2,1)S(1)} all-to-all(bf16[128,2,512]{0,2,1:T(8,128)(2,1)S(1)} %bitcast.156), channel_id=1, replica_groups=mesh['group'=2,'blk'=8,'ulysses'=2] {'ulysses'}, dimensions={1} | all-to-all | bytes 524288 | tf_op jit(solution)/shard_map/all_to_all | solution.py:77
  13.8 3.9 %all_to_all.74 = bf16[128,2,512]{0,2,1:T(8,128)(2,1)S(1)} all-to-all(bf16[128,2,512]{0,2,1:T(8,128)(2,1)S(1)} %bitcast.157), channel_id=1, replica_groups=mesh['group'=2,'blk'=8,'ulysses'=2] {'ulysses'}, dimensions={1} | all-to-all | bytes 524288 | tf_op jit(solution)/shard_map/all_to_all | solution.py:78
  21.1 5.0 %all-to-all-start = ((bf16[128,2,4096]{0,2,1:T(8,128)(2,1)}), bf16[128,2,4096]{0,2,1:T(8,128)(2,1)}, u32[]{:S(2)}, u32[]{:S(2)}) async-start(bf16[128,2,4096]{0,2,1:T(8,128)(2,1)} %bitcast.27), calls=%async_computation | async-start | bytes 4194304 | tf_op jit(solution)/shard_map/all_to_all | solution.py:76
  28.9 35.8 %all-gather.3.cloned.1.call-done = bf16[2048,512]{1,0:T(8,128)(2,1)} async-done(((bf16[256,512]{1,0:T(8,128)(2,1)}), bf16[2048,512]{1,0:T(8,128)(2,1)}) %all-gather.3.cloned.1.call-update) | async-done | bytes 2097168 | tf_op jit(solution)/shard_map/all_gather | solution.py:98
  64.8 4.0 %reshape.141 = bf16[16,128,4,128]{3,2,1,0:T(4,128)(2,1)} reshape(bf16[2048,512]{1,0:T(8,128)(2,1)} %all-gather.3.cloned.1.call-done) | data formatting | bytes 4194304 | tf_op jit(solution)/shard_map/reshape | solution.py:30
  70.9 43.8 %all-gather.5.cloned.1.call-done = bf16[2048,512]{1,0:T(8,128)(2,1)} async-done(((bf16[256,512]{1,0:T(8,128)(2,1)}), bf16[2048,512]{1,0:T(8,128)(2,1)}) %all-gather.5.cloned.1.call-update) | async-done | bytes 2097168 | tf_op jit(solution)/shard_map/all_gather | solution.py:99
  114.7 4.0 %reshape.142 = bf16[16,128,4,128]{3,2,1,0:T(4,128)(2,1)} reshape(bf16[2048,512]{1,0:T(8,128)(2,1)} %all-gather.5.cloned.1.call-done) | data formatting | bytes 4194304 | tf_op jit(solution)/shard_map/reshape | solution.py:30
  118.7 3.5 %copy.65 = bf16[16,128,4,128]{3,1,2,0:T(8,128)(2,1)} copy(bf16[16,128,4,128]{3,2,1,0:T(4,128)(2,1)} %reshape.142) | data formatting | bytes 4194304 | tf_op jit(solution)/shard_map/reshape | solution.py:30
  122.1 3.1 %gather_fusion = bf16[128,128,128]{2,1,0:T(8,128)(2,1)} fusion(bf16[16,128,4,128]{3,1,2,0:T(8,128)(2,1)S(1)} %copy.61, s32[128]{0:T(128)S(1)} %reshape.118), kind=kCustom, calls=%fused_computation | custom fusion | bytes 8389632 | tf_op jit(solution)/shard_map/gather | solution.py:32
  125.2 4.7 %gather_fusion.1 = bf16[128,128,128]{2,1,0:T(8,128)(2,1)} fusion(bf16[16,128,4,128]{3,1,2,0:T(8,128)(2,1)} %copy.65, s32[128]{0:T(128)S(1)} %reshape.118), kind=kCustom, calls=%fused_computation.1 | custom fusion | bytes 8389632 | tf_op jit(solution)/shard_map/gather | solution.py:32
  129.9 89.9 %while.21 = (s32[]{:T(128)}, bf16[2,128,4,8,128]{1,4,3,2,0:T(8,128)(2,1)}, bf16[2,128,4,8,128]{1,4,3,2,0:T(8,128)(2,1)}, f32[2,4,8]{2,1,0:T(4,128)S(1)}, bf16[2,...) while((s32[]{:T(128)}, ...), condition=%wide.region_6.7_spmd, body=%wide.region_1.6_spmd.sunk | while | flops 1108097024 | bytes 46721236 | solution.py:105
  138.7 35.1 %while.22 = (s32[]{:T(128)}, bf16[4,128,8,128]{1,3,2,0:T(8,128)(2,1)S(1)}, bf16[4,16,128,128]{2,3,1,0:T(8,128)(2,1)}, pred[4,16]{1,0:T(4,128)(4,1)S(1)}, pred[4,...) while((s32[]{:T(128)}, ...), condition=%wide.region_5.5_spmd, body=%wide.region_2.4_spmd.sunk | while | flops 1108097024 | bytes 27845104 | solution.py:59
  143.8 3.6 %fusion.60 = bf16[4,128,8,128]{1,3,2,0:T(8,128)(2,1)S(1)} fusion(bf16[4,128,8,128]{1,3,2,0:T(8,128)(2,1)S(1)} %get-tuple-element.347, s32[]{:T(128)} %get-tuple-element.346, f32[16,128,128,8]{2,1,3,0:T(8,128)S(1)} %get-tuple-element.334, f32[8,128]{1,0:T(8,128)S(1)} %get-tuple-element.335, f32[16]{0:T(128)S(1)} %fusion.55, f32[8]{0:T(128)S(1)} %fusion.56, ...), kind=kOutput, calls=%fused_computation.14.clone.1 | convolution fusion | flops 549715968 | bytes 9447424 | tf_op jit(solution)/shard_map/while/body/eval_jaxpr/while/body/eval_jaxpr/ptns,nsd->tpd/dot_general | solution.py:48
  152.6 3.6 %fusion.60 = bf16[4,128,8,128]{1,3,2,0:T(8,128)(2,1)S(1)} fusion(bf16[4,128,8,128]{1,3,2,0:T(8,128)(2,1)S(1)} %get-tuple-element.347, s32[]{:T(128)} %get-tuple-element.346, f32[16,128,128,8]{2,1,3,0:T(8,128)S(1)} %get-tuple-element.334, f32[8,128]{1,0:T(8,128)S(1)} %get-tuple-element.335, f32[16]{0:T(128)S(1)} %fusion.55, f32[8]{0:T(128)S(1)} %fusion.56, ...), kind=kOutput, calls=%fused_computation.14.clone.1 | convolution fusion | flops 549715968 | bytes 9447424 | tf_op jit(solution)/shard_map/while/body/eval_jaxpr/while/body/eval_jaxpr/ptns,nsd->tpd/dot_general | solution.py:48
  161.4 3.6 %fusion.60 = bf16[4,128,8,128]{1,3,2,0:T(8,128)(2,1)S(1)} fusion(bf16[4,128,8,128]{1,3,2,0:T(8,128)(2,1)S(1)} %get-tuple-element.347, s32[]{:T(128)} %get-tuple-element.346, f32[16,128,128,8]{2,1,3,0:T(8,128)S(1)} %get-tuple-element.334, f32[8,128]{1,0:T(8,128)S(1)} %get-tuple-element.335, f32[16]{0:T(128)S(1)} %fusion.55, f32[8]{0:T(128)S(1)} %fusion.56, ...), kind=kOutput, calls=%fused_computation.14.clone.1 | convolution fusion | flops 549715968 | bytes 9447424 | tf_op jit(solution)/shard_map/while/body/eval_jaxpr/while/body/eval_jaxpr/ptns,nsd->tpd/dot_general | solution.py:48
  170.2 3.6 %fusion.60 = bf16[4,128,8,128]{1,3,2,0:T(8,128)(2,1)S(1)} fusion(bf16[4,128,8,128]{1,3,2,0:T(8,128)(2,1)S(1)} %get-tuple-element.347, s32[]{:T(128)} %get-tuple-element.346, f32[16,128,128,8]{2,1,3,0:T(8,128)S(1)} %get-tuple-element.334, f32[8,128]{1,0:T(8,128)S(1)} %get-tuple-element.335, f32[16]{0:T(128)S(1)} %fusion.55, f32[8]{0:T(128)S(1)} %fusion.56, ...), kind=kOutput, calls=%fused_computation.14.clone.1 | convolution fusion | flops 549715968 | bytes 9447424 | tf_op jit(solution)/shard_map/while/body/eval_jaxpr/while/body/eval_jaxpr/ptns,nsd->tpd/dot_general | solution.py:48
  183.6 35.1 %while.22 = (s32[]{:T(128)}, bf16[4,128,8,128]{1,3,2,0:T(8,128)(2,1)S(1)}, bf16[4,16,128,128]{2,3,1,0:T(8,128)(2,1)}, pred[4,16]{1,0:T(4,128)(4,1)S(1)}, pred[4,...) while((s32[]{:T(128)}, ...), condition=%wide.region_5.5_spmd, body=%wide.region_2.4_spmd.sunk | while | flops 1108097024 | bytes 27845104 | solution.py:59
  188.8 3.6 %fusion.60 = bf16[4,128,8,128]{1,3,2,0:T(8,128)(2,1)S(1)} fusion(bf16[4,128,8,128]{1,3,2,0:T(8,128)(2,1)S(1)} %get-tuple-element.347, s32[]{:T(128)} %get-tuple-element.346, f32[16,128,128,8]{2,1,3,0:T(8,128)S(1)} %get-tuple-element.334, f32[8,128]{1,0:T(8,128)S(1)} %get-tuple-element.335, f32[16]{0:T(128)S(1)} %fusion.55, f32[8]{0:T(128)S(1)} %fusion.56, ...), kind=kOutput, calls=%fused_computation.14.clone.1 | convolution fusion | flops 549715968 | bytes 9447424 | tf_op jit(solution)/shard_map/while/body/eval_jaxpr/while/body/eval_jaxpr/ptns,nsd->tpd/dot_general | solution.py:48
  197.5 3.6 %fusion.60 = bf16[4,128,8,128]{1,3,2,0:T(8,128)(2,1)S(1)} fusion(bf16[4,128,8,128]{1,3,2,0:T(8,128)(2,1)S(1)} %get-tuple-element.347, s32[]{:T(128)} %get-tuple-element.346, f32[16,128,128,8]{2,1,3,0:T(8,128)S(1)} %get-tuple-element.334, f32[8,128]{1,0:T(8,128)S(1)} %get-tuple-element.335, f32[16]{0:T(128)S(1)} %fusion.55, f32[8]{0:T(128)S(1)} %fusion.56, ...), kind=kOutput, calls=%fused_computation.14.clone.1 | convolution fusion | flops 549715968 | bytes 9447424 | tf_op jit(solution)/shard_map/while/body/eval_jaxpr/while/body/eval_jaxpr/ptns,nsd->tpd/dot_general | solution.py:48
  206.3 3.6 %fusion.60 = bf16[4,128,8,128]{1,3,2,0:T(8,128)(2,1)S(1)} fusion(bf16[4,128,8,128]{1,3,2,0:T(8,128)(2,1)S(1)} %get-tuple-element.347, s32[]{:T(128)} %get-tuple-element.346, f32[16,128,128,8]{2,1,3,0:T(8,128)S(1)} %get-tuple-element.334, f32[8,128]{1,0:T(8,128)S(1)} %get-tuple-element.335, f32[16]{0:T(128)S(1)} %fusion.55, f32[8]{0:T(128)S(1)} %fusion.56, ...), kind=kOutput, calls=%fused_computation.14.clone.1 | convolution fusion | flops 549715968 | bytes 9447424 | tf_op jit(solution)/shard_map/while/body/eval_jaxpr/while/body/eval_jaxpr/ptns,nsd->tpd/dot_general | solution.py:48
  215.1 3.6 %fusion.60 = bf16[4,128,8,128]{1,3,2,0:T(8,128)(2,1)S(1)} fusion(bf16[4,128,8,128]{1,3,2,0:T(8,128)(2,1)S(1)} %get-tuple-element.347, s32[]{:T(128)} %get-tuple-element.346, f32[16,128,128,8]{2,1,3,0:T(8,128)S(1)} %get-tuple-element.334, f32[8,128]{1,0:T(8,128)S(1)} %get-tuple-element.335, f32[16]{0:T(128)S(1)} %fusion.55, f32[8]{0:T(128)S(1)} %fusion.56, ...), kind=kOutput, calls=%fused_computation.14.clone.1 | convolution fusion | flops 549715968 | bytes 9447424 | tf_op jit(solution)/shard_map/while/body/eval_jaxpr/while/body/eval_jaxpr/ptns,nsd->tpd/dot_general | solution.py:48
  219.8 2.9 %copy.79 = bf16[2,128,4096]{2,1,0:T(8,128)(2,1)S(1)} copy(bf16[2,128,4096]{1,2,0:T(8,128)(2,1)} %bitcast.151) | data formatting | bytes 4194304 | tf_op jit(solution)/shard_map/all_to_all | solution.py:110
  222.7 6.3 %all_to_all.75 = bf16[2,128,4096]{2,1,0:T(8,128)(2,1)} all-to-all(bf16[2,128,4096]{2,1,0:T(8,128)(2,1)S(1)} %copy.79), channel_id=1, replica_groups=mesh['group'=2,'blk'=8,'ulysses'=2] {'ulysses'}, dimensions={0} | all-to-all | bytes 4194304 | tf_op jit(solution)/shard_map/all_to_all | solution.py:110
  229.0 3.1 %copy.69 = bf16[2,128,4096]{1,2,0:T(8,128)(2,1)S(1)} copy(bf16[2,128,4096]{2,1,0:T(8,128)(2,1)} %all_to_all.75) | data formatting | bytes 4194304 | tf_op jit(solution)/shard_map/all_to_all | solution.py:110
  (117 shorter events, 74.7 us)
Async XLA Ops:
  6.5 20.0 %copy-start = (bf16[16,8]{0,1:T(8,128)(2,1)S(1)}, bf16[16,8]{0,1:T(8,128)(2,1)}, u32[]{:S(2)}) copy-start(bf16[16,8]{0,1:T(8,128)(2,1)} %param.15) | copy-start | bytes 772
  6.5 12.1 %copy-start.1 = (bf16[128,8192]{1,0:T(8,128)(2,1)S(1)}, bf16[128,8192]{1,0:T(8,128)(2,1)}, u32[]{:S(2)}) copy-start(bf16[128,8192]{1,0:T(8,128)(2,1)} %param.11) | copy-start | bytes 6291460
  6.5 58.2 %all-gather.3.cloned.1.call-start = ((), (), s32[]{:S(2)}) async-start(), calls=%async_computation.4 | async-start | bytes 2359296 | tf_op jit(solution)/shard_map/all_gather | solution.py:98
  12.6 102.1 %all-gather.5.cloned.1.call-start = ((), (), s32[]{:S(2)}) async-start(), calls=%async_computation.5 | async-start | bytes 2359296 | tf_op jit(solution)/shard_map/all_gather | solution.py:99
  18.6 7.6 %copy-start.2 = (s32[8,8]{1,0:T(8,128)S(1)}, s32[8,8]{1,0:T(8,128)}, u32[]{:S(2)}) copy-start(s32[8,8]{1,0:T(8,128)} %param.17) | copy-start | bytes 772
  18.7 7.6 %copy-start.3 = (s32[8,8]{1,0:T(8,128)S(1)}, s32[8,8]{1,0:T(8,128)}, u32[]{:S(2)}) copy-start(s32[8,8]{1,0:T(8,128)} %param.16) | copy-start | bytes 772
  21.1 7.1 %copy-start.4 = (bf16[2,64]{1,0:T(2,128)(2,1)S(1)}, bf16[2,64]{1,0:T(2,128)(2,1)}, u32[]{:S(2)}) copy-start(bf16[2,64]{1,0:T(2,128)(2,1)} %param.14) | copy-start | bytes 772
  21.1 108.8 %all-to-all-start = ((bf16[128,2,4096]{0,2,1:T(8,128)(2,1)}), bf16[128,2,4096]{0,2,1:T(8,128)(2,1)}, u32[]{:S(2)}, u32[]{:S(2)}) async-start(bf16[128,2,4096]{0,2,1:T(8,128)(2,1)} %bitcast.27), calls=%async_computation | async-start | bytes 4194304 | tf_op jit(solution)/shard_map/all_to_all | solution.py:76
Sparse Core Ops, SparseCore 0:
  12.8 51.9 all-gather.2
  66.9 47.7 all-gather.4
where the time goes:
time: 243 us; the launch traced here: 242 us
  waiting for transfers between devices  79.7 us (33%)
  local copies, waits for them, and re-layouts  58.4 us (24%)
  matrix products  48.1 us (20%)
  other arithmetic  22.2 us (9%)
  blocking collectives  14.2 us (6%)
  between operations  13.6 us (6%)
  starting transfers between devices  5.08 us (2%)
    all_gather x1, waiting for transfers between devices, local(): lax.all_gather(value_here, 'blk', axis=0, tiled=True)  43.8 us
    all_gather x1, waiting for transfers between devices, local(): lax.all_gather(key_here, 'blk', axis=0, tiled=True)  35.8 us
    dot_general x8, matrix products, attend_group(): jnp.einsum('ptns,nsd->tpd', weights.astype(jnp.bfloat16), value_blocks, p...  28.8 us
    reduce_sum x8, other arithmetic, attend_group(): totals = jnp.sum(weights, axis=(2, 3))  19.3 us
    dot_general x8, matrix products, attend_group(): jnp.einsum('tpd,nsd->ptns', query_block, key_blocks, preferred_element_ty...  19.2 us
    dynamic_slice x8, local copies, waits for them, and re-layouts, local(): lax.map(attend_block, (query_blocks, query_scales, key_blocks, value_bloc...  14 us
    reshape x4, local copies, waits for them, and re-layouts, gather_blocks(): shaped = buffer.reshape(buffer.shape[0] // BLOCK, BLOCK, groups, DH)  13.5 us
    all_to_all x3, local copies, waits for them, and re-layouts, local(): lax.all_to_all(merged, 'ulysses', split_axis=0, concat_axis=1, tiled=True)  8.94 us
  transfers between devices with their start and end apart: 3, of which 2 were waited for; matrix products, arithmetic and copies ran while one was open for 12% of the time, Pallas kernels for 0%

commit v1 on v0

v1 whole, which is shorter than its diff:
```python
import functools

import jax
import jax.numpy as jnp
from jax import lax
from jax.experimental import pallas as pl
from jax.experimental.pallas import tpu as pltpu
from jax.sharding import PartitionSpec as P

DH = 128
FLOOR_SCORE = -1e30
LOG2E = 1.4426950408889634
NT = (((1,), (1,)), ((), ()))
F32 = jnp.float32
BF16 = jnp.bfloat16


def attend(count, diagonal, first, group, block, per_group, scale_at, keys_ref, values_ref, query_ref, state):
    most_ref, total_ref, sum_ref = state
    width = per_group * block
    base = pl.multiple_of(group * width, width)
    wide = pl.multiple_of(group * per_group * DH, per_group * DH)
    keys = keys_ref[0 : count * block, :]
    values = values_ref[:, 0 : count * block]

    def dots_of(head):
        query = query_ref[:, pl.ds(wide + head * DH, DH)]
        return lax.dot_general(keys, query, NT, preferred_element_type=F32)

    def weigh(head, dots):
        here = pl.ds(base + head * block, block)
        parts = []
        for slot in range(count):
            part = dots[slot * block : (slot + 1) * block] * scale_at(slot, head)
            if diagonal and slot == 0:
                key_at = lax.broadcasted_iota(jnp.int32, part.shape, 0)
                query_at = lax.broadcasted_iota(jnp.int32, part.shape, 1)
                part = jnp.where(key_at <= query_at, part, FLOOR_SCORE)
            parts.append(part)
        most = functools.reduce(jnp.maximum, [jnp.max(part, axis=0, keepdims=True) for part in parts])
        shrink = None
        if not first:
            before = most_ref[:, here]
            most = jnp.maximum(most, before)
            shrink = jnp.exp2(before - most)
        weights = [jnp.exp2(part - most) for part in parts]
        total = functools.reduce(jnp.add, [jnp.sum(part, axis=0, keepdims=True) for part in weights])
        if not first:
            total = total + total_ref[:, here] * shrink
        most_ref[:, here] = most
        total_ref[:, here] = total
        return jnp.concatenate([part.astype(BF16) for part in weights], axis=0), shrink

    def gather(head, probs, shrink):
        here = pl.ds(base + head * block, block)
        add = jnp.dot(values, probs, preferred_element_type=F32)
        sum_ref[:, here] = add if first else sum_ref[:, here] * shrink + add

    dots = dots_of(0)
    pending = None
    for head in range(per_group):
        ahead = dots_of(head + 1) if head + 1 < per_group else None
        if pending is not None:
            gather(*pending)
        pending = (head,) + weigh(head, dots)
        dots = ahead
    gather(*pending)


def chunk_kernel(pieces, first, last, groups, per_group, block, *refs):
    scale_ref, live_ref, query_ref = refs[:3]
    piece_refs = refs[3 : 3 + pieces]
    rest = refs[3 + pieces :]
    if first:
        state, rest = rest[:3], rest[3:]
    else:
        rest = rest[3:]
        state, rest = rest[:3], rest[3:]
    if last:
        out_ref, rest = rest[0], rest[1:]
    keys_ref, values_ref, slot_ref = rest
    width = per_group * block

    @pl.loop(0, groups)
    def _(group):
        count = jnp.int32(0)
        column = pl.ds(pl.multiple_of(group * DH, DH), DH)
        for piece in range(pieces):
            live = live_ref[piece, group]

            @pl.when(live > 0)
            def _(piece=piece, count=count):
                at = pl.ds(pl.multiple_of(count * block, block), block)
                keys_ref[at, :] = piece_refs[piece][0:block, column]
                values_ref[:, at] = piece_refs[piece][block : 2 * block, column].T
                slot_ref[count] = piece

            count = count + live

        def scale_at(slot, head):
            return scale_ref[slot_ref[slot], group * per_group + head]

        for many in range(1, pieces + 1):

            @pl.when(count == many)
            def _(many=many):
                attend(
                    many, first, first, group, block, per_group, scale_at, keys_ref, values_ref, query_ref, state
                )

        if last:
            for head in range(per_group):
                here = pl.ds(pl.multiple_of(group * width, width) + head * block, block)
                done = state[2][:, here] / state[1][:, here]
                out_ref[:, pl.ds(pl.multiple_of(group * per_group * DH, DH) + head * DH, DH)] = done.T.astype(BF16)


def attend_chunk(query, pieces, scales, live, state, last):
    rows, features = query.shape
    heads = scales.shape[1]
    groups = live.shape[1]
    block = rows
    first = state is None
    count = len(pieces)
    kernel = functools.partial(chunk_kernel, count, first, last, groups, heads // groups, block)
    smem = pl.BlockSpec(memory_space=pltpu.SMEM)
    vmem = pl.BlockSpec(memory_space=pltpu.VMEM)
    state_shape = [
        jax.ShapeDtypeStruct((1, heads * block), F32),
        jax.ShapeDtypeStruct((1, heads * block), F32),
        jax.ShapeDtypeStruct((DH, heads * block), F32),
    ]
    out_shape = state_shape + ([jax.ShapeDtypeStruct(query.shape, BF16)] if last else [])
    operands = [scales, live, query, *pieces] + ([] if first else list(state))
    flops = 4 * count * block * block * heads * DH
    outs = pl.pallas_call(
        kernel,
        in_specs=[smem, smem] + [vmem] * (len(operands) - 2),
        out_specs=[vmem] * len(out_shape),
        out_shape=out_shape,
        scratch_shapes=[
            pltpu.VMEM((count * block, DH), BF16),
            pltpu.VMEM((DH, count * block), BF16),
            pltpu.SMEM((count,), jnp.int32),
        ],
        input_output_aliases={} if first else {3 + count + i: i for i in range(3)},
        compiler_params=pltpu.CompilerParams(vmem_limit_bytes=24 * 2**20),
        cost_estimate=pl.CostEstimate(flops=flops, bytes_accessed=0, transcendentals=0),
    )(*operands)
    return outs[3] if last else outs


def local(spans, cores, query_int, key_int, values, query_scale, key_scale, verticals, slashes):
    block = query_int.shape[0]
    heads = query_int.shape[1] // DH
    groups = key_int.shape[1] // DH
    pair = 2 if spans % 2 == 0 else 1
    lines = spans // pair
    span = lax.axis_index("blk")
    core = lax.axis_index("ulysses")
    line, side = span // pair, span % pair
    here = span * cores + core

    own = jnp.concatenate([key_int, values], axis=0)
    climb = [(s, s + pair) for s in range(spans - pair)]
    swap = [(s, s ^ 1) for s in range(spans)]
    turn = [(c, (c + 1) % cores) for c in range(cores)]

    def both(piece, origin):
        found = [(piece, origin(core))]
        for step in range(1, cores):
            piece = lax.ppermute(piece, "ulysses", turn)
            found.append((piece, origin((core - step) % cores)))
        return found

    chunks = [both(own, lambda c: span * cores + c)]
    climbed = own
    for step in range(lines):
        fresh = []
        crossed = lax.ppermute(climbed, "blk", swap) if pair == 2 else None
        behind = line - step
        if step + 1 < lines:
            climbed = lax.ppermute(climbed, "blk", climb)
            before = behind - 1
            fresh += both(climbed, lambda c: jnp.where(before >= 0, (before * pair + side) * cores + c, here + 1))
        if pair == 2:
            fresh += both(crossed, lambda c: jnp.where(behind >= 0, (behind * pair + 1 - side) * cores + c, here + 1))
        chunks.append(fresh)

    query_scales = lax.dynamic_slice_in_dim(query_scale, core, 1, 0).astype(F32)
    state = None
    for index, chunk in enumerate(chunks):
        places = jnp.stack([place for _, place in chunk]).astype(jnp.int32)
        seen = jnp.any(places[:, None, None] == here - slashes[None], axis=2) | jnp.any(
            places[:, None, None] == verticals[None], axis=2
        )
        live = (seen & (places <= here)[:, None]).astype(jnp.int32)
        key_scales = key_scale[jnp.minimum(places, key_scale.shape[0] - 1)].astype(F32)
        scales = query_scales * jnp.repeat(key_scales, heads // groups, axis=1) * LOG2E
        state = attend_chunk(
            query_int, [piece for piece, _ in chunk], scales, live, state, index + 1 == len(chunks)
        )
    return state


def solution(mesh):
    rows = P(("group", "blk", "ulysses"), None)
    in_specs = (rows, rows, rows, P(("group", "blk"), None), P("group", None), P("group", None), P("group", None))
    run = functools.partial(local, mesh.shape["blk"], mesh.shape["ulysses"])
    return jax.shard_map(run, mesh=mesh, in_specs=in_specs, out_specs=rows, check_vma=False)
```

time: 243 us -> 112 us (0.46)
  the two profiles are of different devices: /device:TPU:0 before, /device:TPU:31 now
where the time goes in v1:
time: 112 us; the launch traced here: 111 us
  Pallas kernels  45.9 us (41%)
  waiting for transfers between devices  38.1 us (34%)
  starting transfers between devices  14.7 us (13%)
  local copies, waits for them, and re-layouts  7.88 us (7%)
  other arithmetic  4.6 us (4%)
    pallas_call x5, Pallas kernels, attend_chunk(): pl.pallas_call(kernel, in_specs=[smem, smem] + [vmem] * (len(operands) -...  45.9 us
    ppermute x3, waiting for transfers between devices, local(): climbed = lax.ppermute(climbed, 'blk', climb)  27 us
    ppermute x4, waiting for transfers between devices, local(): crossed = lax.ppermute(climbed, 'blk', swap) if pair == 2 else None  11.1 us
    ppermute x8, starting transfers between devices, both(): piece = lax.ppermute(piece, 'ulysses', turn)  8.9 us
    ppermute x3, starting transfers between devices, local(): climbed = lax.ppermute(climbed, 'blk', climb)  3.84 us
    unnamed x6, local copies, waits for them, and re-layouts  3.32 us
    gather x5, local copies, waits for them, and re-layouts, local(): key_scale[jnp.minimum(places, key_scale.shape[0] - 1)].astype(F32)  2.82 us
  transfers between devices with their start and end apart: 15, of which 5 were waited for; matrix products, arithmetic and copies ran while one was open for 8% of the time, Pallas kernels for 32%

profile of v1, /device:TPU:31, one launch (start us, length us, event | category | flops | bytes accessed | tf_op | source)
XLA Modules:
  0.0 111.4 jit_solution(12832593841019028975)
XLA Ops:
  0.0 1.0 constant_dynamic-update-slice_fusion.1
  1.0 1.0 constant_dynamic-update-slice_fusion.refs_3_
  2.7 1.3 %collective-permute-start = (bf16[256,1024]{1,0:T(8,128)(2,1)S(1)}, bf16[256,1024]{1,0:T(8,128)(2,1)S(1)}, u32[]{:S(2)}, u32[]{:S(2)}) collective-permute-start(bf16[256,1024]{1,0:T(8,128)(2,1)S(1)} %constant_dynamic-update-slice_fusion.refs_3_), channel_id=1, source_target_pairs={{0,4},{2,6},{4,8},{6,10},{8,12},{10,14},{1,5},{3,7},{5,9},{7,11},{... | collective-permute-start | bytes 1572872 | tf_op jit(solution)/shard_map/ppermute | solution.py:183
  10.0 1.2 %compare_reduce_fusion.1 = (pred[4,8]{1,0:T(4,128)(4,1)S(1)}, pred[4,8]{1,0:T(4,128)(4,1)S(1)}, pred[4,8]{1,0:T(4,128)(4,1)S(1)}, pred[4,8]{1,0:T(4,128)(4,1)S(1...) fusion(s32[8,8]{1,0:T(8,128)S(1)} %broadcast_subtract_fusion, s32[4]{0:T(128)S(1)} %get-tuple-element.49, ...), kind=kLoop, calls=%fused_computation.6 | loop fusion | flops 2880 | bytes 752 | tf_op jit(solution)/shard_map/reduce_or | solution.py:194
  11.3 6.8 %collective-permute-done.refs_3_ = bf16[256,1024]{1,0:T(8,128)(2,1)S(1)} collective-permute-done((bf16[256,1024]{1,0:T(8,128)(2,1)S(1)}, bf16[256,1024]{1,0:T(8,128)(2,1)S(1)}, u32[]{:S(2)}, u32[]{:S(2)}) %collective-permute-start) | collective-permute-done | bytes 524320 | tf_op jit(solution)/shard_map/ppermute | solution.py:183
  18.1 1.3 %collective-permute-start.1 = (bf16[256,1024]{1,0:T(8,128)(2,1)S(1)}, bf16[256,1024]{1,0:T(8,128)(2,1)S(1)}, u32[]{:S(2)}, u32[]{:S(2)}) collective-permute-start(bf16[256,1024]{1,0:T(8,128)(2,1)S(1)} %collective-permute-done.refs_3_), channel_id=1, source_target_pairs={{0,4},{2,6},{4,8},{6,10},{8,12},{10,14},{1,5},{3,7},{5,9},{7,11},{... | collective-permute-start | bytes 1572872 | tf_op jit(solution)/shard_map/ppermute | solution.py:183
  20.1 12.5 %collective-permute-done.1.refs_3_ = bf16[256,1024]{1,0:T(8,128)(2,1)S(1)} collective-permute-done((bf16[256,1024]{1,0:T(8,128)(2,1)S(1)}, bf16[256,1024]{1,0:T(8,128)(2,1)S(1)}, u32[]{:S(2)}, u32[]{:S(2)}) %collective-permute-start.1) | collective-permute-done | bytes 524320 | tf_op jit(solution)/shard_map/ppermute | solution.py:183
  32.6 1.3 %collective-permute-start.2 = (bf16[256,1024]{1,0:T(8,128)(2,1)S(1)}, bf16[256,1024]{1,0:T(8,128)(2,1)S(1)}, u32[]{:S(2)}, u32[]{:S(2)}) collective-permute-start(bf16[256,1024]{1,0:T(8,128)(2,1)S(1)} %collective-permute-done.1.refs_3_), channel_id=1, source_target_pairs={{0,4},{2,6},{4,8},{6,10},{8,12},{10,14},{1,5},{3,7},{5,9},{7,11},{... | collective-permute-start | bytes 1572872 | tf_op jit(solution)/shard_map/ppermute | solution.py:183
  34.0 1.7 %collective-permute-start.11 = (bf16[256,1024]{1,0:T(8,128)(2,1)S(1)}, bf16[256,1024]{1,0:T(8,128)(2,1)S(1)}, u32[]{:S(2)}, u32[]{:S(2)}) collective-permute-start(bf16[256,1024]{1,0:T(8,128)(2,1)S(1)} %collective-permute-done.refs_3_), channel_id=1, source_target_pairs={{0,1},{1,0},{2,3},{3,2},{4,5},{5,4},{6,7},{7,6},{8,9},{9,8},{10,11... | collective-permute-start | bytes 1572872 | tf_op jit(solution)/shard_map/ppermute | solution.py:172
  36.3 1.2 %collective-permute-start.6 = (bf16[256,1024]{1,0:T(8,128)(2,1)S(1)}, bf16[256,1024]{1,0:T(8,128)(2,1)S(1)}, u32[]{:S(2)}, u32[]{:S(2)}) collective-permute-start(bf16[256,1024]{1,0:T(8,128)(2,1)S(1)} %collective-permute-done.1.refs_3_), channel_id=1, source_target_pairs={{0,2},{2,0},{4,6},{6,4},{8,10},{10,8},{12,14},{14,12},{1,3},{3,1},... | collective-permute-start | bytes 1572872 | tf_op jit(solution)/shard_map/ppermute | solution.py:180
  37.5 1.0 compare_reduce_fusion.7
  38.5 7.7 %collective-permute-done.2.refs_3_ = bf16[256,1024]{1,0:T(8,128)(2,1)S(1)} collective-permute-done((bf16[256,1024]{1,0:T(8,128)(2,1)S(1)}, bf16[256,1024]{1,0:T(8,128)(2,1)S(1)}, u32[]{:S(2)}, u32[]{:S(2)}) %collective-permute-start.2) | collective-permute-done | bytes 524320 | tf_op jit(solution)/shard_map/ppermute | solution.py:183
  46.5 2.9 %collective-permute-start.8 = (bf16[256,1024]{1,0:T(8,128)(2,1)S(1)}, bf16[256,1024]{1,0:T(8,128)(2,1)S(1)}, u32[]{:S(2)}, u32[]{:S(2)}) collective-permute-start(bf16[256,1024]{1,0:T(8,128)(2,1)S(1)} %collective-permute-done.1.refs_3_), channel_id=1, source_target_pairs={{0,1},{1,0},{2,3},{3,2},{4,5},{5,4},{6,7},{7,6},{8,9},{9,8},{10,11... | collective-permute-start | bytes 1572872 | tf_op jit(solution)/shard_map/ppermute | solution.py:172
  49.4 1.1 collective-permute-start.10
  50.5 9.9 %collective-permute-done.6.refs_5_ = bf16[256,1024]{1,0:T(8,128)(2,1)S(1)} collective-permute-done((bf16[256,1024]{1,0:T(8,128)(2,1)S(1)}, bf16[256,1024]{1,0:T(8,128)(2,1)S(1)}, u32[]{:S(2)}, u32[]{:S(2)}) %collective-permute-start.6) | collective-permute-done | bytes 524320 | tf_op jit(solution)/shard_map/ppermute | solution.py:180
  60.4 1.3 %collective-permute-start.7 = (bf16[256,1024]{1,0:T(8,128)(2,1)S(1)}, bf16[256,1024]{1,0:T(8,128)(2,1)S(1)}, u32[]{:S(2)}, u32[]{:S(2)}) collective-permute-start(bf16[256,1024]{1,0:T(8,128)(2,1)S(1)} %collective-permute-done.6.refs_5_), channel_id=1, source_target_pairs={{0,1},{1,0},{2,3},{3,2},{4,5},{5,4},{6,7},{7,6},{8,9},{9,8},{10,11... | collective-permute-start | bytes 1572872 | tf_op jit(solution)/shard_map/ppermute | solution.py:172
  61.8 1.6 %copy-done = bf16[128,8192]{1,0:T(8,128)(2,1)S(1)} copy-done((bf16[128,8192]{1,0:T(8,128)(2,1)S(1)}, bf16[128,8192]{1,0:T(8,128)(2,1)}, u32[]{:S(2)}) %copy-start) | copy-done | bytes 2097176
  63.4 7.1 %shard_map.73 = (f32[1,8192]{1,0:T(1,128)S(1)}, f32[1,8192]{1,0:T(1,128)S(1)}, f32[128,8192]{1,0:T(8,128)S(1)}) custom-call(f32[2,64]{1,0:T(2,128)S(1)} %get-tuple-element.56.refs_0_, s32[2,8]{1,0:T(2,128)S(1)} %and_convert_fusion.refs_1_, bf16[128,8192]{1,0:T(8,128)(2,1)S(1)} %copy-done, bf16[256,1024]{1,0:T(8,128)(2,1)S(1)} %constant_dynamic-update-slice_fusion.refs_3_, ...), custom_call_target="tpu_custom_call" | custom-call | flops 1073741824 | tf_op jit(solution)/shard_map/pallas_call | solution.py:136
  70.5 1.1 %collective-permute-done.3.refs_3_ = bf16[256,1024]{1,0:T(8,128)(2,1)S(1)} collective-permute-done((bf16[256,1024]{1,0:T(8,128)(2,1)S(1)}, bf16[256,1024]{1,0:T(8,128)(2,1)S(1)}, u32[]{:S(2)}, u32[]{:S(2)}) %collective-permute-start.3) | collective-permute-done | bytes 524320 | tf_op jit(solution)/shard_map/ppermute | solution.py:180
  71.7 0.8 collective-permute-start.4
  72.5 11.0 %shard_map.74 = (f32[1,8192]{1,0:T(1,128)S(1)}, f32[1,8192]{1,0:T(1,128)S(1)}, f32[128,8192]{1,0:T(8,128)S(1)}) custom-call(f32[4,64]{1,0:T(4,128)S(1)} %get-tuple-element.58.refs_0_, s32[4,8]{1,0:T(4,128)S(1)} %and_convert_fusion.1.refs_1_, bf16[128,8192]{1,0:T(8,128)(2,1)S(1)} %copy-done.1, ...), custom_call_target="tpu_custom_call", output_to_operand_aliasing={{0}: (7, {}), {1}: (8, {}), {2}: (9, {})} | custom-call | flops 2147483648 | tf_op jit(solution)/shard_map/pallas_call | solution.py:136
  83.6 9.7 %shard_map.75 = (f32[1,8192]{1,0:T(1,128)S(1)}, f32[1,8192]{1,0:T(1,128)S(1)}, f32[128,8192]{1,0:T(8,128)S(1)}) custom-call(f32[4,64]{1,0:T(4,128)S(1)} %get-tuple-element.59.refs_0_, s32[4,8]{1,0:T(4,128)S(1)} %and_convert_fusion.2.refs_1_, bf16[128,8192]{1,0:T(8,128)(2,1)S(1)} %copy-done.1, ...), custom_call_target="tpu_custom_call", output_to_operand_aliasing={{0}: (7, {}), {1}: (8, {}), {2}: (9, {})} | custom-call | flops 2147483648 | tf_op jit(solution)/shard_map/pallas_call | solution.py:136
  93.4 8.0 %shard_map.76 = (f32[1,8192]{1,0:T(1,128)S(1)}, f32[1,8192]{1,0:T(1,128)S(1)}, f32[128,8192]{1,0:T(8,128)S(1)}) custom-call(f32[4,64]{1,0:T(4,128)S(1)} %get-tuple-element.60.refs_0_, s32[4,8]{1,0:T(4,128)S(1)} %and_convert_fusion.3.refs_1_, bf16[128,8192]{1,0:T(8,128)(2,1)S(1)} %copy-done.1, ...), custom_call_target="tpu_custom_call", output_to_operand_aliasing={{0}: (7, {}), {1}: (8, {}), {2}: (9, {})} | custom-call | flops 2147483648 | tf_op jit(solution)/shard_map/pallas_call | solution.py:136
  101.4 10.0 %shard_map.77 = (f32[1,8192]{1,0:T(1,128)S(1)}, f32[1,8192]{1,0:T(1,128)S(1)}, f32[128,8192]{1,0:T(8,128)S(1)}, bf16[128,8192]{1,0:T(8,128)(2,1)}) custom-call(f32[2,64]{1,0:T(2,128)S(1)} %get-tuple-element.57.refs_0_, s32[2,8]{1,0:T(2,128)S(1)} %and_convert_fusion.4.refs_1_, ...), custom_call_target="tpu_custom_call", output_to_operand_aliasing={{0}: (5, {}), {1}: (6, {}), {2}: (7, {})} | custom-call | flops 1073741824 | tf_op jit(solution)/shard_map/pallas_call | solution.py:136
  (55 shorter events, 8.6 us)
Async XLA Ops:
  1.9 34.3 %collective-permute-start.14 = (bf16[256,1024]{1,0:T(8,128)(2,1)S(1)}, bf16[256,1024]{1,0:T(8,128)(2,1)S(1)}, u32[]{:S(2)}, u32[]{:S(2)}) collective-permute-start(bf16[256,1024]{1,0:T(8,128)(2,1)S(1)} %constant_dynamic-update-slice_fusion.refs_3_), channel_id=1, source_target_pairs={{0,1},{1,0},{2,3},{3,2},{4,5},{5,4},{6,7},{7,6},{8,9},{9,8},{10,11... | collective-permute-start | bytes 1572872 | tf_op jit(solution)/shard_map/ppermute | solution.py:172
  2.7 15.4 %collective-permute-start = (bf16[256,1024]{1,0:T(8,128)(2,1)S(1)}, bf16[256,1024]{1,0:T(8,128)(2,1)S(1)}, u32[]{:S(2)}, u32[]{:S(2)}) collective-permute-start(bf16[256,1024]{1,0:T(8,128)(2,1)S(1)} %constant_dynamic-update-slice_fusion.refs_3_), channel_id=1, source_target_pairs={{0,4},{2,6},{4,8},{6,10},{8,12},{10,14},{1,5},{3,7},{5,9},{7,11},{... | collective-permute-start | bytes 1572872 | tf_op jit(solution)/shard_map/ppermute | solution.py:183
  4.0 32.0 %collective-permute-start.12 = (bf16[256,1024]{1,0:T(8,128)(2,1)S(1)}, bf16[256,1024]{1,0:T(8,128)(2,1)S(1)}, u32[]{:S(2)}, u32[]{:S(2)}) collective-permute-start(bf16[256,1024]{1,0:T(8,128)(2,1)S(1)} %constant_dynamic-update-slice_fusion.refs_3_), channel_id=1, source_target_pairs={{0,2},{2,0},{4,6},{6,4},{8,10},{10,8},{12,14},{14,12},{1,3},{3,1},... | collective-permute-start | bytes 1572872 | tf_op jit(solution)/shard_map/ppermute | solution.py:180
  18.1 14.5 %collective-permute-start.1 = (bf16[256,1024]{1,0:T(8,128)(2,1)S(1)}, bf16[256,1024]{1,0:T(8,128)(2,1)S(1)}, u32[]{:S(2)}, u32[]{:S(2)}) collective-permute-start(bf16[256,1024]{1,0:T(8,128)(2,1)S(1)} %collective-permute-done.refs_3_), channel_id=1, source_target_pairs={{0,4},{2,6},{4,8},{6,10},{8,12},{10,14},{1,5},{3,7},{5,9},{7,11},{... | collective-permute-start | bytes 1572872 | tf_op jit(solution)/shard_map/ppermute | solution.py:183
  32.6 13.6 %collective-permute-start.2 = (bf16[256,1024]{1,0:T(8,128)(2,1)S(1)}, bf16[256,1024]{1,0:T(8,128)(2,1)S(1)}, u32[]{:S(2)}, u32[]{:S(2)}) collective-permute-start(bf16[256,1024]{1,0:T(8,128)(2,1)S(1)} %collective-permute-done.1.refs_3_), channel_id=1, source_target_pairs={{0,4},{2,6},{4,8},{6,10},{8,12},{10,14},{1,5},{3,7},{5,9},{7,11},{... | collective-permute-start | bytes 1572872 | tf_op jit(solution)/shard_map/ppermute | solution.py:183
  34.0 12.5 %collective-permute-start.11 = (bf16[256,1024]{1,0:T(8,128)(2,1)S(1)}, bf16[256,1024]{1,0:T(8,128)(2,1)S(1)}, u32[]{:S(2)}, u32[]{:S(2)}) collective-permute-start(bf16[256,1024]{1,0:T(8,128)(2,1)S(1)} %collective-permute-done.refs_3_), channel_id=1, source_target_pairs={{0,1},{1,0},{2,3},{3,2},{4,5},{5,4},{6,7},{7,6},{8,9},{9,8},{10,11... | collective-permute-start | bytes 1572872 | tf_op jit(solution)/shard_map/ppermute | solution.py:172
  35.7 13.7 %collective-permute-start.9 = (bf16[256,1024]{1,0:T(8,128)(2,1)S(1)}, bf16[256,1024]{1,0:T(8,128)(2,1)S(1)}, u32[]{:S(2)}, u32[]{:S(2)}) collective-permute-start(bf16[256,1024]{1,0:T(8,128)(2,1)S(1)} %collective-permute-done.refs_3_), channel_id=1, source_target_pairs={{0,2},{2,0},{4,6},{6,4},{8,10},{10,8},{12,14},{14,12},{1,3},{3,1},... | collective-permute-start | bytes 1572872 | tf_op jit(solution)/shard_map/ppermute | solution.py:180
  35.9 14.6 %collective-permute-start.13 = (bf16[256,1024]{1,0:T(8,128)(2,1)S(1)}, bf16[256,1024]{1,0:T(8,128)(2,1)S(1)}, u32[]{:S(2)}, u32[]{:S(2)}) collective-permute-start(bf16[256,1024]{1,0:T(8,128)(2,1)S(1)} %collective-permute-done.12.refs_5_), channel_id=1, source_target_pairs={{0,1},{1,0},{2,3},{3,2},{4,5},{5,4},{6,7},{7,6},{8,9},{9,8},{10,11... | collective-permute-start | bytes 1572872 | tf_op jit(solution)/shard_map/ppermute | solution.py:172
  36.3 24.1 %collective-permute-start.6 = (bf16[256,1024]{1,0:T(8,128)(2,1)S(1)}, bf16[256,1024]{1,0:T(8,128)(2,1)S(1)}, u32[]{:S(2)}, u32[]{:S(2)}) collective-permute-start(bf16[256,1024]{1,0:T(8,128)(2,1)S(1)} %collective-permute-done.1.refs_3_), channel_id=1, source_target_pairs={{0,2},{2,0},{4,6},{6,4},{8,10},{10,8},{12,14},{14,12},{1,3},{3,1},... | collective-permute-start | bytes 1572872 | tf_op jit(solution)/shard_map/ppermute | solution.py:180
  46.2 25.4 %collective-permute-start.3 = (bf16[256,1024]{1,0:T(8,128)(2,1)S(1)}, bf16[256,1024]{1,0:T(8,128)(2,1)S(1)}, u32[]{:S(2)}, u32[]{:S(2)}) collective-permute-start(bf16[256,1024]{1,0:T(8,128)(2,1)S(1)} %collective-permute-done.2.refs_3_), channel_id=1, source_target_pairs={{0,2},{2,0},{4,6},{6,4},{8,10},{10,8},{12,14},{14,12},{1,3},{3,1},... | collective-permute-start | bytes 1572872 | tf_op jit(solution)/shard_map/ppermute | solution.py:180
  46.5 37.0 %collective-permute-start.8 = (bf16[256,1024]{1,0:T(8,128)(2,1)S(1)}, bf16[256,1024]{1,0:T(8,128)(2,1)S(1)}, u32[]{:S(2)}, u32[]{:S(2)}) collective-permute-start(bf16[256,1024]{1,0:T(8,128)(2,1)S(1)} %collective-permute-done.1.refs_3_), channel_id=1, source_target_pairs={{0,1},{1,0},{2,3},{3,2},{4,5},{5,4},{6,7},{7,6},{8,9},{9,8},{10,11... | collective-permute-start | bytes 1572872 | tf_op jit(solution)/shard_map/ppermute | solution.py:172
  49.4 34.1 %collective-permute-start.10 = (bf16[256,1024]{1,0:T(8,128)(2,1)S(1)}, bf16[256,1024]{1,0:T(8,128)(2,1)S(1)}, u32[]{:S(2)}, u32[]{:S(2)}) collective-permute-start(bf16[256,1024]{1,0:T(8,128)(2,1)S(1)} %collective-permute-done.9.refs_5_), channel_id=1, source_target_pairs={{0,1},{1,0},{2,3},{3,2},{4,5},{5,4},{6,7},{7,6},{8,9},{9,8},{10,11... | collective-permute-start | bytes 1572872 | tf_op jit(solution)/shard_map/ppermute | solution.py:172
  50.5 42.8 %collective-permute-start.5 = (bf16[256,1024]{1,0:T(8,128)(2,1)S(1)}, bf16[256,1024]{1,0:T(8,128)(2,1)S(1)}, u32[]{:S(2)}, u32[]{:S(2)}) collective-permute-start(bf16[256,1024]{1,0:T(8,128)(2,1)S(1)} %collective-permute-done.2.refs_3_), channel_id=1, source_target_pairs={{0,1},{1,0},{2,3},{3,2},{4,5},{5,4},{6,7},{7,6},{8,9},{9,8},{10,11... | collective-permute-start | bytes 1572872 | tf_op jit(solution)/shard_map/ppermute | solution.py:172
  60.4 32.9 %collective-permute-start.7 = (bf16[256,1024]{1,0:T(8,128)(2,1)S(1)}, bf16[256,1024]{1,0:T(8,128)(2,1)S(1)}, u32[]{:S(2)}, u32[]{:S(2)}) collective-permute-start(bf16[256,1024]{1,0:T(8,128)(2,1)S(1)} %collective-permute-done.6.refs_5_), channel_id=1, source_target_pairs={{0,1},{1,0},{2,3},{3,2},{4,5},{5,4},{6,7},{7,6},{8,9},{9,8},{10,11... | collective-permute-start | bytes 1572872 | tf_op jit(solution)/shard_map/ppermute | solution.py:172
  61.8 1.6 %copy-start = (bf16[128,8192]{1,0:T(8,128)(2,1)S(1)}, bf16[128,8192]{1,0:T(8,128)(2,1)}, u32[]{:S(2)}) copy-start(bf16[128,8192]{1,0:T(8,128)(2,1)} %refs_2_.9) | copy-start | bytes 6291460
  63.4 9.1 %copy-start.1 = (bf16[128,8192]{1,0:T(8,128)(2,1)S(1)}, bf16[128,8192]{1,0:T(8,128)(2,1)}, u32[]{:S(2)}) copy-start(bf16[128,8192]{1,0:T(8,128)(2,1)} %refs_2_.9) | copy-start | bytes 6291460
  71.7 29.7 %collective-permute-start.4 = (bf16[256,1024]{1,0:T(8,128)(2,1)S(1)}, bf16[256,1024]{1,0:T(8,128)(2,1)S(1)}, u32[]{:S(2)}, u32[]{:S(2)}) collective-permute-start(bf16[256,1024]{1,0:T(8,128)(2,1)S(1)} %collective-permute-done.3.refs_3_), channel_id=1, source_target_pairs={{0,1},{1,0},{2,3},{3,2},{4,5},{5,4},{6,7},{7,6},{8,9},{9,8},{10,11... | collective-permute-start | bytes 1572872 | tf_op jit(solution)/shard_map/ppermute | solution.py:172

commit v2 on v1

--- a/solution.py
+++ b/solution.py
@@ -173,33 +173,39 @@
             found.append((piece, origin((core - step) % cores)))
         return found
 
-    chunks = [both(own, lambda c: span * cores + c)]
-    climbed = own
-    for step in range(lines):
-        fresh = []
-        crossed = lax.ppermute(climbed, "blk", swap) if pair == 2 else None
-        behind = line - step
-        if step + 1 < lines:
-            climbed = lax.ppermute(climbed, "blk", climb)
-            before = behind - 1
-            fresh += both(climbed, lambda c: jnp.where(before >= 0, (before * pair + side) * cores + c, here + 1))
-        if pair == 2:
-            fresh += both(crossed, lambda c: jnp.where(behind >= 0, (behind * pair + 1 - side) * cores + c, here + 1))
-        chunks.append(fresh)
-
     query_scales = lax.dynamic_slice_in_dim(query_scale, core, 1, 0).astype(F32)
-    state = None
-    for index, chunk in enumerate(chunks):
-        places = jnp.stack([place for _, place in chunk]).astype(jnp.int32)
+
+    def table(places):
+        places = jnp.stack(places).astype(jnp.int32)
         seen = jnp.any(places[:, None, None] == here - slashes[None], axis=2) | jnp.any(
             places[:, None, None] == verticals[None], axis=2
         )
         live = (seen & (places <= here)[:, None]).astype(jnp.int32)
         key_scales = key_scale[jnp.minimum(places, key_scale.shape[0] - 1)].astype(F32)
-        scales = query_scales * jnp.repeat(key_scales, heads // groups, axis=1) * LOG2E
-        state = attend_chunk(
-            query_int, [piece for piece, _ in chunk], scales, live, state, index + 1 == len(chunks)
-        )
+        return query_scales * jnp.repeat(key_scales, heads // groups, axis=1) * LOG2E, live
+
+    climbed, crossed, state = own, None, None
+    for step in range(lines + (pair == 2)):
+        behind = line - step
+        fresh = []
+        arrived = []
+        if step < lines:
+            arrived.append((climbed, behind, side))
+        if crossed is not None:
+            arrived.append((crossed, behind + 1, 1 - side))
+        sent = climbed
+        crossed = lax.ppermute(sent, "blk", swap) if pair == 2 and step < lines else None
+        climbed = lax.ppermute(sent, "blk", climb) if step + 1 < lines else None
+        for piece, from_line, from_side in arrived:
+            fresh += both(
+                piece,
+                lambda c: jnp.where(from_line >= 0, (from_line * pair + from_side) * cores + c, here + 1),
+            )
+        scales, live = table([place for _, place in fresh])
+        last = step + 1 == lines + (pair == 2)
+        state = attend_chunk(query_int, [piece for piece, _ in fresh], scales, live, state, last)
+        if not last:
+            climbed, crossed, state = lax.optimization_barrier((climbed, crossed, state))
     return state
 
 

time: 112 us -> 90.8 us (0.81)
  waiting for transfers between devices: 38.1 us -> 10.3 us
  local copies, waits for them, and re-layouts: 7.88 us -> 15.2 us
  starting transfers between devices: 14.7 us -> 11.6 us
  Pallas kernels: 45.9 us -> 47.6 us
    ppermute x7, waiting for transfers between devices: 38.1 us -> 7.25 us  [the longest x3 3.74 us: local(): climbed = lax.ppermute(sent, 'blk', climb) if step + 1 < lines else None]
    unnamed x6 -> x14, local copies, waits for them, and re-layouts: 3.32 us -> 9.95 us
    ppermute x8, starting transfers between devices: 8.9 us -> 4.69 us  [both(): piece = lax.ppermute(piece, 'ulysses', turn)]
    ppermute x8, waiting for transfers between devices: 0.02 us -> 3.09 us  [both(): piece = lax.ppermute(piece, 'ulysses', turn)]
    pallas_call x5, Pallas kernels: 45.9 us -> 47.6 us  [attend_chunk(): pl.pallas_call(kernel, in_specs=[smem, smem] + [vmem] * (len(operands) -...]
  transfers between devices with their start and end apart: 15 -> 15, of which waited for: 5 -> 7; matrix products, arithmetic and copies ran while one was open for 8% -> 10% of each run, Pallas kernels for 32% -> 42%
where the time goes in v2:
time: 90.8 us; the launch traced here: 89.6 us
  Pallas kernels  47.6 us (52%)
  local copies, waits for them, and re-layouts  15.2 us (17%)
  starting transfers between devices  11.6 us (13%)
  waiting for transfers between devices  10.3 us (11%)
  other arithmetic  4.61 us (5%)
    pallas_call x5, Pallas kernels, attend_chunk(): pl.pallas_call(kernel, in_specs=[smem, smem] + [vmem] * (len(operands) -...  47.6 us
    unnamed x14, local copies, waits for them, and re-layouts  9.95 us
    ppermute x8, starting transfers between devices, both(): piece = lax.ppermute(piece, 'ulysses', turn)  4.69 us
    ppermute x3, starting transfers between devices, local(): climbed = lax.ppermute(sent, 'blk', climb) if step + 1 < lines else None  4.02 us
    ppermute x3, waiting for transfers between devices, local(): climbed = lax.ppermute(sent, 'blk', climb) if step + 1 < lines else None  3.74 us
    ppermute x4, waiting for transfers between devices, local(): lax.ppermute(sent, 'blk', swap)  3.51 us
    ppermute x8, waiting for transfers between devices, both(): piece = lax.ppermute(piece, 'ulysses', turn)  3.09 us
    ppermute x4, starting transfers between devices, local(): lax.ppermute(sent, 'blk', swap)  2.93 us
  transfers between devices with their start and end apart: 15, of which 7 were waited for; matrix products, arithmetic and copies ran while one was open for 10% of the time, Pallas kernels for 42%

profile of v2, /device:TPU:31, one launch (start us, length us, event | category | flops | bytes accessed | tf_op | source)
XLA Modules:
  0.0 89.6 jit_solution(4866827197248450247)
XLA Ops:
  0.0 1.7 %constant_dynamic-update-slice_fusion.1 = bf16[256,1024]{1,0:T(8,128)(2,1)} fusion(bf16[128,1024]{1,0:T(8,128)(2,1)} %param.8), kind=kLoop, calls=%fused_computation.21 | loop fusion | bytes 524288
  1.7 1.7 %constant_dynamic-update-slice_fusion.refs_3_ = bf16[256,1024]{1,0:T(8,128)(2,1)} fusion(bf16[256,1024]{1,0:T(8,128)(2,1)} %constant_dynamic-update-slice_fusion.1, bf16[128,1024]{1,0:T(8,128)(2,1)} %param.9), kind=kLoop, calls=%fused_computation.20 | loop fusion | bytes 524288 | tf_op jit(solution)/shard_map/concatenate | solution.py:164
  4.2 1.3 %collective-permute-start = (bf16[256,1024]{1,0:T(8,128)(2,1)}, bf16[256,1024]{1,0:T(8,128)(2,1)S(1)}, u32[]{:S(2)}, u32[]{:S(2)}) collective-permute-start(bf16[256,1024]{1,0:T(8,128)(2,1)} %constant_dynamic-update-slice_fusion.refs_3_), channel_id=1, source_target_pairs={{0,4},{2,6},{4,8},{6,10},{8,12},{10,14},{1,5},{3,7},{5,9},{7,11},{... | collective-permute-start | bytes 1572872 | tf_op jit(solution)/shard_map/ppermute | solution.py:198
  9.6 1.0 %compare_reduce_fusion.7 = (pred[2,8]{1,0:T(4,128)(4,1)S(1)}, pred[2,8]{1,0:T(4,128)(4,1)S(1)}, pred[2,8]{1,0:T(4,128)(4,1)S(1)}, pred[2,8]{1,0:T(4,128)(4,1)S(1)}) fusion(s32[8,8]{1,0:T(8,128)S(1)} %broadcast_subtract_fusion, s32[2]{0:T(128)S(1)} %get-tuple-element.91, s32[2]{0:T(128)S(1)} %get-tuple-element.102, s32[8,8]{1,0:T(8,128)} %param.12), kind=kLoop, calls=%fused_computation.12 | loop fusion | flops 960 | bytes 592 | tf_op jit(solution)/shard_map/reduce_or | solution.py:180
  10.7 1.2 %compare_reduce_fusion.1 = (pred[4,8]{1,0:T(4,128)(4,1)S(1)}, pred[4,8]{1,0:T(4,128)(4,1)S(1)}, pred[4,8]{1,0:T(4,128)(4,1)S(1)}, pred[4,8]{1,0:T(4,128)(4,1)S(1...) fusion(s32[8,8]{1,0:T(8,128)S(1)} %broadcast_subtract_fusion, s32[4]{0:T(128)S(1)} %get-tuple-element.85, ...), kind=kLoop, calls=%fused_computation.6 | loop fusion | flops 2880 | bytes 752 | tf_op jit(solution)/shard_map/reduce_or | solution.py:180
  13.0 1.6 %copy-done.2 = bf16[128,8192]{1,0:T(8,128)(2,1)S(1)} copy-done((bf16[128,8192]{1,0:T(8,128)(2,1)S(1)}, bf16[128,8192]{1,0:T(8,128)(2,1)}, u32[]{:S(2)}) %copy-start.2) | copy-done | bytes 2097176
  14.5 1.0 %copy-done.5 = bf16[256,1024]{1,0:T(8,128)(2,1)S(1)} copy-done((bf16[256,1024]{1,0:T(8,128)(2,1)S(1)}, bf16[256,1024]{1,0:T(8,128)(2,1)}, u32[]{:S(2)}) %copy-start.5) | copy-done | bytes 524312
  15.6 7.7 %shard_map.73 = (f32[1,8192]{1,0:T(1,128)S(1)}, f32[1,8192]{1,0:T(1,128)S(1)}, f32[128,8192]{1,0:T(8,128)S(1)}) custom-call(f32[2,64]{1,0:T(2,128)S(1)} %get-tuple-element.97.refs_0_, s32[2,8]{1,0:T(2,128)S(1)} %and_convert_fusion.3.refs_1_, bf16[128,8192]{1,0:T(8,128)(2,1)S(1)} %copy-done.2, bf16[256,1024]{1,0:T(8,128)(2,1)} %constant_dynamic-update-slice_fusion.refs_3_, ...), custom_call_target="tpu_custom_call" | custom-call | flops 1073741824 | tf_op jit(solution)/shard_map/pallas_call | solution.py:136
  23.3 1.9 %copy-done = f32[128,8192]{1,0:T(8,128)} copy-done((f32[128,8192]{1,0:T(8,128)}, f32[128,8192]{1,0:T(8,128)S(1)}, u32[]{:S(2)}) %copy-start) | copy-done | bytes 4194328
  25.2 1.0 %collective-permute-start.6 = (bf16[256,1024]{1,0:T(8,128)(2,1)S(1)}, bf16[256,1024]{1,0:T(8,128)(2,1)}, u32[]{:S(2)}, u32[]{:S(2)}) collective-permute-start(bf16[256,1024]{1,0:T(8,128)(2,1)S(1)} %collective-permute-done.1.refs_5_), channel_id=1, source_target_pairs={{0,1},{1,0},{2,3},{3,2},{4,5},{5,4},{6,7},{7,6},{8,9},{9,8},{10,11... | collective-permute-start | bytes 1572872 | tf_op jit(solution)/shard_map/ppermute | solution.py:172
  26.3 1.2 %collective-permute-start.4 = (bf16[256,1024]{1,0:T(8,128)(2,1)S(1)}, bf16[256,1024]{1,0:T(8,128)(2,1)}, u32[]{:S(2)}, u32[]{:S(2)}) collective-permute-start(bf16[256,1024]{1,0:T(8,128)(2,1)S(1)} %collective-permute-done.refs_3_), channel_id=1, source_target_pairs={{0,2},{2,0},{4,6},{6,4},{8,10},{10,8},{12,14},{14,12},{1,3},{3,1},... | collective-permute-start | bytes 1572872 | tf_op jit(solution)/shard_map/ppermute | solution.py:197
  27.6 1.3 %collective-permute-start.3 = (bf16[256,1024]{1,0:T(8,128)(2,1)S(1)}, bf16[256,1024]{1,0:T(8,128)(2,1)}, u32[]{:S(2)}, u32[]{:S(2)}) collective-permute-start(bf16[256,1024]{1,0:T(8,128)(2,1)S(1)} %collective-permute-done.refs_3_), channel_id=1, source_target_pairs={{0,4},{2,6},{4,8},{6,10},{8,12},{10,14},{1,5},{3,7},{5,9},{7,11},{... | collective-permute-start | bytes 1572872 | tf_op jit(solution)/shard_map/ppermute | solution.py:198
  31.1 2.2 %copy-done.1 = f32[128,8192]{1,0:T(8,128)S(1)} copy-done((f32[128,8192]{1,0:T(8,128)S(1)}, f32[128,8192]{1,0:T(8,128)}, u32[]{:S(2)}) %copy-start.1) | copy-done | bytes 4194328
  33.3 11.6 %shard_map.74 = (f32[1,8192]{1,0:T(1,128)S(1)}, f32[1,8192]{1,0:T(1,128)S(1)}, f32[128,8192]{1,0:T(8,128)S(1)}) custom-call(f32[4,64]{1,0:T(4,128)S(1)} %get-tuple-element.96.refs_0_, s32[4,8]{1,0:T(4,128)S(1)} %and_convert_fusion.2.refs_1_, bf16[128,8192]{1,0:T(8,128)(2,1)S(1)} %copy-done.3, ...), custom_call_target="tpu_custom_call", output_to_operand_aliasing={{0}: (7, {}), {1}: (8, {}), {2}: (9, {})} | custom-call | flops 2147483648 | tf_op jit(solution)/shard_map/pallas_call | solution.py:136
  45.6 1.5 %collective-permute-start.7 = (bf16[256,1024]{1,0:T(8,128)(2,1)}, bf16[256,1024]{1,0:T(8,128)(2,1)S(1)}, u32[]{:S(2)}, u32[]{:S(2)}) collective-permute-start(bf16[256,1024]{1,0:T(8,128)(2,1)} %collective-permute-done.3.refs_3_), channel_id=1, source_target_pairs={{0,4},{2,6},{4,8},{6,10},{8,12},{10,14},{1,5},{3,7},{5,9},{7,11},{... | collective-permute-start | bytes 1572872 | tf_op jit(solution)/shard_map/ppermute | solution.py:198
  48.0 9.8 %shard_map.75 = (f32[1,8192]{1,0:T(1,128)S(1)}, f32[1,8192]{1,0:T(1,128)S(1)}, f32[128,8192]{1,0:T(8,128)S(1)}) custom-call(f32[4,64]{1,0:T(4,128)S(1)} %get-tuple-element.95.refs_0_, s32[4,8]{1,0:T(4,128)S(1)} %and_convert_fusion.1.refs_1_, bf16[128,8192]{1,0:T(8,128)(2,1)S(1)} %copy-done.3, ...), custom_call_target="tpu_custom_call", output_to_operand_aliasing={{0}: (7, {}), {1}: (8, {}), {2}: (9, {})} | custom-call | flops 2147483648 | tf_op jit(solution)/shard_map/pallas_call | solution.py:136
  57.8 1.0 %collective-permute-done.8.refs_5_ = bf16[256,1024]{1,0:T(8,128)(2,1)S(1)} collective-permute-done((bf16[256,1024]{1,0:T(8,128)(2,1)}, bf16[256,1024]{1,0:T(8,128)(2,1)S(1)}, u32[]{:S(2)}, u32[]{:S(2)}) %collective-permute-start.8) | collective-permute-done | bytes 524320 | tf_op jit(solution)/shard_map/ppermute | solution.py:197
  58.8 3.7 %collective-permute-done.7.refs_3_ = bf16[256,1024]{1,0:T(8,128)(2,1)S(1)} collective-permute-done((bf16[256,1024]{1,0:T(8,128)(2,1)}, bf16[256,1024]{1,0:T(8,128)(2,1)S(1)}, u32[]{:S(2)}, u32[]{:S(2)}) %collective-permute-start.7) | collective-permute-done | bytes 524320 | tf_op jit(solution)/shard_map/ppermute | solution.py:198
  63.5 1.5 %collective-permute-start.11 = (bf16[256,1024]{1,0:T(8,128)(2,1)S(1)}, bf16[256,1024]{1,0:T(8,128)(2,1)S(1)}, u32[]{:S(2)}, u32[]{:S(2)}) collective-permute-start(bf16[256,1024]{1,0:T(8,128)(2,1)S(1)} %collective-permute-done.7.refs_3_), channel_id=1, source_target_pairs={{0,2},{2,0},{4,6},{6,4},{8,10},{10,8},{12,14},{14,12},{1,3},{3,1},... | collective-permute-start | bytes 1572872 | tf_op jit(solution)/shard_map/ppermute | solution.py:197
  65.8 8.2 %shard_map.76 = (f32[1,8192]{1,0:T(1,128)S(1)}, f32[1,8192]{1,0:T(1,128)S(1)}, f32[128,8192]{1,0:T(8,128)S(1)}) custom-call(f32[4,64]{1,0:T(4,128)S(1)} %get-tuple-element.94.refs_0_, s32[4,8]{1,0:T(4,128)S(1)} %and_convert_fusion.refs_1_, bf16[128,8192]{1,0:T(8,128)(2,1)S(1)} %copy-done.3, ...), custom_call_target="tpu_custom_call", output_to_operand_aliasing={{0}: (7, {}), {1}: (8, {}), {2}: (9, {})} | custom-call | flops 2147483648 | tf_op jit(solution)/shard_map/pallas_call | solution.py:136
  74.1 2.5 %collective-permute-done.11.refs_3_ = bf16[256,1024]{1,0:T(8,128)(2,1)S(1)} collective-permute-done((bf16[256,1024]{1,0:T(8,128)(2,1)S(1)}, bf16[256,1024]{1,0:T(8,128)(2,1)S(1)}, u32[]{:S(2)}, u32[]{:S(2)}) %collective-permute-start.11) | collective-permute-done | bytes 524320 | tf_op jit(solution)/shard_map/ppermute | solution.py:197
  76.5 1.4 %collective-permute-start.14 = (bf16[256,1024]{1,0:T(8,128)(2,1)S(1)}, bf16[256,1024]{1,0:T(8,128)(2,1)S(1)}, u32[]{:S(2)}, u32[]{:S(2)}) collective-permute-start(bf16[256,1024]{1,0:T(8,128)(2,1)S(1)} %collective-permute-done.11.refs_3_), channel_id=1, source_target_pairs={{0,1},{1,0},{2,3},{3,2},{4,5},{5,4},{6,7},{7,6},{8,9},{9,8},{10,11... | collective-permute-start | bytes 1572872 | tf_op jit(solution)/shard_map/ppermute | solution.py:172
  78.0 1.5 %collective-permute-done.14.refs_4_ = bf16[256,1024]{1,0:T(8,128)(2,1)S(1)} collective-permute-done((bf16[256,1024]{1,0:T(8,128)(2,1)S(1)}, bf16[256,1024]{1,0:T(8,128)(2,1)S(1)}, u32[]{:S(2)}, u32[]{:S(2)}) %collective-permute-start.14) | collective-permute-done | bytes 524320 | tf_op jit(solution)/shard_map/ppermute | solution.py:172
  79.4 10.2 %shard_map.77 = (f32[1,8192]{1,0:T(1,128)S(1)}, f32[1,8192]{1,0:T(1,128)S(1)}, f32[128,8192]{1,0:T(8,128)S(1)}, bf16[128,8192]{1,0:T(8,128)(2,1)}) custom-call(f32[2,64]{1,0:T(2,128)S(1)} %get-tuple-element.98.refs_0_, s32[2,8]{1,0:T(2,128)S(1)} %and_convert_fusion.4.refs_1_, ...), custom_call_target="tpu_custom_call", output_to_operand_aliasing={{0}: (5, {}), {1}: (6, {}), {2}: (7, {})} | custom-call | flops 1073741824 | tf_op jit(solution)/shard_map/pallas_call | solution.py:136
  (63 shorter events, 11.7 us)
Async XLA Ops:
  3.3 8.8 %collective-permute-start.2 = (bf16[256,1024]{1,0:T(8,128)(2,1)}, bf16[256,1024]{1,0:T(8,128)(2,1)S(1)}, u32[]{:S(2)}, u32[]{:S(2)}) collective-permute-start(bf16[256,1024]{1,0:T(8,128)(2,1)} %constant_dynamic-update-slice_fusion.refs_3_), channel_id=1, source_target_pairs={{0,1},{1,0},{2,3},{3,2},{4,5},{5,4},{6,7},{7,6},{8,9},{9,8},{10,11... | collective-permute-start | bytes 1572872 | tf_op jit(solution)/shard_map/ppermute | solution.py:172
  4.0 21.2 %collective-permute-start.1 = (bf16[256,1024]{1,0:T(8,128)(2,1)}, bf16[256,1024]{1,0:T(8,128)(2,1)S(1)}, u32[]{:S(2)}, u32[]{:S(2)}) collective-permute-start(bf16[256,1024]{1,0:T(8,128)(2,1)} %constant_dynamic-update-slice_fusion.refs_3_), channel_id=1, source_target_pairs={{0,2},{2,0},{4,6},{6,4},{8,10},{10,8},{12,14},{14,12},{1,3},{3,1},... | collective-permute-start | bytes 1572872 | tf_op jit(solution)/shard_map/ppermute | solution.py:197
  4.2 21.0 %collective-permute-start = (bf16[256,1024]{1,0:T(8,128)(2,1)}, bf16[256,1024]{1,0:T(8,128)(2,1)S(1)}, u32[]{:S(2)}, u32[]{:S(2)}) collective-permute-start(bf16[256,1024]{1,0:T(8,128)(2,1)} %constant_dynamic-update-slice_fusion.refs_3_), channel_id=1, source_target_pairs={{0,4},{2,6},{4,8},{6,10},{8,12},{10,14},{1,5},{3,7},{5,9},{7,11},{... | collective-permute-start | bytes 1572872 | tf_op jit(solution)/shard_map/ppermute | solution.py:198
  12.2 0.8 copy-start.4
  13.0 1.6 %copy-start.2 = (bf16[128,8192]{1,0:T(8,128)(2,1)S(1)}, bf16[128,8192]{1,0:T(8,128)(2,1)}, u32[]{:S(2)}) copy-start(bf16[128,8192]{1,0:T(8,128)(2,1)} %refs_2_.9) | copy-start | bytes 6291460
  14.5 1.0 %copy-start.5 = (bf16[256,1024]{1,0:T(8,128)(2,1)S(1)}, bf16[256,1024]{1,0:T(8,128)(2,1)}, u32[]{:S(2)}) copy-start(bf16[256,1024]{1,0:T(8,128)(2,1)} %copy-done.4) | copy-start | bytes 1572868
  15.6 15.5 %copy-start.3 = (bf16[128,8192]{1,0:T(8,128)(2,1)S(1)}, bf16[128,8192]{1,0:T(8,128)(2,1)}, u32[]{:S(2)}) copy-start(bf16[128,8192]{1,0:T(8,128)(2,1)} %refs_2_.9) | copy-start | bytes 6291460
  23.3 1.9 %copy-start = (f32[128,8192]{1,0:T(8,128)}, f32[128,8192]{1,0:T(8,128)S(1)}, u32[]{:S(2)}) copy-start(f32[128,8192]{1,0:T(8,128)S(1)} %get-tuple-element.44.refs_9_) | copy-start | bytes 12582916
  25.2 5.8 %collective-permute-start.6 = (bf16[256,1024]{1,0:T(8,128)(2,1)S(1)}, bf16[256,1024]{1,0:T(8,128)(2,1)}, u32[]{:S(2)}, u32[]{:S(2)}) collective-permute-start(bf16[256,1024]{1,0:T(8,128)(2,1)S(1)} %collective-permute-done.1.refs_5_), channel_id=1, source_target_pairs={{0,1},{1,0},{2,3},{3,2},{4,5},{5,4},{6,7},{7,6},{8,9},{9,8},{10,11... | collective-permute-start | bytes 1572872 | tf_op jit(solution)/shard_map/ppermute | solution.py:172
  26.2 4.9 %collective-permute-start.5 = (bf16[256,1024]{1,0:T(8,128)(2,1)S(1)}, bf16[256,1024]{1,0:T(8,128)(2,1)}, u32[]{:S(2)}, u32[]{:S(2)}) collective-permute-start(bf16[256,1024]{1,0:T(8,128)(2,1)S(1)} %collective-permute-done.refs_3_), channel_id=1, source_target_pairs={{0,1},{1,0},{2,3},{3,2},{4,5},{5,4},{6,7},{7,6},{8,9},{9,8},{10,11... | collective-permute-start | bytes 1572872 | tf_op jit(solution)/shard_map/ppermute | solution.py:172
  26.3 18.6 %collective-permute-start.4 = (bf16[256,1024]{1,0:T(8,128)(2,1)S(1)}, bf16[256,1024]{1,0:T(8,128)(2,1)}, u32[]{:S(2)}, u32[]{:S(2)}) collective-permute-start(bf16[256,1024]{1,0:T(8,128)(2,1)S(1)} %collective-permute-done.refs_3_), channel_id=1, source_target_pairs={{0,2},{2,0},{4,6},{6,4},{8,10},{10,8},{12,14},{14,12},{1,3},{3,1},... | collective-permute-start | bytes 1572872 | tf_op jit(solution)/shard_map/ppermute | solution.py:197
  27.6 17.3 %collective-permute-start.3 = (bf16[256,1024]{1,0:T(8,128)(2,1)S(1)}, bf16[256,1024]{1,0:T(8,128)(2,1)}, u32[]{:S(2)}, u32[]{:S(2)}) collective-permute-start(bf16[256,1024]{1,0:T(8,128)(2,1)S(1)} %collective-permute-done.refs_3_), channel_id=1, source_target_pairs={{0,4},{2,6},{4,8},{6,10},{8,12},{10,14},{1,5},{3,7},{5,9},{7,11},{... | collective-permute-start | bytes 1572872 | tf_op jit(solution)/shard_map/ppermute | solution.py:198
  31.1 2.2 %copy-start.1 = (f32[128,8192]{1,0:T(8,128)S(1)}, f32[128,8192]{1,0:T(8,128)}, u32[]{:S(2)}) copy-start(f32[128,8192]{1,0:T(8,128)} %copy-done) | copy-start | bytes 12582916
  44.9 2.3 %collective-permute-start.10 = (bf16[256,1024]{1,0:T(8,128)(2,1)}, bf16[256,1024]{1,0:T(8,128)(2,1)S(1)}, u32[]{:S(2)}, u32[]{:S(2)}) collective-permute-start(bf16[256,1024]{1,0:T(8,128)(2,1)} %collective-permute-done.4.refs_5_), channel_id=1, source_target_pairs={{0,1},{1,0},{2,3},{3,2},{4,5},{5,4},{6,7},{7,6},{8,9},{9,8},{10,11... | collective-permute-start | bytes 1572872 | tf_op jit(solution)/shard_map/ppermute | solution.py:172
  45.5 2.5 %collective-permute-start.9 = (bf16[256,1024]{1,0:T(8,128)(2,1)}, bf16[256,1024]{1,0:T(8,128)(2,1)S(1)}, u32[]{:S(2)}, u32[]{:S(2)}) collective-permute-start(bf16[256,1024]{1,0:T(8,128)(2,1)} %collective-permute-done.3.refs_3_), channel_id=1, source_target_pairs={{0,1},{1,0},{2,3},{3,2},{4,5},{5,4},{6,7},{7,6},{8,9},{9,8},{10,11... | collective-permute-start | bytes 1572872 | tf_op jit(solution)/shard_map/ppermute | solution.py:172
  45.6 13.3 %collective-permute-start.8 = (bf16[256,1024]{1,0:T(8,128)(2,1)}, bf16[256,1024]{1,0:T(8,128)(2,1)S(1)}, u32[]{:S(2)}, u32[]{:S(2)}) collective-permute-start(bf16[256,1024]{1,0:T(8,128)(2,1)} %collective-permute-done.3.refs_3_), channel_id=1, source_target_pairs={{0,2},{2,0},{4,6},{6,4},{8,10},{10,8},{12,14},{14,12},{1,3},{3,1},... | collective-permute-start | bytes 1572872 | tf_op jit(solution)/shard_map/ppermute | solution.py:197
  45.6 17.0 %collective-permute-start.7 = (bf16[256,1024]{1,0:T(8,128)(2,1)}, bf16[256,1024]{1,0:T(8,128)(2,1)S(1)}, u32[]{:S(2)}, u32[]{:S(2)}) collective-permute-start(bf16[256,1024]{1,0:T(8,128)(2,1)} %collective-permute-done.3.refs_3_), channel_id=1, source_target_pairs={{0,4},{2,6},{4,8},{6,10},{8,12},{10,14},{1,5},{3,7},{5,9},{7,11},{... | collective-permute-start | bytes 1572872 | tf_op jit(solution)/shard_map/ppermute | solution.py:198
  62.6 2.5 %collective-permute-start.13 = (bf16[256,1024]{1,0:T(8,128)(2,1)S(1)}, bf16[256,1024]{1,0:T(8,128)(2,1)S(1)}, u32[]{:S(2)}, u32[]{:S(2)}) collective-permute-start(bf16[256,1024]{1,0:T(8,128)(2,1)S(1)} %collective-permute-done.8.refs_5_), channel_id=1, source_target_pairs={{0,1},{1,0},{2,3},{3,2},{4,5},{5,4},{6,7},{7,6},{8,9},{9,8},{10,11... | collective-permute-start | bytes 1572872 | tf_op jit(solution)/shard_map/ppermute | solution.py:172
  63.5 2.3 %collective-permute-start.12 = (bf16[256,1024]{1,0:T(8,128)(2,1)S(1)}, bf16[256,1024]{1,0:T(8,128)(2,1)S(1)}, u32[]{:S(2)}, u32[]{:S(2)}) collective-permute-start(bf16[256,1024]{1,0:T(8,128)(2,1)S(1)} %collective-permute-done.7.refs_3_), channel_id=1, source_target_pairs={{0,1},{1,0},{2,3},{3,2},{4,5},{5,4},{6,7},{7,6},{8,9},{9,8},{10,11... | collective-permute-start | bytes 1572872 | tf_op jit(solution)/shard_map/ppermute | solution.py:172
  63.5 13.0 %collective-permute-start.11 = (bf16[256,1024]{1,0:T(8,128)(2,1)S(1)}, bf16[256,1024]{1,0:T(8,128)(2,1)S(1)}, u32[]{:S(2)}, u32[]{:S(2)}) collective-permute-start(bf16[256,1024]{1,0:T(8,128)(2,1)S(1)} %collective-permute-done.7.refs_3_), channel_id=1, source_target_pairs={{0,2},{2,0},{4,6},{6,4},{8,10},{10,8},{12,14},{14,12},{1,3},{3,1},... | collective-permute-start | bytes 1572872 | tf_op jit(solution)/shard_map/ppermute | solution.py:197
  76.5 2.9 %collective-permute-start.14 = (bf16[256,1024]{1,0:T(8,128)(2,1)S(1)}, bf16[256,1024]{1,0:T(8,128)(2,1)S(1)}, u32[]{:S(2)}, u32[]{:S(2)}) collective-permute-start(bf16[256,1024]{1,0:T(8,128)(2,1)S(1)} %collective-permute-done.11.refs_3_), channel_id=1, source_target_pairs={{0,1},{1,0},{2,3},{3,2},{4,5},{5,4},{6,7},{7,6},{8,9},{9,8},{10,11... | collective-permute-start | bytes 1572872 | tf_op jit(solution)/shard_map/ppermute | solution.py:172

commit v3 on v2

v3 whole, which is shorter than its diff:
```python
import functools

import jax
import jax.numpy as jnp
from jax import lax
from jax.experimental import pallas as pl
from jax.experimental.pallas import tpu as pltpu
from jax.sharding import PartitionSpec as P

DH = 128
FLOOR_SCORE = -1e30
LOG2E = 1.4426950408889634
NT = (((1,), (1,)), ((), ()))
F32 = jnp.float32
BF16 = jnp.bfloat16
VMEM_LIMIT = 16 * 2**20


def along_rows(combine, parts):
    rows = [part[at : at + 8] for part in parts for at in range(0, part.shape[0], 8)]
    lanes = rows[:4]
    for at, row in enumerate(rows[4:]):
        lanes[at % 4] = combine(lanes[at % 4], row)
    return functools.reduce(combine, lanes)


def attend(count, diagonal, first, group, block, per_group, scale_at, keys_ref, values_ref, query_ref, state):
    most_ref, total_ref, sum_ref = state
    base = pl.multiple_of(group * per_group * block, per_group * block)
    keys = keys_ref[0 : count * block, :]
    values = values_ref[:, 0 : count * block]

    def dots_of(head):
        return lax.dot_general(keys, query_ref[:, head * DH : (head + 1) * DH], NT, preferred_element_type=F32)

    def weigh(head, dots):
        here = pl.ds(base + head * block, block)
        parts = []
        for slot in range(count):
            part = dots[slot * block : (slot + 1) * block] * scale_at(slot, head)
            if diagonal and slot == 0:
                key_at = lax.broadcasted_iota(jnp.int32, part.shape, 0)
                query_at = lax.broadcasted_iota(jnp.int32, part.shape, 1)
                part = jnp.where(key_at <= query_at, part, FLOOR_SCORE)
            parts.append(part)
        most = jnp.max(along_rows(jnp.maximum, parts), axis=0, keepdims=True)
        shrink = None
        if not first:
            old = most_ref[:, here]
            most = jnp.maximum(most, old)
            shrink = jnp.exp2(old - most)
        weights = [jnp.exp2(part - most) for part in parts]
        total = jnp.sum(along_rows(jnp.add, weights), axis=0, keepdims=True)
        if not first:
            total = total + total_ref[:, here] * shrink
        most_ref[:, here] = most
        total_ref[:, here] = total
        return jnp.concatenate([part.astype(BF16) for part in weights], axis=0), shrink

    def gather(head, probs, shrink):
        here = pl.ds(base + head * block, block)
        add = jnp.dot(values, probs, preferred_element_type=F32)
        sum_ref[:, here] = add if first else sum_ref[:, here] * shrink + add

    dots = dots_of(0)
    pending = None
    for head in range(per_group):
        ahead = dots_of(head + 1) if head + 1 < per_group else None
        if pending is not None:
            gather(*pending)
        pending = (head,) + weigh(head, dots)
        dots = ahead
    gather(*pending)


def stack_kernel(top_ref, low_ref, out_ref, sems):
    rows = top_ref.shape[0]
    top = pltpu.make_async_copy(top_ref, out_ref.at[0:rows], sems.at[0])
    low = pltpu.make_async_copy(low_ref, out_ref.at[rows : 2 * rows], sems.at[1])
    top.start()
    low.start()
    top.wait()
    low.wait()


def stack(top, low):
    hbm = pl.BlockSpec(memory_space=pl.ANY)
    pinned = [pltpu.with_memory_space_constraint(array, pltpu.HBM) for array in (top, low)]
    return pl.pallas_call(
        stack_kernel,
        in_specs=[hbm, hbm],
        out_specs=pl.BlockSpec(memory_space=pltpu.VMEM),
        out_shape=jax.ShapeDtypeStruct((2 * top.shape[0], top.shape[1]), top.dtype),
        scratch_shapes=[pltpu.SemaphoreType.DMA((2,))],
        compiler_params=pltpu.CompilerParams(vmem_limit_bytes=VMEM_LIMIT),
    )(*pinned)


def live_at(group, place, here, table_ref, groups, width):
    seen = jnp.int32(0)
    back = here - place
    for index in range(width):
        seen = seen | (table_ref[1 + group * width + index] == place).astype(jnp.int32)
        seen = seen | (table_ref[1 + (groups + group) * width + index] == back).astype(jnp.int32)
    return jnp.where((place >= 0) & (back >= 0), seen, 0)


def chunk_kernel(origins, first, last, groups, per_group, block, table_width, heads, *refs):
    pieces = len(origins)
    table_ref, scale_ref, query_hbm = refs[:3]
    piece_refs = refs[3 : 3 + pieces]
    rest = refs[3 + pieces :]
    if not first:
        rest = rest[3:]
    state, rest = rest[:3], rest[3:]
    if last:
        out_hbm, rest = rest[0], rest[1:]
    query_ref, keys_ref, raw_ref, values_ref, slot_ref, count_ref, sems, out_ref, out_sems = rest
    width = per_group * block
    wide = per_group * DH
    here = table_ref[0]
    places = [origin(here) for origin in origins]

    def query_copy(group, buffer):
        columns = pl.ds(pl.multiple_of(group * wide, wide), wide)
        return pltpu.make_async_copy(query_hbm.at[:, columns], query_ref.at[buffer], sems.at[0, buffer])

    def tile_copies(piece, group, buffer, at):
        column = pl.ds(pl.multiple_of(group * DH, DH), DH)
        rows = pl.ds(pl.multiple_of(at * block, block), block)
        source = piece_refs[piece]
        return (
            pltpu.make_async_copy(source.at[0:block, column], keys_ref.at[buffer, rows], sems.at[1, buffer]),
            pltpu.make_async_copy(source.at[block : 2 * block, column], raw_ref.at[buffer, rows], sems.at[2, buffer]),
        )

    def fetch(group, buffer):
        query_copy(group, buffer).start()
        count = jnp.int32(0)
        for piece, place in enumerate(places):
            live = live_at(group, place, here, table_ref, groups, table_width)

            @pl.when(live > 0)
            def _(piece=piece, count=count, place=place):
                for copy in tile_copies(piece, group, buffer, count):
                    copy.start()
                slot_ref[buffer, count] = place

            count = count + live
        count_ref[buffer] = count

    def out_copy(group, buffer):
        columns = pl.ds(pl.multiple_of(group * wide, wide), wide)
        return pltpu.make_async_copy(out_ref.at[buffer], out_hbm.at[:, columns], out_sems.at[buffer])

    fetch(0, 0)

    @pl.loop(0, groups)
    def _(group):
        buffer = lax.rem(group, 2)

        @pl.when(group + 1 < groups)
        def _():
            fetch(group + 1, 1 - buffer)

        query_copy(group, buffer).wait()
        count = count_ref[buffer]
        for at in range(pieces):

            @pl.when(at < count)
            def _(at=at):
                for copy in tile_copies(0, group, buffer, at):
                    copy.wait()

        def scale_at(slot, head):
            key_scale = scale_ref[heads + slot_ref[buffer, slot] * groups + group]
            return scale_ref[group * per_group + head] * key_scale * LOG2E

        for many in range(1, pieces + 1):

            @pl.when(count == many)
            def _(many=many):
                for at in range(many):
                    values_ref[:, at * block : (at + 1) * block] = raw_ref[buffer, at * block : (at + 1) * block].T
                attend(
                    many, first, first, group, block, per_group, scale_at, keys_ref.at[buffer], values_ref,
                    query_ref.at[buffer], state,
                )

        if last:

            @pl.when(group >= 2)
            def _():
                out_copy(group - 2, buffer).wait()

            for head in range(per_group):
                at = pl.ds(pl.multiple_of(group * width, width) + head * block, block)
                done = state[2][:, at] * (1.0 / state[1][:, at])
                out_ref[buffer, :, head * DH : (head + 1) * DH] = done.T.astype(BF16)
            out_copy(group, buffer).start()

    if last:
        for group in range(max(0, groups - 2), groups):
            out_copy(group, group % 2).wait()


def attend_chunk(table, scales, query, pieces, origins, state, last, groups, table_width):
    rows, features = query.shape
    heads = features // DH
    per_group = heads // groups
    block = rows
    first = state is None
    count = len(pieces)
    kernel = functools.partial(chunk_kernel, origins, first, last, groups, per_group, block, table_width, heads)
    smem = pl.BlockSpec(memory_space=pltpu.SMEM)
    vmem = pl.BlockSpec(memory_space=pltpu.VMEM)
    hbm = pl.BlockSpec(memory_space=pl.ANY)
    state_shape = [
        jax.ShapeDtypeStruct((1, heads * block), F32),
        jax.ShapeDtypeStruct((1, heads * block), F32),
        jax.ShapeDtypeStruct((DH, heads * block), F32),
    ]
    outs = pl.pallas_call(
        kernel,
        in_specs=[smem] * 2 + [hbm] * (1 + count) + ([] if first else [vmem] * 3),
        out_specs=[vmem] * 3 + ([hbm] if last else []),
        out_shape=state_shape + ([jax.ShapeDtypeStruct(query.shape, BF16)] if last else []),
        scratch_shapes=[
            pltpu.VMEM((2, block, per_group * DH), BF16),
            pltpu.VMEM((2, count * block, DH), BF16),
            pltpu.VMEM((2, count * block, DH), BF16),
            pltpu.VMEM((DH, count * block), BF16),
            pltpu.SMEM((2, count), jnp.int32),
            pltpu.SMEM((2,), jnp.int32),
            pltpu.SemaphoreType.DMA((3, 2)),
            pltpu.VMEM((2, block, per_group * DH), BF16),
            pltpu.SemaphoreType.DMA((2,)),
        ],
        input_output_aliases={} if first else {3 + count + i: i for i in range(3)},
        compiler_params=pltpu.CompilerParams(vmem_limit_bytes=VMEM_LIMIT),
        cost_estimate=pl.CostEstimate(flops=1, bytes_accessed=0, transcendentals=0),
    )(table, scales, query, *pieces, *(() if first else state))
    return outs[3] if last else outs


def local(spans, cores, query_int, key_int, values, query_scale, key_scale, verticals, slashes):
    pair = 2 if spans % 2 == 0 else 1
    lines = spans // pair
    span = lax.axis_index("blk")
    core = lax.axis_index("ulysses")
    here = span * cores + core

    own = stack(key_int, values)
    swap = [(s, s ^ 1) for s in range(spans)]
    turn = [(c, (c + 1) % cores) for c in range(cores)]
    climb = [(s, s + pair) for s in range(spans - pair)]
    groups, table_width = verticals.shape
    table = jnp.concatenate([here[None].astype(jnp.int32), verticals.reshape(-1), slashes.reshape(-1)])
    query_scales = lax.dynamic_slice_in_dim(query_scale, core, 1, 0)
    scales = jnp.concatenate([query_scales.reshape(-1), key_scale.reshape(-1)]).astype(F32)

    def both(piece, back, other):
        found = []
        for step in range(cores):
            if step:
                piece = lax.ppermute(piece, "ulysses", turn)

            def origin(at, step=step):
                at_core, at_span = at % cores, at // cores
                at_line, at_side = at_span // pair - back, at_span % pair
                if other:
                    at_side = pair - 1 - at_side
                place = (at_line * pair + at_side) * cores + (at_core + cores - step) % cores
                return jnp.where(at_line >= 0, place, -1)

            found.append((piece, origin))
        return found

    climbed, crossed, state = own, None, None
    steps = lines + (pair == 2)
    for step in range(steps):
        fresh = []
        sent, arrived = climbed, crossed
        climbed = lax.ppermute(sent, "blk", climb) if step + 1 < lines else None
        crossed = lax.ppermute(sent, "blk", swap) if pair == 2 and sent is not None else None
        if sent is not None:
            fresh += both(sent, step, False)
        if arrived is not None:
            fresh += both(arrived, step - 1, True)
        last = step + 1 == steps
        pieces, origins = zip(*fresh)
        state = attend_chunk(table, scales, query_int, pieces, origins, state, last, groups, table_width)
        if not last:
            climbed, crossed, state = lax.optimization_barrier((climbed, crossed, state))
    return state


def solution(mesh):
    rows = P(("group", "blk", "ulysses"), None)
    in_specs = (rows, rows, rows, P(("group", "blk"), None), P("group", None), P("group", None), P("group", None))
    run = functools.partial(local, mesh.shape["blk"], mesh.shape["ulysses"])
    return jax.shard_map(run, mesh=mesh, in_specs=in_specs, out_specs=rows, check_vma=False)
```

time: 90.8 us -> 78.8 us (0.87)
  local copies, waits for them, and re-layouts: 15.2 us -> 4 us
  waiting for transfers between devices: 10.3 us -> 15.3 us
  other arithmetic: 4.61 us -> 0.15 us
  Pallas kernels: 47.6 us -> 44.4 us
  starting transfers between devices: 11.6 us -> 13.4 us
    unnamed x14 -> x7, local copies, waits for them, and re-layouts: 9.95 us -> 2.36 us
    pallas_call x5 -> x6, Pallas kernels: 47.6 us -> 44.4 us  [the longest x5 43.3 us: attend_chunk(): pl.pallas_call(kernel, in_specs=[smem] * 2 + [hbm] * (1 + count) + ([] if...]
    gather x5 -> x0, local copies, waits for them, and re-layouts: 2.81 us -> none  [table(): key_scale[jnp.minimum(places, key_scale.shape[0] - 1)].astype(F32)]
    ppermute x3, waiting for transfers between devices: 3.74 us -> 6.38 us  [local(): climbed = lax.ppermute(sent, 'blk', climb) if step + 1 < lines else None]
    reduce_or x2 -> x0, other arithmetic: 2.22 us -> none  [table(): jnp.any(places[:, None, None] == here - slashes[None], axis=2)]
    ppermute x4, waiting for transfers between devices: 3.51 us -> 5.62 us  [local(): lax.ppermute(sent, 'blk', swap)]
    ppermute x8, starting transfers between devices: 4.69 us -> 6.64 us  [both(): piece = lax.ppermute(piece, 'ulysses', turn)]
    concatenate x1 -> x0, local copies, waits for them, and re-layouts: 1.67 us -> none  [local(): own = jnp.concatenate([key_int, values], axis=0)]
  transfers between devices with their start and end apart: 15 -> 15, of which waited for: 7 -> 10; matrix products, arithmetic and copies ran while one was open for 10% -> 3% of each run, Pallas kernels for 42% -> 44%
where the time goes in v3:
time: 78.8 us; the launch traced here: 77.6 us
  Pallas kernels  44.4 us (56%)
  waiting for transfers between devices  15.3 us (19%)
  starting transfers between devices  13.4 us (17%)
  local copies, waits for them, and re-layouts  4 us (5%)
    pallas_call x5, Pallas kernels, attend_chunk(): pl.pallas_call(kernel, in_specs=[smem] * 2 + [hbm] * (1 + count) + ([] if...  43.3 us
    ppermute x8, starting transfers between devices, both(): piece = lax.ppermute(piece, 'ulysses', turn)  6.64 us
    ppermute x3, waiting for transfers between devices, local(): climbed = lax.ppermute(sent, 'blk', climb) if step + 1 < lines else None  6.38 us
    ppermute x4, waiting for transfers between devices, local(): lax.ppermute(sent, 'blk', swap)  5.62 us
    ppermute x3, starting transfers between devices, local(): climbed = lax.ppermute(sent, 'blk', climb) if step + 1 < lines else None  3.84 us
    ppermute x8, waiting for transfers between devices, both(): piece = lax.ppermute(piece, 'ulysses', turn)  3.36 us
    ppermute x4, starting transfers between devices, local(): lax.ppermute(sent, 'blk', swap)  2.95 us
    unnamed x7, local copies, waits for them, and re-layouts  2.36 us
  transfers between devices with their start and end apart: 15, of which 10 were waited for; matrix products, arithmetic and copies ran while one was open for 3% of the time, Pallas kernels for 44%

profile of v3, /device:TPU:31, one launch (start us, length us, event | category | flops | bytes accessed | tf_op | source)
XLA Modules:
  0.0 77.6 jit_solution(7213743678299738329)
XLA Ops:
  0.0 1.1 %shard_map.73.refs_3_ = bf16[256,1024]{1,0:T(8,128)(2,1)S(1)} custom-call(bf16[128,1024]{1,0:T(8,128)(2,1)} %top_ref.1, bf16[128,1024]{1,0:T(8,128)(2,1)} %low_ref.1), custom_call_target="tpu_custom_call" | custom-call | tf_op jit(solution)/shard_map/pallas_call | solution.py:89
  2.1 1.3 %collective-permute-start = (bf16[256,1024]{1,0:T(8,128)(2,1)S(1)}, bf16[256,1024]{1,0:T(8,128)(2,1)S(1)}, u32[]{:S(2)}, u32[]{:S(2)}) collective-permute-start(bf16[256,1024]{1,0:T(8,128)(2,1)S(1)} %shard_map.73.refs_3_), channel_id=1, source_target_pairs={{0,4},{2,6},{4,8},{6,10},{8,12},{10,14},{1,5},{3,7},{5,9},{7,11},{... | collective-permute-start | bytes 1572872 | tf_op jit(solution)/shard_map/ppermute | solution.py:284
  3.3 0.8 reshape.12
  5.9 1.6 %copy-done.1 = bf16[128,8192]{1,0:T(8,128)(2,1)S(1)} copy-done((bf16[128,8192]{1,0:T(8,128)(2,1)S(1)}, bf16[128,8192]{1,0:T(8,128)(2,1)}, u32[]{:S(2)}) %copy-start.1) | copy-done | bytes 2097176
  7.5 6.9 %shard_map.74 = (f32[1,8192]{1,0:T(1,128)S(1)}, f32[1,8192]{1,0:T(1,128)S(1)}, f32[128,8192]{1,0:T(8,128)S(1)}) custom-call(s32[129]{0:T(256)S(1)} %pad_add_fusion.refs_0_, f32[192]{0:T(256)S(1)} %maximum_convert_fusion.refs_1_, bf16[128,8192]{1,0:T(8,128)(2,1)S(1)} %copy-done.1, bf16[256,1024]{1,0:T(8,128)(2,1)S(1)} %shard_map.73.refs_3_, ...), custom_call_target="tpu_custom_call" | custom-call | flops 1 | tf_op jit(solution)/shard_map/pallas_call | solution.py:223
  14.5 0.9 %collective-permute-done.1.refs_5_ = bf16[256,1024]{1,0:T(8,128)(2,1)S(1)} collective-permute-done((bf16[256,1024]{1,0:T(8,128)(2,1)S(1)}, bf16[256,1024]{1,0:T(8,128)(2,1)S(1)}, u32[]{:S(2)}, u32[]{:S(2)}) %collective-permute-start.1) | collective-permute-done | bytes 524320 | tf_op jit(solution)/shard_map/ppermute | solution.py:285
  15.3 1.8 %collective-permute-done.refs_3_ = bf16[256,1024]{1,0:T(8,128)(2,1)S(1)} collective-permute-done((bf16[256,1024]{1,0:T(8,128)(2,1)S(1)}, bf16[256,1024]{1,0:T(8,128)(2,1)S(1)}, u32[]{:S(2)}, u32[]{:S(2)}) %collective-permute-start) | collective-permute-done | bytes 524320 | tf_op jit(solution)/shard_map/ppermute | solution.py:284
  17.1 1.2 %collective-permute-start.6 = (bf16[256,1024]{1,0:T(8,128)(2,1)S(1)}, bf16[256,1024]{1,0:T(8,128)(2,1)S(1)}, u32[]{:S(2)}, u32[]{:S(2)}) collective-permute-start(bf16[256,1024]{1,0:T(8,128)(2,1)S(1)} %collective-permute-done.1.refs_5_), channel_id=1, source_target_pairs={{0,1},{1,0},{2,3},{3,2},{4,5},{5,4},{6,7},{7,6},{8,9},{9,8},{10,11... | collective-permute-start | bytes 1572872 | tf_op jit(solution)/shard_map/ppermute | solution.py:266
  18.3 1.2 %collective-permute-start.4 = (bf16[256,1024]{1,0:T(8,128)(2,1)S(1)}, bf16[256,1024]{1,0:T(8,128)(2,1)S(1)}, u32[]{:S(2)}, u32[]{:S(2)}) collective-permute-start(bf16[256,1024]{1,0:T(8,128)(2,1)S(1)} %collective-permute-done.refs_3_), channel_id=1, source_target_pairs={{0,2},{2,0},{4,6},{6,4},{8,10},{10,8},{12,14},{14,12},{1,3},{3,1},... | collective-permute-start | bytes 1572872 | tf_op jit(solution)/shard_map/ppermute | solution.py:285
  19.5 1.3 %collective-permute-start.3 = (bf16[256,1024]{1,0:T(8,128)(2,1)S(1)}, bf16[256,1024]{1,0:T(8,128)(2,1)S(1)}, u32[]{:S(2)}, u32[]{:S(2)}) collective-permute-start(bf16[256,1024]{1,0:T(8,128)(2,1)S(1)} %collective-permute-done.refs_3_), channel_id=1, source_target_pairs={{0,4},{2,6},{4,8},{6,10},{8,12},{10,14},{1,5},{3,7},{5,9},{7,11},{... | collective-permute-start | bytes 1572872 | tf_op jit(solution)/shard_map/ppermute | solution.py:284
  20.8 10.4 %shard_map.75 = (f32[1,8192]{1,0:T(1,128)S(1)}, f32[1,8192]{1,0:T(1,128)S(1)}, f32[128,8192]{1,0:T(8,128)S(1)}) custom-call(s32[129]{0:T(256)S(1)} %pad_add_fusion.refs_0_, f32[192]{0:T(256)S(1)} %maximum_convert_fusion.refs_1_, bf16[128,8192]{1,0:T(8,128)(2,1)S(1)} %copy-done.2, ...), custom_call_target="tpu_custom_call", output_to_operand_aliasing={{0}: (7, {}), {1}: (8, {}), {2}: (9, {})} | custom-call | flops 1 | tf_op jit(solution)/shard_map/pallas_call | solution.py:223
  31.3 2.8 %collective-permute-done.3.refs_3_ = bf16[256,1024]{1,0:T(8,128)(2,1)S(1)} collective-permute-done((bf16[256,1024]{1,0:T(8,128)(2,1)S(1)}, bf16[256,1024]{1,0:T(8,128)(2,1)S(1)}, u32[]{:S(2)}, u32[]{:S(2)}) %collective-permute-start.3) | collective-permute-done | bytes 524320 | tf_op jit(solution)/shard_map/ppermute | solution.py:284
  34.1 1.7 %collective-permute-start.10 = (bf16[256,1024]{1,0:T(8,128)(2,1)S(1)}, bf16[256,1024]{1,0:T(8,128)(2,1)S(1)}, u32[]{:S(2)}, u32[]{:S(2)}) collective-permute-start(bf16[256,1024]{1,0:T(8,128)(2,1)S(1)} %collective-permute-done.4.refs_5_), channel_id=1, source_target_pairs={{0,1},{1,0},{2,3},{3,2},{4,5},{5,4},{6,7},{7,6},{8,9},{9,8},{10,11... | collective-permute-start | bytes 1572872 | tf_op jit(solution)/shard_map/ppermute | solution.py:266
  36.0 1.3 %collective-permute-start.7 = (bf16[256,1024]{1,0:T(8,128)(2,1)S(1)}, bf16[256,1024]{1,0:T(8,128)(2,1)S(1)}, u32[]{:S(2)}, u32[]{:S(2)}) collective-permute-start(bf16[256,1024]{1,0:T(8,128)(2,1)S(1)} %collective-permute-done.3.refs_3_), channel_id=1, source_target_pairs={{0,4},{2,6},{4,8},{6,10},{8,12},{10,14},{1,5},{3,7},{5,9},{7,11},{... | collective-permute-start | bytes 1572872 | tf_op jit(solution)/shard_map/ppermute | solution.py:284
  38.0 9.6 %shard_map.76 = (f32[1,8192]{1,0:T(1,128)S(1)}, f32[1,8192]{1,0:T(1,128)S(1)}, f32[128,8192]{1,0:T(8,128)S(1)}) custom-call(s32[129]{0:T(256)S(1)} %pad_add_fusion.refs_0_, f32[192]{0:T(256)S(1)} %maximum_convert_fusion.refs_1_, bf16[128,8192]{1,0:T(8,128)(2,1)S(1)} %copy-done.2, ...), custom_call_target="tpu_custom_call", output_to_operand_aliasing={{0}: (7, {}), {1}: (8, {}), {2}: (9, {})} | custom-call | flops 1 | tf_op jit(solution)/shard_map/pallas_call | solution.py:223
  47.6 1.1 %collective-permute-done.8.refs_5_ = bf16[256,1024]{1,0:T(8,128)(2,1)S(1)} collective-permute-done((bf16[256,1024]{1,0:T(8,128)(2,1)S(1)}, bf16[256,1024]{1,0:T(8,128)(2,1)S(1)}, u32[]{:S(2)}, u32[]{:S(2)}) %collective-permute-start.8) | collective-permute-done | bytes 524320 | tf_op jit(solution)/shard_map/ppermute | solution.py:285
  48.7 1.8 %collective-permute-done.7.refs_3_ = bf16[256,1024]{1,0:T(8,128)(2,1)S(1)} collective-permute-done((bf16[256,1024]{1,0:T(8,128)(2,1)S(1)}, bf16[256,1024]{1,0:T(8,128)(2,1)S(1)}, u32[]{:S(2)}, u32[]{:S(2)}) %collective-permute-start.7) | collective-permute-done | bytes 524320 | tf_op jit(solution)/shard_map/ppermute | solution.py:284
  50.5 1.7 %collective-permute-start.13 = (bf16[256,1024]{1,0:T(8,128)(2,1)S(1)}, bf16[256,1024]{1,0:T(8,128)(2,1)S(1)}, u32[]{:S(2)}, u32[]{:S(2)}) collective-permute-start(bf16[256,1024]{1,0:T(8,128)(2,1)S(1)} %collective-permute-done.8.refs_5_), channel_id=1, source_target_pairs={{0,1},{1,0},{2,3},{3,2},{4,5},{5,4},{6,7},{7,6},{8,9},{9,8},{10,11... | collective-permute-start | bytes 1572872 | tf_op jit(solution)/shard_map/ppermute | solution.py:266
  52.2 1.2 %collective-permute-start.11 = (bf16[256,1024]{1,0:T(8,128)(2,1)S(1)}, bf16[256,1024]{1,0:T(8,128)(2,1)S(1)}, u32[]{:S(2)}, u32[]{:S(2)}) collective-permute-start(bf16[256,1024]{1,0:T(8,128)(2,1)S(1)} %collective-permute-done.7.refs_3_), channel_id=1, source_target_pairs={{0,2},{2,0},{4,6},{6,4},{8,10},{10,8},{12,14},{14,12},{1,3},{3,1},... | collective-permute-start | bytes 1572872 | tf_op jit(solution)/shard_map/ppermute | solution.py:285
  54.5 7.1 %shard_map.77 = (f32[1,8192]{1,0:T(1,128)S(1)}, f32[1,8192]{1,0:T(1,128)S(1)}, f32[128,8192]{1,0:T(8,128)S(1)}) custom-call(s32[129]{0:T(256)S(1)} %pad_add_fusion.refs_0_, f32[192]{0:T(256)S(1)} %maximum_convert_fusion.refs_1_, bf16[128,8192]{1,0:T(8,128)(2,1)S(1)} %copy-done.2, ...), custom_call_target="tpu_custom_call", output_to_operand_aliasing={{0}: (7, {}), {1}: (8, {}), {2}: (9, {})} | custom-call | flops 1 | tf_op jit(solution)/shard_map/pallas_call | solution.py:223
  61.6 3.6 %collective-permute-done.11.refs_3_ = bf16[256,1024]{1,0:T(8,128)(2,1)S(1)} collective-permute-done((bf16[256,1024]{1,0:T(8,128)(2,1)S(1)}, bf16[256,1024]{1,0:T(8,128)(2,1)S(1)}, u32[]{:S(2)}, u32[]{:S(2)}) %collective-permute-start.11) | collective-permute-done | bytes 524320 | tf_op jit(solution)/shard_map/ppermute | solution.py:285
  65.2 1.4 %collective-permute-start.14 = (bf16[256,1024]{1,0:T(8,128)(2,1)S(1)}, bf16[256,1024]{1,0:T(8,128)(2,1)S(1)}, u32[]{:S(2)}, u32[]{:S(2)}) collective-permute-start(bf16[256,1024]{1,0:T(8,128)(2,1)S(1)} %collective-permute-done.11.refs_3_), channel_id=1, source_target_pairs={{0,1},{1,0},{2,3},{3,2},{4,5},{5,4},{6,7},{7,6},{8,9},{9,8},{10,11... | collective-permute-start | bytes 1572872 | tf_op jit(solution)/shard_map/ppermute | solution.py:266
  66.5 1.5 %collective-permute-done.14.refs_4_ = bf16[256,1024]{1,0:T(8,128)(2,1)S(1)} collective-permute-done((bf16[256,1024]{1,0:T(8,128)(2,1)S(1)}, bf16[256,1024]{1,0:T(8,128)(2,1)S(1)}, u32[]{:S(2)}, u32[]{:S(2)}) %collective-permute-start.14) | collective-permute-done | bytes 524320 | tf_op jit(solution)/shard_map/ppermute | solution.py:266
  68.1 9.4 %shard_map.78 = (f32[1,8192]{1,0:T(1,128)S(1)}, f32[1,8192]{1,0:T(1,128)S(1)}, f32[128,8192]{1,0:T(8,128)S(1)}, bf16[128,8192]{1,0:T(8,128)(2,1)}) custom-call(s32[129]{0:T(256)S(1)} %pad_add_fusion.refs_0_, f32[192]{0:T(256)S(1)} %maximum_convert_fusion.refs_1_, ...), custom_call_target="tpu_custom_call", output_to_operand_aliasing={{0}: (5, {}), {1}: (6, {}), {2}: (7, {})} | custom-call | flops 1 | tf_op jit(solution)/shard_map/pallas_call | solution.py:223
  (25 shorter events, 4.9 us)
Async XLA Ops:
  0.0 5.7 %copy-start = (bf16[2,64]{1,0:T(2,128)(2,1)S(1)}, bf16[2,64]{1,0:T(2,128)(2,1)}, u32[]{:S(2)}) copy-start(bf16[2,64]{1,0:T(2,128)(2,1)} %param.10) | copy-start | bytes 772
  1.1 4.9 %collective-permute-start.2 = (bf16[256,1024]{1,0:T(8,128)(2,1)S(1)}, bf16[256,1024]{1,0:T(8,128)(2,1)S(1)}, u32[]{:S(2)}, u32[]{:S(2)}) collective-permute-start(bf16[256,1024]{1,0:T(8,128)(2,1)S(1)} %shard_map.73.refs_3_), channel_id=1, source_target_pairs={{0,1},{1,0},{2,3},{3,2},{4,5},{5,4},{6,7},{7,6},{8,9},{9,8},{10,11... | collective-permute-start | bytes 1572872 | tf_op jit(solution)/shard_map/ppermute | solution.py:266
  1.8 13.5 %collective-permute-start.1 = (bf16[256,1024]{1,0:T(8,128)(2,1)S(1)}, bf16[256,1024]{1,0:T(8,128)(2,1)S(1)}, u32[]{:S(2)}, u32[]{:S(2)}) collective-permute-start(bf16[256,1024]{1,0:T(8,128)(2,1)S(1)} %shard_map.73.refs_3_), channel_id=1, source_target_pairs={{0,2},{2,0},{4,6},{6,4},{8,10},{10,8},{12,14},{14,12},{1,3},{3,1},... | collective-permute-start | bytes 1572872 | tf_op jit(solution)/shard_map/ppermute | solution.py:285
  2.1 15.0 %collective-permute-start = (bf16[256,1024]{1,0:T(8,128)(2,1)S(1)}, bf16[256,1024]{1,0:T(8,128)(2,1)S(1)}, u32[]{:S(2)}, u32[]{:S(2)}) collective-permute-start(bf16[256,1024]{1,0:T(8,128)(2,1)S(1)} %shard_map.73.refs_3_), channel_id=1, source_target_pairs={{0,4},{2,6},{4,8},{6,10},{8,12},{10,14},{1,5},{3,7},{5,9},{7,11},{... | collective-permute-start | bytes 1572872 | tf_op jit(solution)/shard_map/ppermute | solution.py:284
  5.9 1.6 %copy-start.1 = (bf16[128,8192]{1,0:T(8,128)(2,1)S(1)}, bf16[128,8192]{1,0:T(8,128)(2,1)}, u32[]{:S(2)}) copy-start(bf16[128,8192]{1,0:T(8,128)(2,1)} %refs_2_.9) | copy-start | bytes 6291460
  7.5 13.3 %copy-start.2 = (bf16[128,8192]{1,0:T(8,128)(2,1)S(1)}, bf16[128,8192]{1,0:T(8,128)(2,1)}, u32[]{:S(2)}) copy-start(bf16[128,8192]{1,0:T(8,128)(2,1)} %refs_2_.9) | copy-start | bytes 6291460
  17.1 3.7 %collective-permute-start.6 = (bf16[256,1024]{1,0:T(8,128)(2,1)S(1)}, bf16[256,1024]{1,0:T(8,128)(2,1)S(1)}, u32[]{:S(2)}, u32[]{:S(2)}) collective-permute-start(bf16[256,1024]{1,0:T(8,128)(2,1)S(1)} %collective-permute-done.1.refs_5_), channel_id=1, source_target_pairs={{0,1},{1,0},{2,3},{3,2},{4,5},{5,4},{6,7},{7,6},{8,9},{9,8},{10,11... | collective-permute-start | bytes 1572872 | tf_op jit(solution)/shard_map/ppermute | solution.py:266
  18.3 2.5 %collective-permute-start.5 = (bf16[256,1024]{1,0:T(8,128)(2,1)S(1)}, bf16[256,1024]{1,0:T(8,128)(2,1)S(1)}, u32[]{:S(2)}, u32[]{:S(2)}) collective-permute-start(bf16[256,1024]{1,0:T(8,128)(2,1)S(1)} %collective-permute-done.refs_3_), channel_id=1, source_target_pairs={{0,1},{1,0},{2,3},{3,2},{4,5},{5,4},{6,7},{7,6},{8,9},{9,8},{10,11... | collective-permute-start | bytes 1572872 | tf_op jit(solution)/shard_map/ppermute | solution.py:266
  18.3 13.0 %collective-permute-start.4 = (bf16[256,1024]{1,0:T(8,128)(2,1)S(1)}, bf16[256,1024]{1,0:T(8,128)(2,1)S(1)}, u32[]{:S(2)}, u32[]{:S(2)}) collective-permute-start(bf16[256,1024]{1,0:T(8,128)(2,1)S(1)} %collective-permute-done.refs_3_), channel_id=1, source_target_pairs={{0,2},{2,0},{4,6},{6,4},{8,10},{10,8},{12,14},{14,12},{1,3},{3,1},... | collective-permute-start | bytes 1572872 | tf_op jit(solution)/shard_map/ppermute | solution.py:285
  19.5 14.5 %collective-permute-start.3 = (bf16[256,1024]{1,0:T(8,128)(2,1)S(1)}, bf16[256,1024]{1,0:T(8,128)(2,1)S(1)}, u32[]{:S(2)}, u32[]{:S(2)}) collective-permute-start(bf16[256,1024]{1,0:T(8,128)(2,1)S(1)} %collective-permute-done.refs_3_), channel_id=1, source_target_pairs={{0,4},{2,6},{4,8},{6,10},{8,12},{10,14},{1,5},{3,7},{5,9},{7,11},{... | collective-permute-start | bytes 1572872 | tf_op jit(solution)/shard_map/ppermute | solution.py:284
  34.1 3.2 %collective-permute-start.10 = (bf16[256,1024]{1,0:T(8,128)(2,1)S(1)}, bf16[256,1024]{1,0:T(8,128)(2,1)S(1)}, u32[]{:S(2)}, u32[]{:S(2)}) collective-permute-start(bf16[256,1024]{1,0:T(8,128)(2,1)S(1)} %collective-permute-done.4.refs_5_), channel_id=1, source_target_pairs={{0,1},{1,0},{2,3},{3,2},{4,5},{5,4},{6,7},{7,6},{8,9},{9,8},{10,11... | collective-permute-start | bytes 1572872 | tf_op jit(solution)/shard_map/ppermute | solution.py:266
  35.7 2.3 %collective-permute-start.9 = (bf16[256,1024]{1,0:T(8,128)(2,1)S(1)}, bf16[256,1024]{1,0:T(8,128)(2,1)S(1)}, u32[]{:S(2)}, u32[]{:S(2)}) collective-permute-start(bf16[256,1024]{1,0:T(8,128)(2,1)S(1)} %collective-permute-done.3.refs_3_), channel_id=1, source_target_pairs={{0,1},{1,0},{2,3},{3,2},{4,5},{5,4},{6,7},{7,6},{8,9},{9,8},{10,11... | collective-permute-start | bytes 1572872 | tf_op jit(solution)/shard_map/ppermute | solution.py:266
  35.7 13.0 %collective-permute-start.8 = (bf16[256,1024]{1,0:T(8,128)(2,1)S(1)}, bf16[256,1024]{1,0:T(8,128)(2,1)S(1)}, u32[]{:S(2)}, u32[]{:S(2)}) collective-permute-start(bf16[256,1024]{1,0:T(8,128)(2,1)S(1)} %collective-permute-done.3.refs_3_), channel_id=1, source_target_pairs={{0,2},{2,0},{4,6},{6,4},{8,10},{10,8},{12,14},{14,12},{1,3},{3,1},... | collective-permute-start | bytes 1572872 | tf_op jit(solution)/shard_map/ppermute | solution.py:285
  36.0 14.5 %collective-permute-start.7 = (bf16[256,1024]{1,0:T(8,128)(2,1)S(1)}, bf16[256,1024]{1,0:T(8,128)(2,1)S(1)}, u32[]{:S(2)}, u32[]{:S(2)}) collective-permute-start(bf16[256,1024]{1,0:T(8,128)(2,1)S(1)} %collective-permute-done.3.refs_3_), channel_id=1, source_target_pairs={{0,4},{2,6},{4,8},{6,10},{8,12},{10,14},{1,5},{3,7},{5,9},{7,11},{... | collective-permute-start | bytes 1572872 | tf_op jit(solution)/shard_map/ppermute | solution.py:284
  50.5 3.2 %collective-permute-start.13 = (bf16[256,1024]{1,0:T(8,128)(2,1)S(1)}, bf16[256,1024]{1,0:T(8,128)(2,1)S(1)}, u32[]{:S(2)}, u32[]{:S(2)}) collective-permute-start(bf16[256,1024]{1,0:T(8,128)(2,1)S(1)} %collective-permute-done.8.refs_5_), channel_id=1, source_target_pairs={{0,1},{1,0},{2,3},{3,2},{4,5},{5,4},{6,7},{7,6},{8,9},{9,8},{10,11... | collective-permute-start | bytes 1572872 | tf_op jit(solution)/shard_map/ppermute | solution.py:266
  52.2 2.3 %collective-permute-start.12 = (bf16[256,1024]{1,0:T(8,128)(2,1)S(1)}, bf16[256,1024]{1,0:T(8,128)(2,1)S(1)}, u32[]{:S(2)}, u32[]{:S(2)}) collective-permute-start(bf16[256,1024]{1,0:T(8,128)(2,1)S(1)} %collective-permute-done.7.refs_3_), channel_id=1, source_target_pairs={{0,1},{1,0},{2,3},{3,2},{4,5},{5,4},{6,7},{7,6},{8,9},{9,8},{10,11... | collective-permute-start | bytes 1572872 | tf_op jit(solution)/shard_map/ppermute | solution.py:266
  52.2 13.0 %collective-permute-start.11 = (bf16[256,1024]{1,0:T(8,128)(2,1)S(1)}, bf16[256,1024]{1,0:T(8,128)(2,1)S(1)}, u32[]{:S(2)}, u32[]{:S(2)}) collective-permute-start(bf16[256,1024]{1,0:T(8,128)(2,1)S(1)} %collective-permute-done.7.refs_3_), channel_id=1, source_target_pairs={{0,2},{2,0},{4,6},{6,4},{8,10},{10,8},{12,14},{14,12},{1,3},{3,1},... | collective-permute-start | bytes 1572872 | tf_op jit(solution)/shard_map/ppermute | solution.py:285
  65.2 2.9 %collective-permute-start.14 = (bf16[256,1024]{1,0:T(8,128)(2,1)S(1)}, bf16[256,1024]{1,0:T(8,128)(2,1)S(1)}, u32[]{:S(2)}, u32[]{:S(2)}) collective-permute-start(bf16[256,1024]{1,0:T(8,128)(2,1)S(1)} %collective-permute-done.11.refs_3_), channel_id=1, source_target_pairs={{0,1},{1,0},{2,3},{3,2},{4,5},{5,4},{6,7},{7,6},{8,9},{9,8},{10,11... | collective-permute-start | bytes 1572872 | tf_op jit(solution)/shard_map/ppermute | solution.py:266

commit v4 on v2

v4 whole, which is shorter than its diff:
```python
import functools

import jax
import jax.numpy as jnp
from jax import lax
from jax.experimental import pallas as pl
from jax.experimental.pallas import tpu as pltpu
from jax.sharding import PartitionSpec as P

DH = 128
FLOOR_SCORE = -1e30
LOG2E = 1.4426950408889634
NT = (((1,), (1,)), ((), ()))
F32 = jnp.float32
BF16 = jnp.bfloat16
VMEM_LIMIT = 16 * 2**20
ANYWHERE = pl.BlockSpec(memory_space=pl.ANY)
IN_VMEM = pl.BlockSpec(memory_space=pltpu.VMEM)
PARAMS = pltpu.CompilerParams(vmem_limit_bytes=VMEM_LIMIT)


def along_rows(combine, parts):
    rows = [part[at : at + 8] for part in parts for at in range(0, part.shape[0], 8)]
    lanes = rows[:4]
    for at, row in enumerate(rows[4:]):
        lanes[at % 4] = combine(lanes[at % 4], row)
    return functools.reduce(combine, lanes)


def attend(count, diagonal, block, per_group, scale_at, keys, values, query_ref, before, after, finish):
    abreast = 2 if count == 1 and per_group % 2 == 0 else 1

    def dots_of(head):
        queries = [query_ref[:, at * DH : (at + 1) * DH] for at in range(head, head + abreast)]
        return lax.dot_general(keys, jnp.concatenate(queries, axis=0), NT, preferred_element_type=F32)

    def weigh(head, dots):
        probs, shrinks, totals = [], [], []
        for at in range(abreast):
            parts = []
            for slot in range(count):
                part = dots[slot * block : (slot + 1) * block, at * block : (at + 1) * block]
                part = part * scale_at(slot, head + at)
                if diagonal and slot == 0:
                    key_at = lax.broadcasted_iota(jnp.int32, part.shape, 0)
                    query_at = lax.broadcasted_iota(jnp.int32, part.shape, 1)
                    part = jnp.where(key_at <= query_at, part, FLOOR_SCORE)
                parts.append(part)
            most = jnp.max(along_rows(jnp.maximum, parts), axis=0, keepdims=True)
            if before is not None:
                there = pl.ds(before[1] + (head + at) * block, block)
                old = before[0][0][:, there]
                most = jnp.maximum(most, old)
                shrinks.append(jnp.exp2(old - most))
            weights = [jnp.exp2(part - most) for part in parts]
            total = jnp.sum(along_rows(jnp.add, weights), axis=0, keepdims=True)
            if before is not None:
                total = total + before[0][1][:, there] * shrinks[-1]
            if after is not None:
                here = pl.ds(after[1] + (head + at) * block, block)
                after[0][0][:, here] = most
                after[0][1][:, here] = total
            totals.append(total)
            probs.append(jnp.concatenate([part.astype(BF16) for part in weights], axis=0))
        shrink = None if before is None else jnp.concatenate(shrinks, axis=1)
        return jnp.concatenate(probs, axis=1), shrink, jnp.concatenate(totals, axis=1)

    def gather(head, probs, shrink, total):
        add = jnp.dot(values, probs, preferred_element_type=F32)
        if before is not None:
            add = before[0][2][:, pl.ds(before[1] + head * block, abreast * block)] * shrink + add
        if finish is None:
            after[0][2][:, pl.ds(after[1] + head * block, abreast * block)] = add
            return
        for at in range(abreast):
            part = slice(at * block, (at + 1) * block)
            finish(head + at, add[:, part], total[:, part])

    dots = dots_of(0)
    pending = None
    for head in range(0, per_group, abreast):
        ahead = dots_of(head + abreast) if head + abreast < per_group else None
        if pending is not None:
            gather(*pending)
        pending = (head,) + weigh(head, dots)
        dots = ahead
    gather(*pending)


def run_copies(copies):
    for copy in copies:
        copy.start()
    for copy in copies:
        copy.wait()


def deal_kernel(cores, key_ref, value_ref, *rest):
    shares, sems = rest[:-1], rest[-1]
    rows, columns = key_ref.shape[0], key_ref.shape[1] // cores
    core = lax.axis_index("ulysses")
    copies = []
    for step, share in enumerate(shares):
        part = pl.ds(pl.multiple_of(lax.rem(core + cores - step, cores) * columns, columns), columns)
        copies.append(pltpu.make_async_copy(key_ref.at[:, part], share.at[0:rows], sems.at[step, 0]))
        copies.append(pltpu.make_async_copy(value_ref.at[:, part], share.at[rows : 2 * rows], sems.at[step, 1]))
    run_copies(copies)


def deal(cores, key_int, values):
    rows, columns = key_int.shape
    pinned = [pltpu.with_memory_space_constraint(array, pltpu.HBM) for array in (key_int, values)]
    return pl.pallas_call(
        functools.partial(deal_kernel, cores),
        in_specs=[ANYWHERE] * 2,
        out_specs=[IN_VMEM] * cores,
        out_shape=[jax.ShapeDtypeStruct((2 * rows, columns // cores), key_int.dtype)] * cores,
        scratch_shapes=[pltpu.SemaphoreType.DMA((cores, 2))],
        compiler_params=PARAMS,
    )(*pinned)


def stack_kernel(*refs):
    parts, out_ref, sems = refs[:-2], refs[-2], refs[-1]
    rows = parts[0].shape[0]
    run_copies(
        [
            pltpu.make_async_copy(part, out_ref.at[at * rows : (at + 1) * rows], sems.at[at])
            for at, part in enumerate(parts)
        ]
    )


def stack(parts):
    rows, columns = parts[0].shape
    return pl.pallas_call(
        stack_kernel,
        in_specs=[IN_VMEM] * len(parts),
        out_specs=IN_VMEM,
        out_shape=jax.ShapeDtypeStruct((len(parts) * rows, columns), parts[0].dtype),
        scratch_shapes=[pltpu.SemaphoreType.DMA((len(parts),))],
        compiler_params=PARAMS,
    )(*parts)


def join_kernel(cores, *refs):
    parts, out_ref, sems = refs[1:-2], refs[-2], refs[-1]
    columns = parts[0].shape[1]
    core = lax.axis_index("ulysses")
    copies = []
    for at, part in enumerate(parts):
        place = pl.multiple_of(lax.rem(core + cores - at - 1, cores) * columns, columns)
        copies.append(pltpu.make_async_copy(part, out_ref.at[:, pl.ds(place, columns)], sems.at[at]))
    run_copies(copies)


def join(cores, out, parts):
    return pl.pallas_call(
        functools.partial(join_kernel, cores),
        in_specs=[ANYWHERE] + [IN_VMEM] * len(parts),
        out_specs=ANYWHERE,
        out_shape=jax.ShapeDtypeStruct(out.shape, out.dtype),
        scratch_shapes=[pltpu.SemaphoreType.DMA((len(parts),))],
        input_output_aliases={0: 0},
        compiler_params=PARAMS,
    )(out, *parts)


def bits(table_ref, row, low):
    word = jnp.int32(0)
    for index in range(table_ref.shape[1]):
        entry = table_ref[row, index] - low
        inside = (entry >= 0) & (entry < 32)
        word = word | jnp.where(inside, lax.shift_left(jnp.int32(1), jnp.where(inside, entry, 0)), 0)
    return word


def bit_at(word, place):
    return lax.shift_right_logical(word, place) & 1


def chunk_kernel(sizes, units, first, last, turns, *refs):
    cores, pair, groups, per_group, block, blocks = sizes
    table_hbm, scale_hbm, *query_hbm = refs[: 2 + cores]
    unit_refs = refs[2 + cores : 2 + cores + len(units)]
    rest = refs[2 + cores + len(units) :]
    old = None
    if not first:
        old, rest = rest[:3], rest[3:]
    if last:
        out_hbm, rest = rest[: len(turns)], rest[len(turns) :]
    else:
        new, rest = rest[:3], rest[3:]
    query_ref, tile_ref, values_ref, slot_ref, count_ref, mask_ref, table_ref, scale_ref, sems, table_sems = rest[:10]
    if last:
        out_ref, out_sems = rest[10:]
    groups_here = groups // cores
    width = per_group * block
    wide = per_group * DH
    words = -(-blocks // 32)
    slots = len(units) * cores
    core = lax.axis_index("ulysses")
    span = lax.axis_index("blk")
    line, side = lax.div(span, pair), lax.rem(span, pair)
    spans = []
    for back, other in units:
        at_line = line - back
        spans.append(jnp.where(at_line >= 0, at_line * pair + (pair - 1 - side if other else side), -1))
    steps = len(turns) * groups_here

    def turn_at(step):
        return turns[0] - lax.div(step, groups_here), lax.rem(step, groups_here)

    def row_of(turn):
        return lax.rem(core + turn, cores)

    def by_turn(step, act):
        turn, group = turn_at(step)
        for index, at in enumerate(turns):

            @pl.when(turn == at)
            def _(index=index, at=at):
                act(index, at, group)

    def query_copy(at, group, buffer):
        place = (core * groups_here + group) * wide
        source = query_hbm[at].at[:, pl.ds(pl.multiple_of(place, wide), wide)]
        return pltpu.make_async_copy(source, query_ref.at[buffer], sems.at[0, buffer])

    def out_copy(index, at, group, buffer):
        place = (core * groups_here + group if at == 0 else group) * wide
        target = out_hbm[index].at[:, pl.ds(pl.multiple_of(place, wide), wide)]
        return pltpu.make_async_copy(out_ref.at[buffer], target, out_sems.at[buffer])

    def tile_copy(unit, part, group, buffer, at):
        column = pl.ds(pl.multiple_of(group * DH, DH), DH)
        rows = pl.ds(pl.multiple_of(part * (2 * block), 2 * block), 2 * block)
        return pltpu.make_async_copy(unit_refs[unit].at[rows, column], tile_ref.at[buffer, at], sems.at[1, buffer])

    by_turn(0, lambda index, at, group: query_copy(at, group, 0).start())
    run_copies(
        [
            pltpu.make_async_copy(table_hbm, table_ref, table_sems.at[0]),
            pltpu.make_async_copy(scale_hbm, scale_ref, table_sems.at[1]),
        ]
    )

    for group in range(groups_here):
        mask_ref[group, 0] = bits(table_ref, groups + core * groups_here + group, 0)
        for word in range(words):
            mask_ref[group, 1 + word] = bits(table_ref, core * groups_here + group, word * 32)

    def fetch(step, buffer):
        turn, group = turn_at(step)
        here = span * cores + row_of(turn)
        slash_bits = mask_ref[group, 0]
        count = jnp.int32(0)
        for unit in range(len(units)):
            for ahead in range(cores):
                part = lax.rem(turn + ahead, cores)
                place = spans[unit] * cores + lax.rem(core + part, cores)
                back = here - place
                valid = (spans[unit] >= 0) & (back >= 0)
                at = jnp.where(valid, place, 0)
                vertical_bits = mask_ref[group, 1 + lax.shift_right_logical(at, 5)]
                near = jnp.where(back < 32, bit_at(slash_bits, back & 31), 0)
                live = jnp.where(valid, near | bit_at(vertical_bits, at & 31), 0)

                @pl.when(live > 0)
                def _(unit=unit, part=part, count=count, place=place):
                    tile_copy(unit, part, group, buffer, count).start()
                    slot_ref[buffer, count] = place

                count = count + live
        count_ref[buffer] = count

    fetch(0, 0)

    @pl.loop(0, steps)
    def _(step):
        buffer = lax.rem(step, 2)

        @pl.when(step + 1 < steps)
        def _():
            by_turn(step + 1, lambda index, at, group: query_copy(at, group, 1 - buffer).start())
            fetch(step + 1, 1 - buffer)

        turn, group = turn_at(step)
        query_copy(turns[0], 0, buffer).wait()
        count = count_ref[buffer]
        for at in range(slots):

            @pl.when(at < count)
            def _(at=at):
                tile_copy(0, 0, 0, buffer, at).wait()

        own_group = core * groups_here + group
        head_base = own_group * per_group
        scale_row = row_of(turn)

        def scale_at(slot, head):
            return scale_ref[scale_row, head_base + head] * scale_ref[cores + slot_ref[buffer, slot], own_group] * LOG2E

        if last:

            @pl.when(step >= 2)
            def _():
                out_copy(0, turns[0], 0, buffer).wait()

        def finish(head, total_values, total):
            done = total_values * (1.0 / total)
            out_ref[buffer, :, head * DH : (head + 1) * DH] = done.T.astype(BF16)

        base = pl.multiple_of((turn * groups_here + group) * width, width)
        for many in range(1, slots + 1):

            @pl.when(count == many)
            def _(many=many):
                for at in range(many):
                    values_ref[:, at * block : (at + 1) * block] = tile_ref[buffer, at, block : 2 * block, :].T
                attend(
                    many,
                    first,
                    block,
                    per_group,
                    scale_at,
                    jnp.concatenate([tile_ref[buffer, at, 0:block, :] for at in range(many)], axis=0),
                    values_ref[:, 0 : many * block],
                    query_ref.at[buffer],
                    None if first else (old, base),
                    None if last else (new, base),
                    finish if last else None,
                )

        if last:
            if not first:

                @pl.when(count == 0)
                def _():
                    for head in range(per_group):
                        at = pl.ds(base + head * block, block)
                        finish(head, old[2][:, at], old[1][:, at])

            by_turn(step, lambda index, at, group: out_copy(index, at, group, buffer).start())

    if last:
        for step in range(max(0, steps - 2), steps):
            out_copy(0, turns[0], 0, step % 2).wait()


def attend_chunk(sizes, table, scales, queries, units, arrays, state, turns, last):
    cores, pair, groups, per_group, block, blocks = sizes
    first = state is None
    width = per_group * block
    slots = len(units) * cores
    kernel = functools.partial(chunk_kernel, sizes, units, first, last, turns)
    places = cores * (groups // cores)
    state_shape = [
        jax.ShapeDtypeStruct((1, places * width), F32),
        jax.ShapeDtypeStruct((1, places * width), F32),
        jax.ShapeDtypeStruct((DH, places * width), F32),
    ]
    own, others = queries[0].shape, (block, queries[0].shape[1] // cores)
    out_shape = [jax.ShapeDtypeStruct(own if turn == 0 else others, BF16) for turn in turns]
    scratch = [
        pltpu.VMEM((2, block, per_group * DH), BF16),
        pltpu.VMEM((2, slots, 2 * block, DH), BF16),
        pltpu.VMEM((DH, slots * block), BF16),
        pltpu.SMEM((2, slots), jnp.int32),
        pltpu.SMEM((2,), jnp.int32),
        pltpu.SMEM((groups // cores, 1 + -(-blocks // 32)), jnp.int32),
        pltpu.SMEM(table.shape, jnp.int32),
        pltpu.SMEM(scales.shape, F32),
        pltpu.SemaphoreType.DMA((2, 2)),
        pltpu.SemaphoreType.DMA((2,)),
    ]
    if last:
        scratch += [
            pltpu.VMEM((2, block, per_group * DH), BF16),
            pltpu.SemaphoreType.DMA((2,)),
        ]
    base = 2 + cores + len(units)
    return pl.pallas_call(
        kernel,
        in_specs=[ANYWHERE] * (2 + cores + len(units)) + ([] if first else [IN_VMEM] * 3),
        out_specs=[ANYWHERE] * len(turns) if last else [IN_VMEM] * 3,
        out_shape=out_shape if last else state_shape,
        scratch_shapes=scratch,
        input_output_aliases={} if first or last else {base + i: i for i in range(3)},
        compiler_params=PARAMS,
        cost_estimate=pl.CostEstimate(flops=1, bytes_accessed=0, transcendentals=0),
    )(table, scales, *queries, *arrays, *(() if first else state))


def local(spans, cores, query_int, key_int, values, query_scale, key_scale, verticals, slashes):
    block = query_int.shape[0]
    groups, blocks = verticals.shape[0], key_scale.shape[0]
    per_group = query_int.shape[1] // DH // groups
    columns = query_int.shape[1] // cores
    pair = 2 if spans % 2 == 0 else 1
    lines = spans // pair
    core = lax.axis_index("ulysses")
    sizes = (cores, pair, groups, per_group, block, blocks)

    turned = [[(c, (c - step) % cores) for c in range(cores)] for step in range(cores)]
    back = [[(c, (c + step) % cores) for c in range(cores)] for step in range(cores)]
    shares = deal(cores, key_int, values)
    own = stack(
        [shares[0]] + [lax.ppermute(shares[step], "ulysses", turned[step]) for step in range(1, cores)]
    )
    waiting, _ = lax.optimization_barrier((query_int, own))
    queries = [query_int] + [lax.ppermute(waiting, "ulysses", turned[step]) for step in range(1, cores)]
    table = jnp.concatenate([verticals, slashes], axis=0)
    key_scales = jnp.pad(key_scale, ((0, 0), (0, query_scale.shape[1] - groups)))
    scales = jnp.concatenate([query_scale, key_scales], axis=0).astype(F32)

    climb = [(s, s + pair) for s in range(spans - pair)]
    swap = [(s, s ^ 1) for s in range(spans)]
    turns = tuple(range(cores - 1, -1, -1))
    climbed, crossed, state = own, None, None
    steps = lines + (pair == 2)
    for step in range(steps):
        last = step + 1 == steps
        sent, arrived = climbed, crossed
        climbed = lax.ppermute(sent, "blk", climb) if step + 1 < lines else None
        crossed = lax.ppermute(sent, "blk", swap) if pair == 2 and sent is not None else None
        units, arrays = [], []
        if sent is not None:
            units.append((step, False))
            arrays.append(sent)
        if arrived is not None:
            units.append((step - 1, True))
            arrays.append(arrived)
        run = functools.partial(attend_chunk, sizes, table, scales, queries, tuple(units), arrays, state)
        if not last:
            state = run(turns, False)
            climbed, crossed, state = lax.optimization_barrier((climbed, crossed, state))
    if cores == 1:
        return run(turns, True)[0]
    others = run(turns[:-1], True)
    out = run(turns[-1:], True)[0]
    arrived = [
        lax.ppermute(one, "ulysses", back[turn]) for turn, one in sorted(zip(turns[:-1], others), key=lambda x: x[0])
    ]
    return join(cores, out, arrived)


def solution(mesh):
    rows = P(("group", "blk", "ulysses"), None)
    in_specs = (rows, rows, rows, P(("group", "blk"), None), P("group", None), P("group", None), P("group", None))
    run = functools.partial(local, mesh.shape["blk"], mesh.shape["ulysses"])
    return jax.shard_map(run, mesh=mesh, in_specs=in_specs, out_specs=rows, check_vma=False)
```

time: 90.8 us -> 72.2 us (0.80)
  local copies, waits for them, and re-layouts: 15.2 us -> 3.73 us
  other arithmetic: 4.61 us -> 0.66 us
  Pallas kernels: 47.6 us -> 45.5 us
  waiting for transfers between devices: 10.3 us -> 9.21 us
    unnamed x14 -> x6, local copies, waits for them, and re-layouts: 9.95 us -> 3.04 us
    gather x5 -> x0, local copies, waits for them, and re-layouts: 2.81 us -> none  [table(): key_scale[jnp.minimum(places, key_scale.shape[0] - 1)].astype(F32)]
    reduce_or x2 -> x0, other arithmetic: 2.22 us -> none  [table(): jnp.any(places[:, None, None] == here - slashes[None], axis=2)]
    pallas_call x5 -> x9, Pallas kernels: 47.6 us -> 45.5 us  [the longest x6 43.3 us: attend_chunk(): pl.pallas_call(kernel, in_specs=[ANYWHERE] * (2 + cores + len(units)) + (...]
    ppermute x8 -> x3, waiting for transfers between devices: 3.09 us -> 1.17 us  [the longest x1 1.16 us: local(): lax.ppermute(shares[step], 'ulysses', turned[step])]
    ppermute x3, waiting for transfers between devices: 3.74 us -> 4.92 us  [local(): climbed = lax.ppermute(sent, 'blk', climb) if step + 1 < lines else None]
    ppermute x8 -> x3, starting transfers between devices: 4.69 us -> 5.68 us  [the longest x1 4.5 us: local(): lax.ppermute(one, 'ulysses', back[turn])]
    concatenate x1, local copies, waits for them, and re-layouts: 1.67 us -> 0.69 us  [local(): table = jnp.concatenate([verticals, slashes], axis=0)]
  transfers between devices with their start and end apart: 15 -> 10, of which waited for: 7 -> 7; matrix products, arithmetic and copies ran while one was open for 10% -> 4% of each run, Pallas kernels for 42% -> 54%
where the time goes in v4:
time: 72.2 us; the launch traced here: 71.8 us
  Pallas kernels  45.5 us (63%)
  starting transfers between devices  12.5 us (17%)
  waiting for transfers between devices  9.21 us (13%)
  local copies, waits for them, and re-layouts  3.73 us (5%)
    pallas_call x6, Pallas kernels, attend_chunk(): pl.pallas_call(kernel, in_specs=[ANYWHERE] * (2 + cores + len(units)) + (...  43.3 us
    ppermute x3, waiting for transfers between devices, local(): climbed = lax.ppermute(sent, 'blk', climb) if step + 1 < lines else None  4.92 us
    ppermute x1, starting transfers between devices, local(): lax.ppermute(one, 'ulysses', back[turn])  4.5 us
    ppermute x3, starting transfers between devices, local(): climbed = lax.ppermute(sent, 'blk', climb) if step + 1 < lines else None  3.84 us
    ppermute x4, waiting for transfers between devices, local(): lax.ppermute(sent, 'blk', swap)  3.13 us
    unnamed x6, local copies, waits for them, and re-layouts  3.04 us
    ppermute x4, starting transfers between devices, local(): lax.ppermute(sent, 'blk', swap)  2.93 us
  transfers between devices with their start and end apart: 10, of which 7 were waited for; matrix products, arithmetic and copies ran while one was open for 4% of the time, Pallas kernels for 54%

profile of v4, /device:TPU:31, one launch (start us, length us, event | category | flops | bytes accessed | tf_op | source)
XLA Modules:
  0.0 71.8 jit_solution(11647677708214221133)
XLA Ops:
  0.0 1.1 %shard_map.73 = (bf16[256,512]{1,0:T(8,128)(2,1)S(1)}, bf16[256,512]{1,0:T(8,128)(2,1)S(1)}) custom-call(bf16[128,1024]{1,0:T(8,128)(2,1)} %key_ref.1, bf16[128,1024]{1,0:T(8,128)(2,1)} %value_ref.1), custom_call_target="tpu_custom_call" | custom-call | tf_op jit(solution)/shard_map/pallas_call | solution.py:112
  1.1 0.7 %collective-permute-start = (bf16[256,512]{1,0:T(8,128)(2,1)S(1)}, bf16[256,512]{1,0:T(8,128)(2,1)S(1)}, u32[]{:S(2)}, u32[]{:S(2)}) collective-permute-start(bf16[256,512]{1,0:T(8,128)(2,1)S(1)} %get-tuple-element.40), channel_id=1, source_target_pairs={{0,1},{1,0},{2,3},{3,2},{4,5},{5,4},{6,7},{7,6},{8,9},{9,8},{10,11... | collective-permute-start | bytes 786440 | tf_op jit(solution)/shard_map/ppermute | solution.py:408
  1.9 1.2 %collective-permute-done.refs_1_ = bf16[256,512]{1,0:T(8,128)(2,1)S(1)} collective-permute-done((bf16[256,512]{1,0:T(8,128)(2,1)S(1)}, bf16[256,512]{1,0:T(8,128)(2,1)S(1)}, u32[]{:S(2)}, u32[]{:S(2)}) %collective-permute-start) | collective-permute-done | bytes 262176 | tf_op jit(solution)/shard_map/ppermute | solution.py:408
  3.8 1.3 %collective-permute-start.2 = (bf16[512,512]{1,0:T(8,128)(2,1)S(1)}, bf16[512,512]{1,0:T(8,128)(2,1)S(1)}, u32[]{:S(2)}, u32[]{:S(2)}) collective-permute-start(bf16[512,512]{1,0:T(8,128)(2,1)S(1)} %shard_map.74.refs_4_), channel_id=1, source_target_pairs={{0,4},{2,6},{4,8},{6,10},{8,12},{10,14},{1,5},{3,7},{5,9},{7,11},{... | collective-permute-start | bytes 1572872 | tf_op jit(solution)/shard_map/ppermute | solution.py:424
  5.1 0.8 %copy.18 = bf16[16,8]{1,0:T(8,128)(2,1)S(1)} copy(bf16[16,8]{0,1:T(8,128)(2,1)} %param.11) | data formatting | bytes 512 | tf_op args[4]
  5.8 0.7 constant_dynamic-update-slice_fusion.1
  7.9 1.6 %copy-done = bf16[128,8192]{1,0:T(8,128)(2,1)S(1)} copy-done((bf16[128,8192]{1,0:T(8,128)(2,1)S(1)}, bf16[128,8192]{1,0:T(8,128)(2,1)}, u32[]{:S(2)}) %copy-start) | copy-done | bytes 2097176
  9.5 6.6 %shard_map.75 = (f32[1,8192]{1,0:T(1,128)S(1)}, f32[1,8192]{1,0:T(1,128)S(1)}, f32[128,8192]{1,0:T(8,128)S(1)}) custom-call(s32[16,8]{1,0:T(8,128)S(1)} %constant_dynamic-update-slice_fusion.refs_0_, f32[18,64]{1,0:T(8,128)S(1)} %fusion.2.refs_1_, bf16[128,8192]{1,0:T(8,128)(2,1)S(1)} %copy-done, bf16[128,8192]{1,0:T(8,128)(2,1)S(1)} %collective-permute-done.1.refs_3_, ...), custom_call_target="tpu_custom_call" | custom-call | flops 1 | tf_op jit(solution)/shard_map/pallas_call | solution.py:382
  16.0 1.0 %collective-permute-done.3.refs_5_ = bf16[512,512]{1,0:T(8,128)(2,1)} collective-permute-done((bf16[512,512]{1,0:T(8,128)(2,1)S(1)}, bf16[512,512]{1,0:T(8,128)(2,1)}, u32[]{:S(2)}, u32[]{:S(2)}) %collective-permute-start.3) | collective-permute-done | bytes 524320 | tf_op jit(solution)/shard_map/ppermute | solution.py:425
  17.0 1.7 %collective-permute-done.2.refs_4_ = bf16[512,512]{1,0:T(8,128)(2,1)S(1)} collective-permute-done((bf16[512,512]{1,0:T(8,128)(2,1)S(1)}, bf16[512,512]{1,0:T(8,128)(2,1)S(1)}, u32[]{:S(2)}, u32[]{:S(2)}) %collective-permute-start.2) | collective-permute-done | bytes 524320 | tf_op jit(solution)/shard_map/ppermute | solution.py:424
  18.7 1.2 %collective-permute-start.5 = (bf16[512,512]{1,0:T(8,128)(2,1)S(1)}, bf16[512,512]{1,0:T(8,128)(2,1)S(1)}, u32[]{:S(2)}, u32[]{:S(2)}) collective-permute-start(bf16[512,512]{1,0:T(8,128)(2,1)S(1)} %collective-permute-done.2.refs_4_), channel_id=1, source_target_pairs={{0,2},{2,0},{4,6},{6,4},{8,10},{10,8},{12,14},{14,12},{1,3},{3,1},... | collective-permute-start | bytes 1572872 | tf_op jit(solution)/shard_map/ppermute | solution.py:425
  20.0 1.3 %collective-permute-start.4 = (bf16[512,512]{1,0:T(8,128)(2,1)S(1)}, bf16[512,512]{1,0:T(8,128)(2,1)S(1)}, u32[]{:S(2)}, u32[]{:S(2)}) collective-permute-start(bf16[512,512]{1,0:T(8,128)(2,1)S(1)} %collective-permute-done.2.refs_4_), channel_id=1, source_target_pairs={{0,4},{2,6},{4,8},{6,10},{8,12},{10,14},{1,5},{3,7},{5,9},{7,11},{... | collective-permute-start | bytes 1572872 | tf_op jit(solution)/shard_map/ppermute | solution.py:424
  21.3 11.0 %shard_map.76 = (f32[1,8192]{1,0:T(1,128)S(1)}, f32[1,8192]{1,0:T(1,128)S(1)}, f32[128,8192]{1,0:T(8,128)S(1)}) custom-call(s32[16,8]{1,0:T(8,128)S(1)} %constant_dynamic-update-slice_fusion.refs_0_, f32[18,64]{1,0:T(8,128)S(1)} %fusion.2.refs_1_, bf16[128,8192]{1,0:T(8,128)(2,1)S(1)} %copy-done.1, ...), custom_call_target="tpu_custom_call", output_to_operand_aliasing={{0}: (6, {}), {1}: (7, {}), {2}: (8, {})} | custom-call | flops 1 | tf_op jit(solution)/shard_map/pallas_call | solution.py:382
  32.3 1.4 %collective-permute-done.4.refs_4_ = bf16[512,512]{1,0:T(8,128)(2,1)S(1)} collective-permute-done((bf16[512,512]{1,0:T(8,128)(2,1)S(1)}, bf16[512,512]{1,0:T(8,128)(2,1)S(1)}, u32[]{:S(2)}, u32[]{:S(2)}) %collective-permute-start.4) | collective-permute-done | bytes 524320 | tf_op jit(solution)/shard_map/ppermute | solution.py:424
  33.9 1.3 %collective-permute-start.6 = (bf16[512,512]{1,0:T(8,128)(2,1)S(1)}, bf16[512,512]{1,0:T(8,128)(2,1)S(1)}, u32[]{:S(2)}, u32[]{:S(2)}) collective-permute-start(bf16[512,512]{1,0:T(8,128)(2,1)S(1)} %collective-permute-done.4.refs_4_), channel_id=1, source_target_pairs={{0,4},{2,6},{4,8},{6,10},{8,12},{10,14},{1,5},{3,7},{5,9},{7,11},{... | collective-permute-start | bytes 1572872 | tf_op jit(solution)/shard_map/ppermute | solution.py:424
  35.2 9.1 %shard_map.77 = (f32[1,8192]{1,0:T(1,128)S(1)}, f32[1,8192]{1,0:T(1,128)S(1)}, f32[128,8192]{1,0:T(8,128)S(1)}) custom-call(s32[16,8]{1,0:T(8,128)S(1)} %constant_dynamic-update-slice_fusion.refs_0_, f32[18,64]{1,0:T(8,128)S(1)} %fusion.2.refs_1_, bf16[128,8192]{1,0:T(8,128)(2,1)S(1)} %copy-done.1, ...), custom_call_target="tpu_custom_call", output_to_operand_aliasing={{0}: (6, {}), {1}: (7, {}), {2}: (8, {})} | custom-call | flops 1 | tf_op jit(solution)/shard_map/pallas_call | solution.py:382
  44.6 1.8 %collective-permute-done.6.refs_4_ = bf16[512,512]{1,0:T(8,128)(2,1)S(1)} collective-permute-done((bf16[512,512]{1,0:T(8,128)(2,1)S(1)}, bf16[512,512]{1,0:T(8,128)(2,1)S(1)}, u32[]{:S(2)}, u32[]{:S(2)}) %collective-permute-start.6) | collective-permute-done | bytes 524320 | tf_op jit(solution)/shard_map/ppermute | solution.py:424
  46.5 1.2 %collective-permute-start.8 = (bf16[512,512]{1,0:T(8,128)(2,1)S(1)}, bf16[512,512]{1,0:T(8,128)(2,1)S(1)}, u32[]{:S(2)}, u32[]{:S(2)}) collective-permute-start(bf16[512,512]{1,0:T(8,128)(2,1)S(1)} %collective-permute-done.6.refs_4_), channel_id=1, source_target_pairs={{0,2},{2,0},{4,6},{6,4},{8,10},{10,8},{12,14},{14,12},{1,3},{3,1},... | collective-permute-start | bytes 1572872 | tf_op jit(solution)/shard_map/ppermute | solution.py:425
  47.7 6.7 %shard_map.78 = (f32[1,8192]{1,0:T(1,128)S(1)}, f32[1,8192]{1,0:T(1,128)S(1)}, f32[128,8192]{1,0:T(8,128)S(1)}) custom-call(s32[16,8]{1,0:T(8,128)S(1)} %constant_dynamic-update-slice_fusion.refs_0_, f32[18,64]{1,0:T(8,128)S(1)} %fusion.2.refs_1_, bf16[128,8192]{1,0:T(8,128)(2,1)S(1)} %copy-done.1, ...), custom_call_target="tpu_custom_call", output_to_operand_aliasing={{0}: (6, {}), {1}: (7, {}), {2}: (8, {})} | custom-call | flops 1 | tf_op jit(solution)/shard_map/pallas_call | solution.py:382
  54.4 1.8 %collective-permute-done.8.refs_4_ = bf16[512,512]{1,0:T(8,128)(2,1)S(1)} collective-permute-done((bf16[512,512]{1,0:T(8,128)(2,1)S(1)}, bf16[512,512]{1,0:T(8,128)(2,1)S(1)}, u32[]{:S(2)}, u32[]{:S(2)}) %collective-permute-start.8) | collective-permute-done | bytes 524320 | tf_op jit(solution)/shard_map/ppermute | solution.py:425
  56.2 4.7 %shard_map.80 = bf16[128,4096]{1,0:T(8,128)(2,1)S(1)} custom-call(s32[16,8]{1,0:T(8,128)S(1)} %constant_dynamic-update-slice_fusion.refs_0_, f32[18,64]{1,0:T(8,128)S(1)} %fusion.2.refs_1_, bf16[128,8192]{1,0:T(8,128)(2,1)S(1)} %copy-done.1, bf16[128,8192]{1,0:T(8,128)(2,1)S(1)} %collective-permute-done.1.refs_3_, ...), custom_call_target="tpu_custom_call" | custom-call | flops 1 | tf_op jit(solution)/shard_map/pallas_call | solution.py:382
  61.0 4.5 %collective-permute-start.9 = (bf16[128,4096]{1,0:T(8,128)(2,1)S(1)}, bf16[128,4096]{1,0:T(8,128)(2,1)S(1)}, u32[]{:S(2)}, u32[]{:S(2)}) collective-permute-start(bf16[128,4096]{1,0:T(8,128)(2,1)S(1)} %shard_map.80), channel_id=1, source_target_pairs={{0,1},{1,0},{2,3},{3,2},{4,5},{5,4},{6,7},{7,6},{8,9},{9,8},{10,11... | collective-permute-start | bytes 3145736 | tf_op jit(solution)/shard_map/ppermute | solution.py:442
  65.5 5.2 %shard_map.79.refs_0_ = bf16[128,8192]{1,0:T(8,128)(2,1)} custom-call(s32[16,8]{1,0:T(8,128)S(1)} %constant_dynamic-update-slice_fusion.refs_0_, f32[18,64]{1,0:T(8,128)S(1)} %fusion.2.refs_1_, bf16[128,8192]{1,0:T(8,128)(2,1)S(1)} %copy-done.1, bf16[128,8192]{1,0:T(8,128)(2,1)S(1)} %collective-permute-done.1.refs_3_, ...), custom_call_target="tpu_custom_call" | custom-call | flops 1 | tf_op jit(solution)/shard_map/pallas_call | solution.py:382
  70.6 1.0 %shard_map.81 = bf16[128,8192]{1,0:T(8,128)(2,1)} custom-call(bf16[128,8192]{1,0:T(8,128)(2,1)} %shard_map.79.refs_0_, bf16[128,4096]{1,0:T(8,128)(2,1)S(1)} %collective-permute-done.9.refs_1_), custom_call_target="tpu_custom_call", output_to_operand_aliasing={{}: (0, {})} | custom-call | tf_op jit(solution)/shard_map/pallas_call | solution.py:157
  (13 shorter events, 2.6 us)
Async XLA Ops:
  1.1 1.9 %collective-permute-start = (bf16[256,512]{1,0:T(8,128)(2,1)S(1)}, bf16[256,512]{1,0:T(8,128)(2,1)S(1)}, u32[]{:S(2)}, u32[]{:S(2)}) collective-permute-start(bf16[256,512]{1,0:T(8,128)(2,1)S(1)} %get-tuple-element.40), channel_id=1, source_target_pairs={{0,1},{1,0},{2,3},{3,2},{4,5},{5,4},{6,7},{7,6},{8,9},{9,8},{10,11... | collective-permute-start | bytes 786440 | tf_op jit(solution)/shard_map/ppermute | solution.py:408
  3.1 4.8 %collective-permute-start.1 = (bf16[128,8192]{1,0:T(8,128)(2,1)}, bf16[128,8192]{1,0:T(8,128)(2,1)S(1)}, u32[]{:S(2)}, u32[]{:S(2)}) collective-permute-start(bf16[128,8192]{1,0:T(8,128)(2,1)} %refs_2_.11), channel_id=1, source_target_pairs={{0,1},{1,0},{2,3},{3,2},{4,5},{5,4},{6,7},{7,6},{8,9},{9,8},{10,11... | collective-permute-start | bytes 6291464 | tf_op jit(solution)/shard_map/ppermute | solution.py:411
  3.5 13.5 %collective-permute-start.3 = (bf16[512,512]{1,0:T(8,128)(2,1)S(1)}, bf16[512,512]{1,0:T(8,128)(2,1)}, u32[]{:S(2)}, u32[]{:S(2)}) collective-permute-start(bf16[512,512]{1,0:T(8,128)(2,1)S(1)} %shard_map.74.refs_4_), channel_id=1, source_target_pairs={{0,2},{2,0},{4,6},{6,4},{8,10},{10,8},{12,14},{14,12},{1,3},{3,1},... | collective-permute-start | bytes 1572872 | tf_op jit(solution)/shard_map/ppermute | solution.py:425
  3.8 14.9 %collective-permute-start.2 = (bf16[512,512]{1,0:T(8,128)(2,1)S(1)}, bf16[512,512]{1,0:T(8,128)(2,1)S(1)}, u32[]{:S(2)}, u32[]{:S(2)}) collective-permute-start(bf16[512,512]{1,0:T(8,128)(2,1)S(1)} %shard_map.74.refs_4_), channel_id=1, source_target_pairs={{0,4},{2,6},{4,8},{6,10},{8,12},{10,14},{1,5},{3,7},{5,9},{7,11},{... | collective-permute-start | bytes 1572872 | tf_op jit(solution)/shard_map/ppermute | solution.py:424
  7.9 1.6 %copy-start = (bf16[128,8192]{1,0:T(8,128)(2,1)S(1)}, bf16[128,8192]{1,0:T(8,128)(2,1)}, u32[]{:S(2)}) copy-start(bf16[128,8192]{1,0:T(8,128)(2,1)} %refs_2_.11) | copy-start | bytes 6291460
  9.5 11.8 %copy-start.1 = (bf16[128,8192]{1,0:T(8,128)(2,1)S(1)}, bf16[128,8192]{1,0:T(8,128)(2,1)}, u32[]{:S(2)}) copy-start(bf16[128,8192]{1,0:T(8,128)(2,1)} %refs_2_.11) | copy-start | bytes 6291460
  18.7 13.6 %collective-permute-start.5 = (bf16[512,512]{1,0:T(8,128)(2,1)S(1)}, bf16[512,512]{1,0:T(8,128)(2,1)S(1)}, u32[]{:S(2)}, u32[]{:S(2)}) collective-permute-start(bf16[512,512]{1,0:T(8,128)(2,1)S(1)} %collective-permute-done.2.refs_4_), channel_id=1, source_target_pairs={{0,2},{2,0},{4,6},{6,4},{8,10},{10,8},{12,14},{14,12},{1,3},{3,1},... | collective-permute-start | bytes 1572872 | tf_op jit(solution)/shard_map/ppermute | solution.py:425
  20.0 13.7 %collective-permute-start.4 = (bf16[512,512]{1,0:T(8,128)(2,1)S(1)}, bf16[512,512]{1,0:T(8,128)(2,1)S(1)}, u32[]{:S(2)}, u32[]{:S(2)}) collective-permute-start(bf16[512,512]{1,0:T(8,128)(2,1)S(1)} %collective-permute-done.2.refs_4_), channel_id=1, source_target_pairs={{0,4},{2,6},{4,8},{6,10},{8,12},{10,14},{1,5},{3,7},{5,9},{7,11},{... | collective-permute-start | bytes 1572872 | tf_op jit(solution)/shard_map/ppermute | solution.py:424
  33.7 10.9 %collective-permute-start.7 = (bf16[512,512]{1,0:T(8,128)(2,1)S(1)}, bf16[512,512]{1,0:T(8,128)(2,1)S(1)}, u32[]{:S(2)}, u32[]{:S(2)}) collective-permute-start(bf16[512,512]{1,0:T(8,128)(2,1)S(1)} %collective-permute-done.4.refs_4_), channel_id=1, source_target_pairs={{0,2},{2,0},{4,6},{6,4},{8,10},{10,8},{12,14},{14,12},{1,3},{3,1},... | collective-permute-start | bytes 1572872 | tf_op jit(solution)/shard_map/ppermute | solution.py:425
  33.9 12.5 %collective-permute-start.6 = (bf16[512,512]{1,0:T(8,128)(2,1)S(1)}, bf16[512,512]{1,0:T(8,128)(2,1)S(1)}, u32[]{:S(2)}, u32[]{:S(2)}) collective-permute-start(bf16[512,512]{1,0:T(8,128)(2,1)S(1)} %collective-permute-done.4.refs_4_), channel_id=1, source_target_pairs={{0,4},{2,6},{4,8},{6,10},{8,12},{10,14},{1,5},{3,7},{5,9},{7,11},{... | collective-permute-start | bytes 1572872 | tf_op jit(solution)/shard_map/ppermute | solution.py:424
  46.5 9.7 %collective-permute-start.8 = (bf16[512,512]{1,0:T(8,128)(2,1)S(1)}, bf16[512,512]{1,0:T(8,128)(2,1)S(1)}, u32[]{:S(2)}, u32[]{:S(2)}) collective-permute-start(bf16[512,512]{1,0:T(8,128)(2,1)S(1)} %collective-permute-done.6.refs_4_), channel_id=1, source_target_pairs={{0,2},{2,0},{4,6},{6,4},{8,10},{10,8},{12,14},{14,12},{1,3},{3,1},... | collective-permute-start | bytes 1572872 | tf_op jit(solution)/shard_map/ppermute | solution.py:425
  61.0 9.7 %collective-permute-start.9 = (bf16[128,4096]{1,0:T(8,128)(2,1)S(1)}, bf16[128,4096]{1,0:T(8,128)(2,1)S(1)}, u32[]{:S(2)}, u32[]{:S(2)}) collective-permute-start(bf16[128,4096]{1,0:T(8,128)(2,1)S(1)} %shard_map.80), channel_id=1, source_target_pairs={{0,1},{1,0},{2,3},{3,2},{4,5},{5,4},{6,7},{7,6},{8,9},{9,8},{10,11... | collective-permute-start | bytes 3145736 | tf_op jit(solution)/shard_map/ppermute | solution.py:442

commit v5 on v4

--- a/solution.py
+++ b/solution.py
@@ -165,13 +165,10 @@
     )(out, *parts)
 
 
-def bits(table_ref, row, low):
-    word = jnp.int32(0)
-    for index in range(table_ref.shape[1]):
-        entry = table_ref[row, index] - low
-        inside = (entry >= 0) & (entry < 32)
-        word = word | jnp.where(inside, lax.shift_left(jnp.int32(1), jnp.where(inside, entry, 0)), 0)
-    return word
+def bits(rows, low):
+    entries = rows - low
+    inside = (entries >= 0) & (entries < 32)
+    return jnp.sum(jnp.where(inside, lax.shift_left(jnp.ones_like(entries), entries & 31), 0), axis=1)
 
 
 def bit_at(word, place):
@@ -179,7 +176,7 @@
 
 
 def chunk_kernel(sizes, units, first, last, turns, *refs):
-    cores, pair, groups, per_group, block, blocks = sizes
+    cores, pair, groups, per_group, block = sizes
     table_hbm, scale_hbm, *query_hbm = refs[: 2 + cores]
     unit_refs = refs[2 + cores : 2 + cores + len(units)]
     rest = refs[2 + cores + len(units) :]
@@ -190,13 +187,12 @@
         out_hbm, rest = rest[: len(turns)], rest[len(turns) :]
     else:
         new, rest = rest[:3], rest[3:]
-    query_ref, tile_ref, values_ref, slot_ref, count_ref, mask_ref, table_ref, scale_ref, sems, table_sems = rest[:10]
+    query_ref, tile_ref, values_ref, slot_ref, count_ref, table_ref, scale_ref, sems, table_sems = rest[:9]
     if last:
-        out_ref, out_sems = rest[10:]
+        out_ref, out_sems = rest[9:]
     groups_here = groups // cores
     width = per_group * block
     wide = per_group * DH
-    words = -(-blocks // 32)
     slots = len(units) * cores
     core = lax.axis_index("ulysses")
     span = lax.axis_index("blk")
@@ -244,15 +240,11 @@
         ]
     )
 
-    for group in range(groups_here):
-        mask_ref[group, 0] = bits(table_ref, groups + core * groups_here + group, 0)
-        for word in range(words):
-            mask_ref[group, 1 + word] = bits(table_ref, core * groups_here + group, word * 32)
-
     def fetch(step, buffer):
         turn, group = turn_at(step)
         here = span * cores + row_of(turn)
-        slash_bits = mask_ref[group, 0]
+        own_group = core * groups_here + group
+        slash_bits = table_ref[own_group, 0]
         count = jnp.int32(0)
         for unit in range(len(units)):
             for ahead in range(cores):
@@ -261,7 +253,7 @@
                 back = here - place
                 valid = (spans[unit] >= 0) & (back >= 0)
                 at = jnp.where(valid, place, 0)
-                vertical_bits = mask_ref[group, 1 + lax.shift_right_logical(at, 5)]
+                vertical_bits = table_ref[own_group, 1 + lax.shift_right_logical(at, 5)]
                 near = jnp.where(back < 32, bit_at(slash_bits, back & 31), 0)
                 live = jnp.where(valid, near | bit_at(vertical_bits, at & 31), 0)
 
@@ -348,7 +340,7 @@
 
 
 def attend_chunk(sizes, table, scales, queries, units, arrays, state, turns, last):
-    cores, pair, groups, per_group, block, blocks = sizes
+    cores, pair, groups, per_group, block = sizes
     first = state is None
     width = per_group * block
     slots = len(units) * cores
@@ -367,7 +359,6 @@
         pltpu.VMEM((DH, slots * block), BF16),
         pltpu.SMEM((2, slots), jnp.int32),
         pltpu.SMEM((2,), jnp.int32),
-        pltpu.SMEM((groups // cores, 1 + -(-blocks // 32)), jnp.int32),
         pltpu.SMEM(table.shape, jnp.int32),
         pltpu.SMEM(scales.shape, F32),
         pltpu.SemaphoreType.DMA((2, 2)),
@@ -399,7 +390,7 @@
     pair = 2 if spans % 2 == 0 else 1
     lines = spans // pair
     core = lax.axis_index("ulysses")
-    sizes = (cores, pair, groups, per_group, block, blocks)
+    sizes = (cores, pair, groups, per_group, block)
 
     turned = [[(c, (c - step) % cores) for c in range(cores)] for step in range(cores)]
     back = [[(c, (c + step) % cores) for c in range(cores)] for step in range(cores)]
@@ -409,11 +400,12 @@
     )
     waiting, _ = lax.optimization_barrier((query_int, own))
     queries = [query_int] + [lax.ppermute(waiting, "ulysses", turned[step]) for step in range(1, cores)]
-    table = jnp.concatenate([verticals, slashes], axis=0)
+    words = [bits(slashes, 0)] + [bits(verticals, low) for low in range(0, blocks, 32)]
+    table = jnp.stack(words, axis=1).astype(jnp.int32)
     key_scales = jnp.pad(key_scale, ((0, 0), (0, query_scale.shape[1] - groups)))
     scales = jnp.concatenate([query_scale, key_scales], axis=0).astype(F32)
 
-    climb = [(s, s + pair) for s in range(spans - pair)]
+    climb = [(s, (s + pair) % spans) for s in range(spans)]
     swap = [(s, s ^ 1) for s in range(spans)]
     turns = tuple(range(cores - 1, -1, -1))
     climbed, crossed, state = own, None, None
@@ -433,7 +425,7 @@
         run = functools.partial(attend_chunk, sizes, table, scales, queries, tuple(units), arrays, state)
         if not last:
             state = run(turns, False)
-            climbed, crossed, state = lax.optimization_barrier((climbed, crossed, state))
+            state, crossed, climbed = lax.optimization_barrier((state, crossed, climbed))
     if cores == 1:
         return run(turns, True)[0]
     others = run(turns[:-1], True)

time: 72.2 us -> 69.7 us (0.965)
  starting transfers between devices: 12.5 us -> 9.92 us
  other arithmetic: 0.66 us -> 2.28 us
  Pallas kernels: 45.5 us -> 44.1 us
  local copies, waits for them, and re-layouts: 3.73 us -> 2.43 us
  waiting for transfers between devices: 9.21 us -> 10.3 us
    ppermute x4, waiting for transfers between devices: 3.13 us -> 6.93 us  [local(): lax.ppermute(sent, 'blk', swap)]
    ppermute x3, waiting for transfers between devices: 4.92 us -> 1.54 us  [local(): climbed = lax.ppermute(sent, 'blk', climb) if step + 1 < lines else None]
    ppermute x4, starting transfers between devices: 2.93 us -> 0.91 us  [local(): lax.ppermute(sent, 'blk', swap)]
    reduce_sum x0 -> x2, other arithmetic: none -> 1.61 us  [bits(): jnp.sum(jnp.where(inside, lax.shift_left(jnp.ones_like(entries), entries...]
    pallas_call x6, Pallas kernels: 43.3 us -> 41.9 us  [attend_chunk(): pl.pallas_call(kernel, in_specs=[ANYWHERE] * (2 + cores + len(units)) + (...]
    unnamed x6 -> x3, local copies, waits for them, and re-layouts: 3.04 us -> 2.35 us
  transfers between devices with their start and end apart: 10 -> 10, of which waited for: 7 -> 6; matrix products, arithmetic and copies ran while one was open for 4% -> 5% of each run, Pallas kernels for 54% -> 54%
where the time goes in v5:
time: 69.7 us; the launch traced here: 69.3 us
  Pallas kernels  44.1 us (63%)
  waiting for transfers between devices  10.3 us (15%)
  starting transfers between devices  9.92 us (14%)
  local copies, waits for them, and re-layouts  2.43 us (3%)
  other arithmetic  2.28 us (3%)
    pallas_call x6, Pallas kernels, attend_chunk(): pl.pallas_call(kernel, in_specs=[ANYWHERE] * (2 + cores + len(units)) + (...  41.9 us
    ppermute x4, waiting for transfers between devices, local(): lax.ppermute(sent, 'blk', swap)  6.93 us
    ppermute x1, starting transfers between devices, local(): lax.ppermute(one, 'ulysses', back[turn])  3.96 us
    ppermute x3, starting transfers between devices, local(): climbed = lax.ppermute(sent, 'blk', climb) if step + 1 < lines else None  3.87 us
    unnamed x3, local copies, waits for them, and re-layouts  2.35 us
    reduce_sum x2, other arithmetic, bits(): jnp.sum(jnp.where(inside, lax.shift_left(jnp.ones_like(entries), entries...  1.61 us
    ppermute x3, waiting for transfers between devices, local(): climbed = lax.ppermute(sent, 'blk', climb) if step + 1 < lines else None  1.54 us
  transfers between devices with their start and end apart: 10, of which 6 were waited for; matrix products, arithmetic and copies ran while one was open for 5% of the time, Pallas kernels for 54%

profile of v5, /device:TPU:31, one launch (start us, length us, event | category | flops | bytes accessed | tf_op | source)
XLA Modules:
  0.0 69.3 jit_solution(3756467703664181889)
XLA Ops:
  0.0 1.1 %shard_map.73 = (bf16[256,512]{1,0:T(8,128)(2,1)S(1)}, bf16[256,512]{1,0:T(8,128)(2,1)S(1)}) custom-call(bf16[128,1024]{1,0:T(8,128)(2,1)} %key_ref.1, bf16[128,1024]{1,0:T(8,128)(2,1)} %value_ref.1), custom_call_target="tpu_custom_call" | custom-call | tf_op jit(solution)/shard_map/pallas_call | solution.py:112
  1.1 0.7 %collective-permute-start = (bf16[256,512]{1,0:T(8,128)(2,1)S(1)}, bf16[256,512]{1,0:T(8,128)(2,1)S(1)}, u32[]{:S(2)}, u32[]{:S(2)}) collective-permute-start(bf16[256,512]{1,0:T(8,128)(2,1)S(1)} %get-tuple-element.40), channel_id=1, source_target_pairs={{0,1},{1,0},{2,3},{3,2},{4,5},{5,4},{6,7},{7,6},{8,9},{9,8},{10,11... | collective-permute-start | bytes 786440 | tf_op jit(solution)/shard_map/ppermute | solution.py:399
  1.9 1.2 %collective-permute-done.refs_1_ = bf16[256,512]{1,0:T(8,128)(2,1)S(1)} collective-permute-done((bf16[256,512]{1,0:T(8,128)(2,1)S(1)}, bf16[256,512]{1,0:T(8,128)(2,1)S(1)}, u32[]{:S(2)}, u32[]{:S(2)}) %collective-permute-start) | collective-permute-done | bytes 262176 | tf_op jit(solution)/shard_map/ppermute | solution.py:399
  3.1 0.4 collective-permute-start.1
  3.8 0.8 %select_reduce_fusion = s32[8]{0:T(128)S(1)} fusion(s32[8,8]{1,0:T(8,128)} %param.12), kind=kLoop, calls=%fused_computation.4 | loop fusion | flops 440 | bytes 288 | tf_op jit(solution)/shard_map/reduce_sum | solution.py:171
  4.6 0.8 %select_reduce_fusion.1 = s32[8]{0:T(128)S(1)} fusion(s32[8,8]{1,0:T(8,128)} %param.13), kind=kLoop, calls=%fused_computation.5 | loop fusion | flops 440 | bytes 288 | tf_op jit(solution)/shard_map/reduce_sum | solution.py:171
  5.5 0.8 %copy.21 = bf16[16,8]{1,0:T(8,128)(2,1)S(1)} copy(bf16[16,8]{0,1:T(8,128)(2,1)} %param.11) | data formatting | bytes 512 | tf_op args[4]
  6.2 0.7 fusion.2.refs_1_
  6.9 0.6 collective-permute-done.1.refs_3_
  7.5 1.6 %copy-done = bf16[128,8192]{1,0:T(8,128)(2,1)S(1)} copy-done((bf16[128,8192]{1,0:T(8,128)(2,1)S(1)}, bf16[128,8192]{1,0:T(8,128)(2,1)}, u32[]{:S(2)}) %copy-start) | copy-done | bytes 2097176
  9.1 6.4 %shard_map.75 = (f32[1,8192]{1,0:T(1,128)S(1)}, f32[1,8192]{1,0:T(1,128)S(1)}, f32[128,8192]{1,0:T(8,128)S(1)}) custom-call(s32[8,2]{1,0:T(8,128)S(1)} %copy.26.refs_0_, f32[18,64]{1,0:T(8,128)S(1)} %fusion.2.refs_1_, bf16[128,8192]{1,0:T(8,128)(2,1)S(1)} %copy-done, bf16[128,8192]{1,0:T(8,128)(2,1)S(1)} %collective-permute-done.1.refs_3_, ...), custom_call_target="tpu_custom_call" | custom-call | flops 1 | tf_op jit(solution)/shard_map/pallas_call | solution.py:373
  15.5 1.5 %collective-permute-done.3.refs_4_ = bf16[512,512]{1,0:T(8,128)(2,1)S(1)} collective-permute-done((bf16[512,512]{1,0:T(8,128)(2,1)S(1)}, bf16[512,512]{1,0:T(8,128)(2,1)S(1)}, u32[]{:S(2)}, u32[]{:S(2)}) %collective-permute-start.3) | collective-permute-done | bytes 524320 | tf_op jit(solution)/shard_map/ppermute | solution.py:416
  17.0 1.8 %collective-permute-start.5 = (bf16[512,512]{1,0:T(8,128)(2,1)S(1)}, bf16[512,512]{1,0:T(8,128)(2,1)S(1)}, u32[]{:S(2)}, u32[]{:S(2)}) collective-permute-start(bf16[512,512]{1,0:T(8,128)(2,1)S(1)} %collective-permute-done.3.refs_4_), channel_id=1, source_target_pairs={{0,4},{2,6},{4,8},{6,10},{8,12},{10,14},{12,0},{14,2},{1,5},{3,7},... | collective-permute-start | bytes 1572872 | tf_op jit(solution)/shard_map/ppermute | solution.py:416
  19.0 10.7 %shard_map.76 = (f32[1,8192]{1,0:T(1,128)S(1)}, f32[1,8192]{1,0:T(1,128)S(1)}, f32[128,8192]{1,0:T(8,128)S(1)}) custom-call(s32[8,2]{1,0:T(8,128)S(1)} %copy.26.refs_0_, f32[18,64]{1,0:T(8,128)S(1)} %fusion.2.refs_1_, bf16[128,8192]{1,0:T(8,128)(2,1)S(1)} %copy-done, ...), custom_call_target="tpu_custom_call", output_to_operand_aliasing={{0}: (6, {}), {1}: (7, {}), {2}: (8, {})} | custom-call | flops 1 | tf_op jit(solution)/shard_map/pallas_call | solution.py:373
  29.8 1.3 %collective-permute-done.4.refs_5_ = bf16[512,512]{1,0:T(8,128)(2,1)S(1)} collective-permute-done((bf16[512,512]{1,0:T(8,128)(2,1)S(1)}, bf16[512,512]{1,0:T(8,128)(2,1)S(1)}, u32[]{:S(2)}, u32[]{:S(2)}) %collective-permute-start.4) | collective-permute-done | bytes 524320 | tf_op jit(solution)/shard_map/ppermute | solution.py:417
  31.1 2.1 %collective-permute-start.7 = (bf16[512,512]{1,0:T(8,128)(2,1)S(1)}, bf16[512,512]{1,0:T(8,128)(2,1)S(1)}, u32[]{:S(2)}, u32[]{:S(2)}) collective-permute-start(bf16[512,512]{1,0:T(8,128)(2,1)S(1)} %collective-permute-done.5.refs_4_), channel_id=1, source_target_pairs={{0,4},{2,6},{4,8},{6,10},{8,12},{10,14},{12,0},{14,2},{1,5},{3,7},... | collective-permute-start | bytes 1572872 | tf_op jit(solution)/shard_map/ppermute | solution.py:416
  33.4 9.4 %shard_map.77 = (f32[1,8192]{1,0:T(1,128)S(1)}, f32[1,8192]{1,0:T(1,128)S(1)}, f32[128,8192]{1,0:T(8,128)S(1)}) custom-call(s32[8,2]{1,0:T(8,128)S(1)} %copy.26.refs_0_, f32[18,64]{1,0:T(8,128)S(1)} %fusion.2.refs_1_, bf16[128,8192]{1,0:T(8,128)(2,1)S(1)} %copy-done, ...), custom_call_target="tpu_custom_call", output_to_operand_aliasing={{0}: (6, {}), {1}: (7, {}), {2}: (8, {})} | custom-call | flops 1 | tf_op jit(solution)/shard_map/pallas_call | solution.py:373
  42.8 1.7 %collective-permute-done.6.refs_5_ = bf16[512,512]{1,0:T(8,128)(2,1)S(1)} collective-permute-done((bf16[512,512]{1,0:T(8,128)(2,1)S(1)}, bf16[512,512]{1,0:T(8,128)(2,1)S(1)}, u32[]{:S(2)}, u32[]{:S(2)}) %collective-permute-start.6) | collective-permute-done | bytes 524320 | tf_op jit(solution)/shard_map/ppermute | solution.py:417
  44.7 6.2 %shard_map.78 = (f32[1,8192]{1,0:T(1,128)S(1)}, f32[1,8192]{1,0:T(1,128)S(1)}, f32[128,8192]{1,0:T(8,128)S(1)}) custom-call(s32[8,2]{1,0:T(8,128)S(1)} %copy.26.refs_0_, f32[18,64]{1,0:T(8,128)S(1)} %fusion.2.refs_1_, bf16[128,8192]{1,0:T(8,128)(2,1)S(1)} %copy-done, ...), custom_call_target="tpu_custom_call", output_to_operand_aliasing={{0}: (6, {}), {1}: (7, {}), {2}: (8, {})} | custom-call | flops 1 | tf_op jit(solution)/shard_map/pallas_call | solution.py:373
  51.0 4.0 %collective-permute-done.8.refs_4_ = bf16[512,512]{1,0:T(8,128)(2,1)S(1)} collective-permute-done((bf16[512,512]{1,0:T(8,128)(2,1)S(1)}, bf16[512,512]{1,0:T(8,128)(2,1)S(1)}, u32[]{:S(2)}, u32[]{:S(2)}) %collective-permute-start.8) | collective-permute-done | bytes 524320 | tf_op jit(solution)/shard_map/ppermute | solution.py:417
  55.0 4.4 %shard_map.80 = bf16[128,4096]{1,0:T(8,128)(2,1)S(1)} custom-call(s32[8,2]{1,0:T(8,128)S(1)} %copy.26.refs_0_, f32[18,64]{1,0:T(8,128)S(1)} %fusion.2.refs_1_, bf16[128,8192]{1,0:T(8,128)(2,1)S(1)} %copy-done, bf16[128,8192]{1,0:T(8,128)(2,1)S(1)} %collective-permute-done.1.refs_3_, bf16[512,512]{1,0:T(8,128)(2,1)S(1)} %collective-permute-done.8.refs_4_, ...), custom_call_target="tpu_custom_call" | custom-call | flops 1 | tf_op jit(solution)/shard_map/pallas_call | solution.py:373
  59.3 4.0 %collective-permute-start.9 = (bf16[128,4096]{1,0:T(8,128)(2,1)S(1)}, bf16[128,4096]{1,0:T(8,128)(2,1)S(1)}, u32[]{:S(2)}, u32[]{:S(2)}) collective-permute-start(bf16[128,4096]{1,0:T(8,128)(2,1)S(1)} %shard_map.80), channel_id=1, source_target_pairs={{0,1},{1,0},{2,3},{3,2},{4,5},{5,4},{6,7},{7,6},{8,9},{9,8},{10,11... | collective-permute-start | bytes 3145736 | tf_op jit(solution)/shard_map/ppermute | solution.py:434
  63.3 4.8 %shard_map.79.refs_0_ = bf16[128,8192]{1,0:T(8,128)(2,1)} custom-call(s32[8,2]{1,0:T(8,128)S(1)} %copy.26.refs_0_, f32[18,64]{1,0:T(8,128)S(1)} %fusion.2.refs_1_, bf16[128,8192]{1,0:T(8,128)(2,1)S(1)} %copy-done, bf16[128,8192]{1,0:T(8,128)(2,1)S(1)} %collective-permute-done.1.refs_3_, bf16[512,512]{1,0:T(8,128)(2,1)S(1)} %collective-permute-done.8.refs_4_, ...), custom_call_target="tpu_custom_call" | custom-call | flops 1 | tf_op jit(solution)/shard_map/pallas_call | solution.py:373
  68.1 1.0 %shard_map.81 = bf16[128,8192]{1,0:T(8,128)(2,1)} custom-call(bf16[128,8192]{1,0:T(8,128)(2,1)} %shard_map.79.refs_0_, bf16[128,4096]{1,0:T(8,128)(2,1)S(1)} %collective-permute-done.9.refs_1_), custom_call_target="tpu_custom_call", output_to_operand_aliasing={{}: (0, {})} | custom-call | tf_op jit(solution)/shard_map/pallas_call | solution.py:157
  (13 shorter events, 1.1 us)
Async XLA Ops:
  1.1 1.9 %collective-permute-start = (bf16[256,512]{1,0:T(8,128)(2,1)S(1)}, bf16[256,512]{1,0:T(8,128)(2,1)S(1)}, u32[]{:S(2)}, u32[]{:S(2)}) collective-permute-start(bf16[256,512]{1,0:T(8,128)(2,1)S(1)} %get-tuple-element.40), channel_id=1, source_target_pairs={{0,1},{1,0},{2,3},{3,2},{4,5},{5,4},{6,7},{7,6},{8,9},{9,8},{10,11... | collective-permute-start | bytes 786440 | tf_op jit(solution)/shard_map/ppermute | solution.py:399
  3.1 4.4 %collective-permute-start.1 = (bf16[128,8192]{1,0:T(8,128)(2,1)}, bf16[128,8192]{1,0:T(8,128)(2,1)S(1)}, u32[]{:S(2)}, u32[]{:S(2)}) collective-permute-start(bf16[128,8192]{1,0:T(8,128)(2,1)} %refs_2_.11), channel_id=1, source_target_pairs={{0,1},{1,0},{2,3},{3,2},{4,5},{5,4},{6,7},{7,6},{8,9},{9,8},{10,11... | collective-permute-start | bytes 6291464 | tf_op jit(solution)/shard_map/ppermute | solution.py:402
  3.5 13.5 %collective-permute-start.3 = (bf16[512,512]{1,0:T(8,128)(2,1)S(1)}, bf16[512,512]{1,0:T(8,128)(2,1)S(1)}, u32[]{:S(2)}, u32[]{:S(2)}) collective-permute-start(bf16[512,512]{1,0:T(8,128)(2,1)S(1)} %shard_map.74.refs_4_), channel_id=1, source_target_pairs={{0,4},{2,6},{4,8},{6,10},{8,12},{10,14},{12,0},{14,2},{1,5},{3,7},... | collective-permute-start | bytes 1572872 | tf_op jit(solution)/shard_map/ppermute | solution.py:416
  3.5 13.5 %collective-permute-start.2 = (bf16[512,512]{1,0:T(8,128)(2,1)S(1)}, bf16[512,512]{1,0:T(8,128)(2,1)}, u32[]{:S(2)}, u32[]{:S(2)}) collective-permute-start(bf16[512,512]{1,0:T(8,128)(2,1)S(1)} %shard_map.74.refs_4_), channel_id=1, source_target_pairs={{0,2},{2,0},{4,6},{6,4},{8,10},{10,8},{12,14},{14,12},{1,3},{3,1},... | collective-permute-start | bytes 1572872 | tf_op jit(solution)/shard_map/ppermute | solution.py:417
  7.5 1.6 %copy-start = (bf16[128,8192]{1,0:T(8,128)(2,1)S(1)}, bf16[128,8192]{1,0:T(8,128)(2,1)}, u32[]{:S(2)}) copy-start(bf16[128,8192]{1,0:T(8,128)(2,1)} %refs_2_.11) | copy-start | bytes 6291460
  17.0 12.7 %collective-permute-start.5 = (bf16[512,512]{1,0:T(8,128)(2,1)S(1)}, bf16[512,512]{1,0:T(8,128)(2,1)S(1)}, u32[]{:S(2)}, u32[]{:S(2)}) collective-permute-start(bf16[512,512]{1,0:T(8,128)(2,1)S(1)} %collective-permute-done.3.refs_4_), channel_id=1, source_target_pairs={{0,4},{2,6},{4,8},{6,10},{8,12},{10,14},{12,0},{14,2},{1,5},{3,7},... | collective-permute-start | bytes 1572872 | tf_op jit(solution)/shard_map/ppermute | solution.py:416
  18.8 12.3 %collective-permute-start.4 = (bf16[512,512]{1,0:T(8,128)(2,1)S(1)}, bf16[512,512]{1,0:T(8,128)(2,1)S(1)}, u32[]{:S(2)}, u32[]{:S(2)}) collective-permute-start(bf16[512,512]{1,0:T(8,128)(2,1)S(1)} %collective-permute-done.3.refs_4_), channel_id=1, source_target_pairs={{0,2},{2,0},{4,6},{6,4},{8,10},{10,8},{12,14},{14,12},{1,3},{3,1},... | collective-permute-start | bytes 1572872 | tf_op jit(solution)/shard_map/ppermute | solution.py:417
  31.1 11.8 %collective-permute-start.7 = (bf16[512,512]{1,0:T(8,128)(2,1)S(1)}, bf16[512,512]{1,0:T(8,128)(2,1)S(1)}, u32[]{:S(2)}, u32[]{:S(2)}) collective-permute-start(bf16[512,512]{1,0:T(8,128)(2,1)S(1)} %collective-permute-done.5.refs_4_), channel_id=1, source_target_pairs={{0,4},{2,6},{4,8},{6,10},{8,12},{10,14},{12,0},{14,2},{1,5},{3,7},... | collective-permute-start | bytes 1572872 | tf_op jit(solution)/shard_map/ppermute | solution.py:416
  33.2 11.4 %collective-permute-start.6 = (bf16[512,512]{1,0:T(8,128)(2,1)S(1)}, bf16[512,512]{1,0:T(8,128)(2,1)S(1)}, u32[]{:S(2)}, u32[]{:S(2)}) collective-permute-start(bf16[512,512]{1,0:T(8,128)(2,1)S(1)} %collective-permute-done.5.refs_4_), channel_id=1, source_target_pairs={{0,2},{2,0},{4,6},{6,4},{8,10},{10,8},{12,14},{14,12},{1,3},{3,1},... | collective-permute-start | bytes 1572872 | tf_op jit(solution)/shard_map/ppermute | solution.py:417
  44.5 10.4 %collective-permute-start.8 = (bf16[512,512]{1,0:T(8,128)(2,1)S(1)}, bf16[512,512]{1,0:T(8,128)(2,1)S(1)}, u32[]{:S(2)}, u32[]{:S(2)}) collective-permute-start(bf16[512,512]{1,0:T(8,128)(2,1)S(1)} %collective-permute-done.7.refs_4_), channel_id=1, source_target_pairs={{0,2},{2,0},{4,6},{6,4},{8,10},{10,8},{12,14},{14,12},{1,3},{3,1},... | collective-permute-start | bytes 1572872 | tf_op jit(solution)/shard_map/ppermute | solution.py:417
  59.3 8.8 %collective-permute-start.9 = (bf16[128,4096]{1,0:T(8,128)(2,1)S(1)}, bf16[128,4096]{1,0:T(8,128)(2,1)S(1)}, u32[]{:S(2)}, u32[]{:S(2)}) collective-permute-start(bf16[128,4096]{1,0:T(8,128)(2,1)S(1)} %shard_map.80), channel_id=1, source_target_pairs={{0,1},{1,0},{2,3},{3,2},{4,5},{5,4},{6,7},{7,6},{8,9},{9,8},{10,11... | collective-permute-start | bytes 3145736 | tf_op jit(solution)/shard_map/ppermute | solution.py:434

commit v6 on v5

--- a/solution.py
+++ b/solution.py
@@ -187,7 +187,7 @@
         out_hbm, rest = rest[: len(turns)], rest[len(turns) :]
     else:
         new, rest = rest[:3], rest[3:]
-    query_ref, tile_ref, values_ref, slot_ref, count_ref, table_ref, scale_ref, sems, table_sems = rest[:9]
+    query_ref, tile_ref, values_ref, slot_ref, place_ref, table_ref, scale_ref, sems, table_sems = rest[:9]
     if last:
         out_ref, out_sems = rest[9:]
     groups_here = groups // cores
@@ -227,12 +227,39 @@
         target = out_hbm[index].at[:, pl.ds(pl.multiple_of(place, wide), wide)]
         return pltpu.make_async_copy(out_ref.at[buffer], target, out_sems.at[buffer])
 
-    def tile_copy(unit, part, group, buffer, at):
+    def part_of(turn, slot):
+        return lax.rem(turn + slot, cores) if first else slot % cores
+
+    def tile_copy(slot, part, group, buffer):
         column = pl.ds(pl.multiple_of(group * DH, DH), DH)
         rows = pl.ds(pl.multiple_of(part * (2 * block), 2 * block), 2 * block)
-        return pltpu.make_async_copy(unit_refs[unit].at[rows, column], tile_ref.at[buffer, at], sems.at[1, buffer])
-
-    by_turn(0, lambda index, at, group: query_copy(at, group, 0).start())
+        source = unit_refs[slot // cores].at[rows, column]
+        return pltpu.make_async_copy(source, tile_ref.at[buffer, slot], sems.at[1, buffer])
+
+    def fetch(step, buffer):
+        by_turn(step, lambda index, at, group: query_copy(at, group, buffer).start())
+        turn, group = turn_at(step)
+        for slot in range(slots):
+            tile_copy(slot, part_of(turn, slot), group, buffer).start()
+
+    def list_live(turn, own_group):
+        here = span * cores + row_of(turn)
+        slash_bits = table_ref[own_group, 0]
+        count = jnp.int32(0)
+        for slot in range(slots):
+            at_span = spans[slot // cores]
+            place = at_span * cores + lax.rem(core + part_of(turn, slot), cores)
+            back = here - place
+            valid = (at_span >= 0) & (back >= 0)
+            at = jnp.where(valid, place, 0)
+            near = jnp.where(back < 32, bit_at(slash_bits, back & 31), 0)
+            far = bit_at(table_ref[own_group, 1 + lax.shift_right_logical(at, 5)], at & 31)
+            slot_ref[count] = slot
+            place_ref[count] = at
+            count = count + jnp.where(valid, near | far, 0)
+        return count
+
+    fetch(0, 0)
     run_copies(
         [
             pltpu.make_async_copy(table_hbm, table_ref, table_sems.at[0]),
@@ -240,57 +267,26 @@
         ]
     )
 
-    def fetch(step, buffer):
-        turn, group = turn_at(step)
-        here = span * cores + row_of(turn)
-        own_group = core * groups_here + group
-        slash_bits = table_ref[own_group, 0]
-        count = jnp.int32(0)
-        for unit in range(len(units)):
-            for ahead in range(cores):
-                part = lax.rem(turn + ahead, cores)
-                place = spans[unit] * cores + lax.rem(core + part, cores)
-                back = here - place
-                valid = (spans[unit] >= 0) & (back >= 0)
-                at = jnp.where(valid, place, 0)
-                vertical_bits = table_ref[own_group, 1 + lax.shift_right_logical(at, 5)]
-                near = jnp.where(back < 32, bit_at(slash_bits, back & 31), 0)
-                live = jnp.where(valid, near | bit_at(vertical_bits, at & 31), 0)
-
-                @pl.when(live > 0)
-                def _(unit=unit, part=part, count=count, place=place):
-                    tile_copy(unit, part, group, buffer, count).start()
-                    slot_ref[buffer, count] = place
-
-                count = count + live
-        count_ref[buffer] = count
-
-    fetch(0, 0)
-
     @pl.loop(0, steps)
     def _(step):
         buffer = lax.rem(step, 2)
 
         @pl.when(step + 1 < steps)
         def _():
-            by_turn(step + 1, lambda index, at, group: query_copy(at, group, 1 - buffer).start())
             fetch(step + 1, 1 - buffer)
 
         turn, group = turn_at(step)
+        count = list_live(turn, core * groups_here + group)
         query_copy(turns[0], 0, buffer).wait()
-        count = count_ref[buffer]
-        for at in range(slots):
-
-            @pl.when(at < count)
-            def _(at=at):
-                tile_copy(0, 0, 0, buffer, at).wait()
+        for slot in range(slots):
+            tile_copy(slot, 0, 0, buffer).wait()
 
         own_group = core * groups_here + group
         head_base = own_group * per_group
         scale_row = row_of(turn)
 
         def scale_at(slot, head):
-            return scale_ref[scale_row, head_base + head] * scale_ref[cores + slot_ref[buffer, slot], own_group] * LOG2E
+            return scale_ref[scale_row, head_base + head] * scale_ref[cores + place_ref[slot], own_group] * LOG2E
 
         if last:
 
@@ -307,15 +303,16 @@
 
             @pl.when(count == many)
             def _(many=many):
-                for at in range(many):
-                    values_ref[:, at * block : (at + 1) * block] = tile_ref[buffer, at, block : 2 * block, :].T
+                tiles = [slot_ref[at] for at in range(many)]
+                for at, tile in enumerate(tiles):
+                    values_ref[:, at * block : (at + 1) * block] = tile_ref[buffer, tile, block : 2 * block, :].T
                 attend(
                     many,
                     first,
                     block,
                     per_group,
                     scale_at,
-                    jnp.concatenate([tile_ref[buffer, at, 0:block, :] for at in range(many)], axis=0),
+                    jnp.concatenate([tile_ref[buffer, tile, 0:block, :] for tile in tiles], axis=0),
                     values_ref[:, 0 : many * block],
                     query_ref.at[buffer],
                     None if first else (old, base),
@@ -357,8 +354,8 @@
         pltpu.VMEM((2, block, per_group * DH), BF16),
         pltpu.VMEM((2, slots, 2 * block, DH), BF16),
         pltpu.VMEM((DH, slots * block), BF16),
-        pltpu.SMEM((2, slots), jnp.int32),
-        pltpu.SMEM((2,), jnp.int32),
+        pltpu.SMEM((slots,), jnp.int32),
+        pltpu.SMEM((slots,), jnp.int32),
         pltpu.SMEM(table.shape, jnp.int32),
         pltpu.SMEM(scales.shape, F32),
         pltpu.SemaphoreType.DMA((2, 2)),
@@ -406,6 +403,7 @@
     scales = jnp.concatenate([query_scale, key_scales], axis=0).astype(F32)
 
     climb = [(s, (s + pair) % spans) for s in range(spans)]
+    up = [(s, s + pair) for s in range(spans - pair)]
     swap = [(s, s ^ 1) for s in range(spans)]
     turns = tuple(range(cores - 1, -1, -1))
     climbed, crossed, state = own, None, None
@@ -413,7 +411,7 @@
     for step in range(steps):
         last = step + 1 == steps
         sent, arrived = climbed, crossed
-        climbed = lax.ppermute(sent, "blk", climb) if step + 1 < lines else None
+        climbed = lax.ppermute(sent, "blk", up if step > 1 else climb) if step + 1 < lines else None
         crossed = lax.ppermute(sent, "blk", swap) if pair == 2 and sent is not None else None
         units, arrays = [], []
         if sent is not None:

time: 69.7 us -> 69 us (0.990)
    ppermute x4, waiting for transfers between devices: 6.93 us -> 3.83 us  [local(): lax.ppermute(sent, 'blk', swap)]
    ppermute x3, waiting for transfers between devices: 1.54 us -> 4.62 us  [local(): lax.ppermute(sent, 'blk', up if step > 1 else climb)]
  transfers between devices with their start and end apart: 10 -> 10, of which waited for: 6 -> 7; matrix products, arithmetic and copies ran while one was open for 5% -> 5% of each run, Pallas kernels for 54% -> 55%
where the time goes in v6:
time: 69 us; the launch traced here: 68.3 us
  Pallas kernels  43.7 us (63%)
  waiting for transfers between devices  10.3 us (15%)
  starting transfers between devices  9.36 us (14%)
  local copies, waits for them, and re-layouts  2.43 us (4%)
  other arithmetic  2.28 us (3%)
    pallas_call x6, Pallas kernels, attend_chunk(): pl.pallas_call(kernel, in_specs=[ANYWHERE] * (2 + cores + len(units)) + (...  41.5 us
    ppermute x3, waiting for transfers between devices, local(): lax.ppermute(sent, 'blk', up if step > 1 else climb)  4.62 us
    ppermute x1, starting transfers between devices, local(): lax.ppermute(one, 'ulysses', back[turn])  3.98 us
    ppermute x4, waiting for transfers between devices, local(): lax.ppermute(sent, 'blk', swap)  3.83 us
    ppermute x3, starting transfers between devices, local(): lax.ppermute(sent, 'blk', up if step > 1 else climb)  3.23 us
    unnamed x3, local copies, waits for them, and re-layouts  2.35 us
    reduce_sum x2, other arithmetic, bits(): jnp.sum(jnp.where(inside, lax.shift_left(jnp.ones_like(entries), entries...  1.61 us
  transfers between devices with their start and end apart: 10, of which 7 were waited for; matrix products, arithmetic and copies ran while one was open for 5% of the time, Pallas kernels for 55%

profile of v6, /device:TPU:31, one launch (start us, length us, event | category | flops | bytes accessed | tf_op | source)
XLA Modules:
  0.0 68.3 jit_solution(15131401963330167266)
XLA Ops:
  0.0 1.1 %shard_map.73 = (bf16[256,512]{1,0:T(8,128)(2,1)S(1)}, bf16[256,512]{1,0:T(8,128)(2,1)S(1)}) custom-call(bf16[128,1024]{1,0:T(8,128)(2,1)} %key_ref.1, bf16[128,1024]{1,0:T(8,128)(2,1)} %value_ref.1), custom_call_target="tpu_custom_call" | custom-call | tf_op jit(solution)/shard_map/pallas_call | solution.py:112
  1.1 0.7 %collective-permute-start = (bf16[256,512]{1,0:T(8,128)(2,1)S(1)}, bf16[256,512]{1,0:T(8,128)(2,1)S(1)}, u32[]{:S(2)}, u32[]{:S(2)}) collective-permute-start(bf16[256,512]{1,0:T(8,128)(2,1)S(1)} %get-tuple-element.40), channel_id=1, source_target_pairs={{0,1},{1,0},{2,3},{3,2},{4,5},{5,4},{6,7},{7,6},{8,9},{9,8},{10,11... | collective-permute-start | bytes 786440 | tf_op jit(solution)/shard_map/ppermute | solution.py:396
  1.9 1.2 %collective-permute-done.refs_1_ = bf16[256,512]{1,0:T(8,128)(2,1)S(1)} collective-permute-done((bf16[256,512]{1,0:T(8,128)(2,1)S(1)}, bf16[256,512]{1,0:T(8,128)(2,1)S(1)}, u32[]{:S(2)}, u32[]{:S(2)}) %collective-permute-start) | collective-permute-done | bytes 262176 | tf_op jit(solution)/shard_map/ppermute | solution.py:396
  3.8 0.8 %select_reduce_fusion = s32[8]{0:T(128)S(1)} fusion(s32[8,8]{1,0:T(8,128)} %param.12), kind=kLoop, calls=%fused_computation.4 | loop fusion | flops 440 | bytes 288 | tf_op jit(solution)/shard_map/reduce_sum | solution.py:171
  4.6 0.8 %select_reduce_fusion.1 = s32[8]{0:T(128)S(1)} fusion(s32[8,8]{1,0:T(8,128)} %param.13), kind=kLoop, calls=%fused_computation.5 | loop fusion | flops 440 | bytes 288 | tf_op jit(solution)/shard_map/reduce_sum | solution.py:171
  5.5 0.8 %copy.21 = bf16[16,8]{1,0:T(8,128)(2,1)S(1)} copy(bf16[16,8]{0,1:T(8,128)(2,1)} %param.11) | data formatting | bytes 512 | tf_op args[4]
  6.2 0.7 fusion.2.refs_1_
  6.9 0.6 collective-permute-done.1.refs_3_
  7.5 1.6 %copy-done = bf16[128,8192]{1,0:T(8,128)(2,1)S(1)} copy-done((bf16[128,8192]{1,0:T(8,128)(2,1)S(1)}, bf16[128,8192]{1,0:T(8,128)(2,1)}, u32[]{:S(2)}) %copy-start) | copy-done | bytes 2097176
  9.1 6.2 %shard_map.75 = (f32[1,8192]{1,0:T(1,128)S(1)}, f32[1,8192]{1,0:T(1,128)S(1)}, f32[128,8192]{1,0:T(8,128)S(1)}) custom-call(s32[8,2]{1,0:T(8,128)S(1)} %copy.26.refs_0_, f32[18,64]{1,0:T(8,128)S(1)} %fusion.2.refs_1_, bf16[128,8192]{1,0:T(8,128)(2,1)S(1)} %copy-done, bf16[128,8192]{1,0:T(8,128)(2,1)S(1)} %collective-permute-done.1.refs_3_, ...), custom_call_target="tpu_custom_call" | custom-call | flops 1 | tf_op jit(solution)/shard_map/pallas_call | solution.py:370
  15.3 1.7 %collective-permute-done.3.refs_4_ = bf16[512,512]{1,0:T(8,128)(2,1)S(1)} collective-permute-done((bf16[512,512]{1,0:T(8,128)(2,1)S(1)}, bf16[512,512]{1,0:T(8,128)(2,1)S(1)}, u32[]{:S(2)}, u32[]{:S(2)}) %collective-permute-start.3) | collective-permute-done | bytes 524320 | tf_op jit(solution)/shard_map/ppermute | solution.py:414
  17.0 1.8 %collective-permute-start.5 = (bf16[512,512]{1,0:T(8,128)(2,1)S(1)}, bf16[512,512]{1,0:T(8,128)(2,1)S(1)}, u32[]{:S(2)}, u32[]{:S(2)}) collective-permute-start(bf16[512,512]{1,0:T(8,128)(2,1)S(1)} %collective-permute-done.3.refs_4_), channel_id=1, source_target_pairs={{0,4},{2,6},{4,8},{6,10},{8,12},{10,14},{12,0},{14,2},{1,5},{3,7},... | collective-permute-start | bytes 1572872 | tf_op jit(solution)/shard_map/ppermute | solution.py:414
  19.0 9.7 %shard_map.76 = (f32[1,8192]{1,0:T(1,128)S(1)}, f32[1,8192]{1,0:T(1,128)S(1)}, f32[128,8192]{1,0:T(8,128)S(1)}) custom-call(s32[8,2]{1,0:T(8,128)S(1)} %copy.26.refs_0_, f32[18,64]{1,0:T(8,128)S(1)} %fusion.2.refs_1_, bf16[128,8192]{1,0:T(8,128)(2,1)S(1)} %copy-done, ...), custom_call_target="tpu_custom_call", output_to_operand_aliasing={{0}: (6, {}), {1}: (7, {}), {2}: (8, {})} | custom-call | flops 1 | tf_op jit(solution)/shard_map/pallas_call | solution.py:370
  28.8 0.7 %collective-permute-done.5.refs_4_ = bf16[512,512]{1,0:T(8,128)(2,1)S(1)} collective-permute-done((bf16[512,512]{1,0:T(8,128)(2,1)S(1)}, bf16[512,512]{1,0:T(8,128)(2,1)S(1)}, u32[]{:S(2)}, u32[]{:S(2)}) %collective-permute-start.5) | collective-permute-done | bytes 524320 | tf_op jit(solution)/shard_map/ppermute | solution.py:414
  29.5 1.5 %collective-permute-done.4.refs_5_ = bf16[512,512]{1,0:T(8,128)(2,1)S(1)} collective-permute-done((bf16[512,512]{1,0:T(8,128)(2,1)S(1)}, bf16[512,512]{1,0:T(8,128)(2,1)S(1)}, u32[]{:S(2)}, u32[]{:S(2)}) %collective-permute-start.4) | collective-permute-done | bytes 524320 | tf_op jit(solution)/shard_map/ppermute | solution.py:415
  31.1 1.5 %collective-permute-start.7 = (bf16[512,512]{1,0:T(8,128)(2,1)S(1)}, bf16[512,512]{1,0:T(8,128)(2,1)S(1)}, u32[]{:S(2)}, u32[]{:S(2)}) collective-permute-start(bf16[512,512]{1,0:T(8,128)(2,1)S(1)} %collective-permute-done.5.refs_4_), channel_id=1, source_target_pairs={{0,4},{2,6},{4,8},{6,10},{8,12},{10,14},{1,5},{3,7},{5,9},{7,11},{... | collective-permute-start | bytes 1572872 | tf_op jit(solution)/shard_map/ppermute | solution.py:414
  32.8 9.3 %shard_map.77 = (f32[1,8192]{1,0:T(1,128)S(1)}, f32[1,8192]{1,0:T(1,128)S(1)}, f32[128,8192]{1,0:T(8,128)S(1)}) custom-call(s32[8,2]{1,0:T(8,128)S(1)} %copy.26.refs_0_, f32[18,64]{1,0:T(8,128)S(1)} %fusion.2.refs_1_, bf16[128,8192]{1,0:T(8,128)(2,1)S(1)} %copy-done, ...), custom_call_target="tpu_custom_call", output_to_operand_aliasing={{0}: (6, {}), {1}: (7, {}), {2}: (8, {})} | custom-call | flops 1 | tf_op jit(solution)/shard_map/pallas_call | solution.py:370
  42.1 2.2 %collective-permute-done.7.refs_4_ = bf16[512,512]{1,0:T(8,128)(2,1)S(1)} collective-permute-done((bf16[512,512]{1,0:T(8,128)(2,1)S(1)}, bf16[512,512]{1,0:T(8,128)(2,1)S(1)}, u32[]{:S(2)}, u32[]{:S(2)}) %collective-permute-start.7) | collective-permute-done | bytes 524320 | tf_op jit(solution)/shard_map/ppermute | solution.py:414
  44.5 7.9 %shard_map.78 = (f32[1,8192]{1,0:T(1,128)S(1)}, f32[1,8192]{1,0:T(1,128)S(1)}, f32[128,8192]{1,0:T(8,128)S(1)}) custom-call(s32[8,2]{1,0:T(8,128)S(1)} %copy.26.refs_0_, f32[18,64]{1,0:T(8,128)S(1)} %fusion.2.refs_1_, bf16[128,8192]{1,0:T(8,128)(2,1)S(1)} %copy-done, ...), custom_call_target="tpu_custom_call", output_to_operand_aliasing={{0}: (6, {}), {1}: (7, {}), {2}: (8, {})} | custom-call | flops 1 | tf_op jit(solution)/shard_map/pallas_call | solution.py:370
  52.4 2.3 %collective-permute-done.8.refs_4_ = bf16[512,512]{1,0:T(8,128)(2,1)S(1)} collective-permute-done((bf16[512,512]{1,0:T(8,128)(2,1)S(1)}, bf16[512,512]{1,0:T(8,128)(2,1)S(1)}, u32[]{:S(2)}, u32[]{:S(2)}) %collective-permute-start.8) | collective-permute-done | bytes 524320 | tf_op jit(solution)/shard_map/ppermute | solution.py:415
  54.7 3.9 %shard_map.80 = bf16[128,4096]{1,0:T(8,128)(2,1)S(1)} custom-call(s32[8,2]{1,0:T(8,128)S(1)} %copy.26.refs_0_, f32[18,64]{1,0:T(8,128)S(1)} %fusion.2.refs_1_, bf16[128,8192]{1,0:T(8,128)(2,1)S(1)} %copy-done, bf16[128,8192]{1,0:T(8,128)(2,1)S(1)} %collective-permute-done.1.refs_3_, bf16[512,512]{1,0:T(8,128)(2,1)S(1)} %collective-permute-done.8.refs_4_, ...), custom_call_target="tpu_custom_call" | custom-call | flops 1 | tf_op jit(solution)/shard_map/pallas_call | solution.py:370
  58.6 4.0 %collective-permute-start.9 = (bf16[128,4096]{1,0:T(8,128)(2,1)S(1)}, bf16[128,4096]{1,0:T(8,128)(2,1)S(1)}, u32[]{:S(2)}, u32[]{:S(2)}) collective-permute-start(bf16[128,4096]{1,0:T(8,128)(2,1)S(1)} %shard_map.80), channel_id=1, source_target_pairs={{0,1},{1,0},{2,3},{3,2},{4,5},{5,4},{6,7},{7,6},{8,9},{9,8},{10,11... | collective-permute-start | bytes 3145736 | tf_op jit(solution)/shard_map/ppermute | solution.py:432
  62.6 4.5 %shard_map.79.refs_0_ = bf16[128,8192]{1,0:T(8,128)(2,1)} custom-call(s32[8,2]{1,0:T(8,128)S(1)} %copy.26.refs_0_, f32[18,64]{1,0:T(8,128)S(1)} %fusion.2.refs_1_, bf16[128,8192]{1,0:T(8,128)(2,1)S(1)} %copy-done, bf16[128,8192]{1,0:T(8,128)(2,1)S(1)} %collective-permute-done.1.refs_3_, bf16[512,512]{1,0:T(8,128)(2,1)S(1)} %collective-permute-done.8.refs_4_, ...), custom_call_target="tpu_custom_call" | custom-call | flops 1 | tf_op jit(solution)/shard_map/pallas_call | solution.py:370
  67.2 1.0 %shard_map.81 = bf16[128,8192]{1,0:T(8,128)(2,1)} custom-call(bf16[128,8192]{1,0:T(8,128)(2,1)} %shard_map.79.refs_0_, bf16[128,4096]{1,0:T(8,128)(2,1)S(1)} %collective-permute-done.9.refs_1_), custom_call_target="tpu_custom_call", output_to_operand_aliasing={{}: (0, {})} | custom-call | tf_op jit(solution)/shard_map/pallas_call | solution.py:157
  (13 shorter events, 1.6 us)
Async XLA Ops:
  1.1 1.9 %collective-permute-start = (bf16[256,512]{1,0:T(8,128)(2,1)S(1)}, bf16[256,512]{1,0:T(8,128)(2,1)S(1)}, u32[]{:S(2)}, u32[]{:S(2)}) collective-permute-start(bf16[256,512]{1,0:T(8,128)(2,1)S(1)} %get-tuple-element.40), channel_id=1, source_target_pairs={{0,1},{1,0},{2,3},{3,2},{4,5},{5,4},{6,7},{7,6},{8,9},{9,8},{10,11... | collective-permute-start | bytes 786440 | tf_op jit(solution)/shard_map/ppermute | solution.py:396
  3.1 4.4 %collective-permute-start.1 = (bf16[128,8192]{1,0:T(8,128)(2,1)}, bf16[128,8192]{1,0:T(8,128)(2,1)S(1)}, u32[]{:S(2)}, u32[]{:S(2)}) collective-permute-start(bf16[128,8192]{1,0:T(8,128)(2,1)} %refs_2_.11), channel_id=1, source_target_pairs={{0,1},{1,0},{2,3},{3,2},{4,5},{5,4},{6,7},{7,6},{8,9},{9,8},{10,11... | collective-permute-start | bytes 6291464 | tf_op jit(solution)/shard_map/ppermute | solution.py:399
  3.5 13.5 %collective-permute-start.3 = (bf16[512,512]{1,0:T(8,128)(2,1)S(1)}, bf16[512,512]{1,0:T(8,128)(2,1)S(1)}, u32[]{:S(2)}, u32[]{:S(2)}) collective-permute-start(bf16[512,512]{1,0:T(8,128)(2,1)S(1)} %shard_map.74.refs_4_), channel_id=1, source_target_pairs={{0,4},{2,6},{4,8},{6,10},{8,12},{10,14},{12,0},{14,2},{1,5},{3,7},... | collective-permute-start | bytes 1572872 | tf_op jit(solution)/shard_map/ppermute | solution.py:414
  3.5 13.5 %collective-permute-start.2 = (bf16[512,512]{1,0:T(8,128)(2,1)S(1)}, bf16[512,512]{1,0:T(8,128)(2,1)}, u32[]{:S(2)}, u32[]{:S(2)}) collective-permute-start(bf16[512,512]{1,0:T(8,128)(2,1)S(1)} %shard_map.74.refs_4_), channel_id=1, source_target_pairs={{0,2},{2,0},{4,6},{6,4},{8,10},{10,8},{12,14},{14,12},{1,3},{3,1},... | collective-permute-start | bytes 1572872 | tf_op jit(solution)/shard_map/ppermute | solution.py:415
  7.5 1.6 %copy-start = (bf16[128,8192]{1,0:T(8,128)(2,1)S(1)}, bf16[128,8192]{1,0:T(8,128)(2,1)}, u32[]{:S(2)}) copy-start(bf16[128,8192]{1,0:T(8,128)(2,1)} %refs_2_.11) | copy-start | bytes 6291460
  17.0 12.5 %collective-permute-start.5 = (bf16[512,512]{1,0:T(8,128)(2,1)S(1)}, bf16[512,512]{1,0:T(8,128)(2,1)S(1)}, u32[]{:S(2)}, u32[]{:S(2)}) collective-permute-start(bf16[512,512]{1,0:T(8,128)(2,1)S(1)} %collective-permute-done.3.refs_4_), channel_id=1, source_target_pairs={{0,4},{2,6},{4,8},{6,10},{8,12},{10,14},{12,0},{14,2},{1,5},{3,7},... | collective-permute-start | bytes 1572872 | tf_op jit(solution)/shard_map/ppermute | solution.py:414
  18.8 12.3 %collective-permute-start.4 = (bf16[512,512]{1,0:T(8,128)(2,1)S(1)}, bf16[512,512]{1,0:T(8,128)(2,1)S(1)}, u32[]{:S(2)}, u32[]{:S(2)}) collective-permute-start(bf16[512,512]{1,0:T(8,128)(2,1)S(1)} %collective-permute-done.3.refs_4_), channel_id=1, source_target_pairs={{0,2},{2,0},{4,6},{6,4},{8,10},{10,8},{12,14},{14,12},{1,3},{3,1},... | collective-permute-start | bytes 1572872 | tf_op jit(solution)/shard_map/ppermute | solution.py:415
  31.1 13.2 %collective-permute-start.7 = (bf16[512,512]{1,0:T(8,128)(2,1)S(1)}, bf16[512,512]{1,0:T(8,128)(2,1)S(1)}, u32[]{:S(2)}, u32[]{:S(2)}) collective-permute-start(bf16[512,512]{1,0:T(8,128)(2,1)S(1)} %collective-permute-done.5.refs_4_), channel_id=1, source_target_pairs={{0,4},{2,6},{4,8},{6,10},{8,12},{10,14},{1,5},{3,7},{5,9},{7,11},{... | collective-permute-start | bytes 1572872 | tf_op jit(solution)/shard_map/ppermute | solution.py:414
  32.5 11.7 %collective-permute-start.6 = (bf16[512,512]{1,0:T(8,128)(2,1)S(1)}, bf16[512,512]{1,0:T(8,128)(2,1)S(1)}, u32[]{:S(2)}, u32[]{:S(2)}) collective-permute-start(bf16[512,512]{1,0:T(8,128)(2,1)S(1)} %collective-permute-done.5.refs_4_), channel_id=1, source_target_pairs={{0,2},{2,0},{4,6},{6,4},{8,10},{10,8},{12,14},{14,12},{1,3},{3,1},... | collective-permute-start | bytes 1572872 | tf_op jit(solution)/shard_map/ppermute | solution.py:415
  44.3 10.4 %collective-permute-start.8 = (bf16[512,512]{1,0:T(8,128)(2,1)S(1)}, bf16[512,512]{1,0:T(8,128)(2,1)S(1)}, u32[]{:S(2)}, u32[]{:S(2)}) collective-permute-start(bf16[512,512]{1,0:T(8,128)(2,1)S(1)} %collective-permute-done.7.refs_4_), channel_id=1, source_target_pairs={{0,2},{2,0},{4,6},{6,4},{8,10},{10,8},{12,14},{14,12},{1,3},{3,1},... | collective-permute-start | bytes 1572872 | tf_op jit(solution)/shard_map/ppermute | solution.py:415
  58.6 8.5 %collective-permute-start.9 = (bf16[128,4096]{1,0:T(8,128)(2,1)S(1)}, bf16[128,4096]{1,0:T(8,128)(2,1)S(1)}, u32[]{:S(2)}, u32[]{:S(2)}) collective-permute-start(bf16[128,4096]{1,0:T(8,128)(2,1)S(1)} %shard_map.80), channel_id=1, source_target_pairs={{0,1},{1,0},{2,3},{3,2},{4,5},{5,4},{6,7},{7,6},{8,9},{9,8},{10,11... | collective-permute-start | bytes 3145736 | tf_op jit(solution)/shard_map/ppermute | solution.py:432
